TPU v7x, 32 devices: a whole 2x2x4 slice. The times are simulated.
32 devices in a mesh: groups: 2 (over x), blk: 4 (over y, core), row: 4 (over z).
Axes of the slice: x: 2, y: 2, z: 4, core: 2. Of those that a mesh axis runs over, the one named last changes fastest.
Arguments:
- coords: float32 [3, 24576], P(None, ('groups', 'blk', 'row')), parts along dimension 1, may hold values from 0 to 1
- charges: float32 [24576], P(('groups', 'blk', 'row')), parts along dimension 0, may hold values from -1 to 1
- counts: int32 [32], P(('groups', 'blk', 'row')), parts along dimension 0, may hold values from 256 to 768, as said below
- send_slot: int32 [24576], P(('groups', 'blk', 'row')), parts along dimension 0, may hold values from 0 to 1023, as said below
- recv_index: int32 [16384], P(('groups', 'blk', 'row')), parts along dimension 0, may hold values from 0 to 1023, as said below
- wave_ints: int32 [3, 24576], P(None, 'blk'), may hold values from -36 to 36, as said below
Outputs:
- slot_forces: float32 [3, 24576], P(None, ('groups', 'blk', 'row')), parts along dimension 1
- atom_forces: float32 [3, 16384], P(None, ('groups', 'blk', 'row')), parts along dimension 1
There are 2 independent parts, one for each index of `groups`. A program takes and returns all parts, laid end to end along the dimension named above; an argument that names none is the same for every part. Nothing has to cross between parts.
Inputs may be any that keep to these rules, and one draw needn't show every extreme that they name: The counts of one system sum to 8192; the largest is 768. `send_slot`: for a live slot the value is d * 64 + r: the ion goes to k-space device d as its r-th arrival from this owner. Live values of one owner are distinct, and the ranks r to one device are 0 up to the number sent there minus one. Every device receives exactly 512 ions; some owner sends exactly 64 to some device. Slots that are not live hold arbitrary values. `recv_index`: the 512 values of device d are distinct and are exactly the arrivals s * 64 + r sent to d. `wave_ints`: each column is (h, k, l) with |h|, |k| at most 12 and l nonzero.
All inputs are finite; a program needn't handle non-finite values.
Results may differ from a plain program's by a relative error of at most 0.00007.
Values sent between devices are 32-bit elements; how exact they have to be, the bound alone decides.
No kernel may reach another device: no remote copies, remote signals or barrier semaphores. Data moves between devices by JAX's collectives and lax.ppermute only.
A program may use at most 128 MiB of HBM per device.

v0:
```python
import math

import jax
import jax.numpy as jnp
from jax import lax
from jax.sharding import PartitionSpec as P

DOUBLE_PI = 2.0 * math.pi
EWALD_BETA = 30.0
BOX_Z = 3.0
FORCE_GAIN = 400.0


def phys_vectors(wave_float):
    return jnp.stack(
        [DOUBLE_PI * wave_float[0], DOUBLE_PI * wave_float[1], DOUBLE_PI * wave_float[2] / BOX_Z]
    )


def phase_angles(wave_float, frac):
    inner = wave_float[0][:, None] * frac[0][None, :] + wave_float[1][:, None] * frac[1][None, :]
    inner = inner + wave_float[2][:, None] * frac[2][None, :]
    return DOUBLE_PI * inner


def pull_sum(wave_float, cos_weighted, sin_weighted, frac):
    angles = phase_angles(wave_float, frac)
    coef = jnp.sin(angles) * cos_weighted[:, None] - jnp.cos(angles) * sin_weighted[:, None]
    wave_phys = phys_vectors(wave_float)
    return jnp.sum(wave_phys[:, :, None] * coef[None, :, :], axis=1)


def phase_sums(wave_float, atom_rows):
    angles = phase_angles(wave_float, atom_rows[:3])
    return (
        jnp.sum(atom_rows[3][None, :] * jnp.cos(angles), axis=1),
        jnp.sum(atom_rows[3][None, :] * jnp.sin(angles), axis=1),
    )


def body(coords, charges, counts, send_slot, recv_index, wave_ints):
    slots_dev = charges.shape[0]
    atoms_dev = recv_index.shape[0]
    devices = lax.axis_size(("blk", "row"))
    blk_count = lax.axis_size("blk")
    pair_cap = 2 * atoms_dev // devices
    buf_width = devices * pair_cap
    is_live = jnp.arange(slots_dev, dtype=jnp.int32) < counts[0]
    target_slot = jnp.where(is_live, send_slot, buf_width)
    value_entries = jnp.concatenate([coords, charges[None, :]], axis=0)
    outgoing = (
        jnp.zeros((4, buf_width), jnp.float32).at[:, target_slot].set(value_entries, mode="drop")
    )
    arrived = lax.all_to_all(
        outgoing.reshape(4, devices, pair_cap),
        ("blk", "row"),
        split_axis=1,
        concat_axis=1,
        tiled=True,
    )
    atom_rows = arrived.reshape(4, buf_width)[:, recv_index]
    k_local = wave_ints.shape[1]
    wave_float = wave_ints.astype(jnp.float32)
    cos_part, sin_part = phase_sums(
        wave_float, lax.all_gather(atom_rows, "blk", axis=1, tiled=True)
    )
    cos_sum, sin_sum = lax.psum((cos_part, sin_part), "row")
    wave_phys = phys_vectors(wave_float)
    k_squared = jnp.sum(wave_phys * wave_phys, axis=0)
    weight = jnp.exp(-k_squared / (4.0 * EWALD_BETA * EWALD_BETA)) / k_squared
    cos_weighted = weight * cos_sum
    sin_weighted = weight * sin_sum
    force_scale = FORCE_GAIN / math.sqrt(float(atoms_dev * devices * blk_count * k_local))
    package = jnp.concatenate([wave_float, cos_weighted[None, :], sin_weighted[None, :]], axis=0)
    shard_piece = lax.all_gather(package, "blk", axis=1, tiled=True)
    pull_total = pull_sum(shard_piece[:3], shard_piece[3], shard_piece[4], atom_rows[:3])
    atom_forces = force_scale * atom_rows[3][None, :] * pull_total
    homeward = jnp.zeros((3, buf_width), jnp.float32).at[:, recv_index].set(atom_forces)
    returned = lax.all_to_all(
        homeward.reshape(3, devices, pair_cap),
        ("blk", "row"),
        split_axis=1,
        concat_axis=1,
        tiled=True,
    ).reshape(3, buf_width)
    picked = returned[:, jnp.minimum(target_slot, buf_width - 1)]
    slot_forces = jnp.where(is_live[None, :], picked, 0.0)
    return (slot_forces, atom_forces)


def solution(mesh):
    placed = (
        P(None, ("groups", "blk", "row")),
        P(("groups", "blk", "row")),
        P(("groups", "blk", "row")),
        P(("groups", "blk", "row")),
        P(("groups", "blk", "row")),
        P(None, "blk"),
    )
    return jax.shard_map(
        body,
        mesh=mesh,
        in_specs=placed,
        out_specs=(P(None, ("groups", "blk", "row")), P(None, ("groups", "blk", "row"))),
        check_vma=False,
    )
```

profile of v0, /device:TPU:0, one launch (start us, length us, event | category | flops | bytes accessed | tf_op | source)
XLA Modules:
  0.0 503.4 jit_solution(13282981945694816931)
XLA Ops:
  1.3 0.7 broadcast_in_dim.50
  2.0 0.7 maximum_bitcast_fusion
  2.7 0.2 copy.21
  2.9 0.7 compare_select_fusion
  3.6 4.3 scatter_custom_fusion
  7.9 0.2 copy.22
  8.1 0.7 reshape.201
  8.8 7.4 %all-to-all-start = ((f32[16,1,256]{2,1,0:T(1,128)}), f32[16,1,256]{2,1,0:T(1,128)S(1)}, u32[]{:S(2)}, u32[]{:S(2)}) async-start(f32[16,1,256]{2,1,0:T(1,128)} %reshape.201), calls=%async_computation | async-start | bytes 32768 | tf_op jit(solution)/shard_map/all_to_all | solution.py:54
  16.2 0.7 compare_select_fusion.2
  16.9 0.9 convert_element_type.3
  17.8 0.1 broadcast_multiply_fusion.5
  17.9 0.1 fusion.5
  18.1 4.6 all-to-all-done
  22.6 0.5 broadcast.143
  23.1 0.7 reduce.16
  23.8 0.1 reshape.202
  23.9 0.2 copy.23
  24.1 1.0 gather_fusion
  25.2 9.9 %all-gather = f32[4,2048]{0,1:T(8,128)S(1)} all-gather(f32[4,512]{0,1:T(8,128)S(1)} %bitcast.28), channel_id=2, replica_groups=mesh['groups'=2,'blk'=4,'row'=4] {'blk'}, dimensions={1}, use_global_device_ids=true | all-gather | bytes 40960 | tf_op jit(solution)/shard_map/all_gather | solution.py:65
  35.1 0.6 fusion
  35.7 2.0 slice_reduce_fusion.3
  37.7 213.6 %multiply_reduce_fusion.2 = (f32[6144]{0:T(1024)S(1)}, f32[6144]{0:T(1024)S(1)}) fusion(f32[2048]{0:T(1024)S(1)} %get-tuple-element.13, f32[6144]{0:T(1024)S(1)} %bitcast.45, f32[2048]{0:T(1024)S(1)} %get-tuple-element.11, f32[6144]{0:T(1024)S(1)} %bitcast.46, f32[2048]{0:T(1024)S(1)} %get-tuple-element.12, f32[6144]{0:T(1024)S(1)} %bitcast.47, ...), kind=kLoop, calls=%fused_computation.7 | loop fusion | flops 125816832 | bytes 155648 | tf_op jit(solution)/shard_map/reduce_sum | solution.py:36
  251.3 16.7 %all-reduce = (f32[6144]{0:T(1024)S(1)}, f32[6144]{0:T(1024)S(1)}) all-reduce(f32[6144]{0:T(1024)S(1)} %get-tuple-element.19, f32[6144]{0:T(1024)S(1)} %get-tuple-element.18), channel_id=1, replica_groups=mesh['groups'=2,'blk'=4,'row'=4] {'row'}, use_global_device_ids=true, to_apply=%region_5.6 | all-reduce | flops 12288 | bytes 98304 | tf_op jit(solution)/shard_map/psum | solution.py:67
  268.0 0.1 pad_maximum_fusion.1
  268.1 7.8 %all_gather.7 = f32[5,24576]{1,0:T(8,128)S(1)} all-gather(f32[5,6144]{1,0:T(8,128)S(1)} %pad_maximum_fusion.1), channel_id=1, replica_groups=mesh['groups'=2,'blk'=4,'row'=4] {'blk'}, dimensions={1}, use_global_device_ids=true | all-gather | bytes 614400 | tf_op jit(solution)/shard_map/all_gather | solution.py:75
  275.8 0.5 broadcast_multiply_fusion.2
  276.4 0.3 pad_maximum_fusion
  276.7 192.7 %multiply_subtract_fusion = f32[24576,512]{1,0:T(8,128)} fusion(f32[24576]{0:T(1024)S(1)} %bitcast.34, f32[24576]{0:T(1024)S(1)} %bitcast.35, f32[512]{0:T(512)S(1)} %get-tuple-element.16, f32[24576]{0:T(1024)S(1)} %bitcast.36, f32[512]{0:T(512)S(1)} %get-tuple-element.17, f32[24576]{0:T(1024)S(1)} %bitcast.37, f32[512]{0:T(512)S(1)} %get-tuple-element.15, ...), kind=kLoop, calls=%fused_computation.5 | loop fusion | flops 113246208 | bytes 50829312 | tf_op jit(solution)/shard_map/sub | solution.py:28
  469.4 17.6 %multiply_reduce_fusion = f32[3,512]{1,0:T(4,128)S(1)} fusion(f32[24576,512]{1,0:T(8,128)} %multiply_subtract_fusion, f32[3,24576]{1,0:T(4,128)S(1)} %pad_maximum_fusion), kind=kLoop, calls=%fused_computation.4 | loop fusion | flops 75495936 | bytes 50632704 | tf_op jit(solution)/shard_map/reduce_sum | solution.py:30
  487.0 0.1 copy.24
  487.1 1.8 scatter_custom_fusion.1
  489.0 0.2 copy.25
  489.2 0.7 reshape.203
  489.9 3.6 all-to-all-start.1
  493.5 0.6 broadcast_multiply_fusion.6
  494.1 5.8 %all-to-all-done.1 = f32[16,1,192]{2,1,0:T(1,128)S(1)} async-done(((f32[16,1,192]{2,1,0:T(1,128)}), f32[16,1,192]{2,1,0:T(1,128)S(1)}, u32[]{:S(2)}, u32[]{:S(2)}) %all-to-all-start.1) | async-done | bytes 12320 | tf_op jit(solution)/shard_map/all_to_all | solution.py:79
  499.9 0.7 reduce.17
  500.6 0.1 reshape.204
  500.7 0.2 copy.26
  500.9 1.6 gather_fusion.1
  502.5 0.2 select_bitcast_fusion
  502.7 0.8 copy.27
  (5 shorter events, 0.0 us)
Async XLA Ops:
  8.8 13.8 %all-to-all-start = ((f32[16,1,256]{2,1,0:T(1,128)}), f32[16,1,256]{2,1,0:T(1,128)S(1)}, u32[]{:S(2)}, u32[]{:S(2)}) async-start(f32[16,1,256]{2,1,0:T(1,128)} %reshape.201), calls=%async_computation | async-start | bytes 32768 | tf_op jit(solution)/shard_map/all_to_all | solution.py:54
  489.9 10.0 %all-to-all-start.1 = ((f32[16,1,192]{2,1,0:T(1,128)}), f32[16,1,192]{2,1,0:T(1,128)S(1)}, u32[]{:S(2)}, u32[]{:S(2)}) async-start(f32[16,1,192]{2,1,0:T(1,128)} %reshape.203), calls=%async_computation.1 | async-start | bytes 32768 | tf_op jit(solution)/shard_map/all_to_all | solution.py:79
where the time goes:
time: 504 us; the launch traced here: 503 us
  other arithmetic  431 us (86%)
  blocking collectives  34.4 us (7%)
  local copies, waits for them, and re-layouts  15.5 us (3%)
  starting transfers between devices  11 us (2%)
  waiting for transfers between devices  10.4 us (2%)
    reduce_sum x1, other arithmetic, phase_sums(): jnp.sum(atom_rows[3][None, :] * jnp.cos(angles), axis=1)  214 us
    sub x1, other arithmetic, pull_sum(): jnp.sin(angles) * cos_weighted[:, None]  193 us
    reduce_sum x1, other arithmetic, pull_sum(): return jnp.sum(wave_phys[:, :, None] * coef[None, :, :], axis=1)  17.6 us
    psum x1, blocking collectives, body(): cos_sum, sin_sum = lax.psum((cos_part, sin_part), 'row')  16.7 us
  transfers between devices with their start and end apart: 2, of which 2 were waited for; matrix products, arithmetic and copies ran while one was open for 0% of the time, Pallas kernels for 0%

commit v1 on v0

v1 whole, which is shorter than its diff:
```python
import functools
import math

import jax
import jax.numpy as jnp
from jax import lax
from jax.experimental import pallas as pl
from jax.experimental.pallas import tpu as pltpu
from jax.sharding import PartitionSpec as P

DOUBLE_PI = 2.0 * math.pi
EWALD_BETA = 30.0
BOX_Z = 3.0
FORCE_GAIN = 400.0
SIN_POLY = (6.283185, -41.34159, 81.599945, -76.61447, 41.342884, -12.471244)
COS_POLY = (1.0, -19.739204, 64.93912, -85.45014, 60.16763, -25.9676, 6.5286584)

BASIS = 24
PAIR_ROWS = 600
GRID_ROWS = 640
HARM = 40
WEIGHT_LANE = 80
F32 = jnp.float32
BF16 = jnp.bfloat16
NT = (((1,), (1,)), ((), ()))
VMEM_BYTES = 40 * 1024 * 1024


def horner(coefs, v):
    total = jnp.full_like(v, coefs[-1])
    for coef in coefs[-2::-1]:
        total = total * v + coef
    return total


def first_harmonics(pos):
    harm = lax.broadcasted_iota(jnp.int32, (8, pos.shape[1]), 0).astype(F32) + 1.0
    turns = harm * pos
    turns = turns - jnp.floor(turns + 0.5)
    square = turns * turns
    return horner(COS_POLY, square), turns * horner(SIN_POLY, square)


def advance(first, by):
    cos_a, sin_a = first
    cos_b, sin_b = by[0][7:8], by[1][7:8]
    return cos_a * cos_b - sin_a * sin_b, sin_a * cos_b + cos_a * sin_b


def merge_last(cos_part, sin_part):
    low = lax.broadcasted_iota(jnp.int32, cos_part.shape, 0) < 4
    return jnp.where(low, cos_part, pltpu.roll(sin_part, 4, 0))


def short_basis(pos):
    first = first_harmonics(pos)
    second = advance(first, first)
    return [first[0], first[1], merge_last(*second)]


def short_slopes(basis):
    row = lax.broadcasted_iota(jnp.int32, basis[0].shape, 0)
    harm = row.astype(F32) + 1.0
    low = row < 4
    factor = jnp.where(low, -(harm + 8.0), harm + 4.0)
    return [-harm * basis[1], harm * basis[0], factor * pltpu.roll(basis[2], 4, 0)]


def long_basis(pos):
    first = first_harmonics(pos)
    second = advance(first, first)
    third = advance(first, second)
    fourth = advance(second, second)
    fifth = advance(first, fourth)
    parts = (first, second, third, fourth, fifth)
    return [p[0] for p in parts], [p[1] for p in parts]


def split_two(value):
    high = value.astype(BF16)
    return high, (value - high.astype(F32)).astype(BF16)


def prep_kernel(cap, coords_ref, charges_ref, counts_ref, send_ref, waves_ref, out_ref):
    slots = charges_ref.shape[1]
    half = slots // 2
    live = lax.broadcasted_iota(jnp.int32, (1, slots), 1) < counts_ref[0]
    charge = jnp.where(live, charges_ref[...], 0.0)
    send = jnp.where(live, send_ref[...], -1).astype(F32)
    out_ref[...] = jnp.zeros_like(out_ref)
    for part in range(2):
        lanes = slice(part * half, (part + 1) * half)
        out_ref[4 * part : 4 * part + 3, 0:half] = coords_ref[:, lanes]
        out_ref[4 * part + 3 : 4 * part + 4, 0:half] = charge[:, lanes]
    for piece in range(slots // 128):
        out_ref[piece : piece + 1, half : half + 128] = send[:, piece * 128 : (piece + 1) * 128]
    block = half + 128
    rows, width = wave_shape(waves_ref.shape[1])
    for row in range(rows):
        for comp in range(3):
            out_ref[row : row + 1, block + comp * width : block + (comp + 1) * width] = waves_ref[
                comp : comp + 1, row * width : (row + 1) * width
            ].astype(F32)


def wave_shape(k_local):
    rows = 8
    while k_local % (rows * 128):
        rows //= 2
    return rows, k_local // rows


def basis_row(index):
    size = jnp.abs(index)
    sign = jnp.where(index < 0.0, 1.0, 0.0)
    row = jnp.where(size <= 8.0, size - 1.0 + 8.0 * sign, size + 7.0 + 4.0 * sign)
    return jnp.where(size == 0.0, float(BASIS), row)


def basis_size(row):
    low = jnp.where(row < 8, row, row - 8) + 1
    high = jnp.where(row < 20, row - 16, row - 20) + 9
    return jnp.where(row < 16, low, jnp.where(row < BASIS, high, 0))


def weight_table():
    row = lax.broadcasted_iota(jnp.int32, (GRID_ROWS, 128), 0)
    lane = lax.broadcasted_iota(jnp.int32, (GRID_ROWS, 128), 1)
    paired = row < PAIR_ROWS
    row_x = jnp.where(paired, row // BASIS, jnp.minimum(row - PAIR_ROWS, BASIS))
    row_y = jnp.where(paired, row % BASIS, BASIS)
    phys_x = DOUBLE_PI * basis_size(row_x).astype(F32)
    phys_y = DOUBLE_PI * basis_size(row_y).astype(F32)
    phys_z = DOUBLE_PI * jnp.maximum(lane - (WEIGHT_LANE - 1), 1).astype(F32) / BOX_Z
    k_squared = phys_x * phys_x + phys_y * phys_y + phys_z * phys_z
    weight = jnp.exp(-k_squared / (4.0 * EWALD_BETA * EWALD_BETA)) / k_squared
    return jnp.where(lane >= WEIGHT_LANE, weight, 0.0)


def weights_kernel(rows, width, has_base, *refs):
    if has_base:
        base_ref, waves_ref, out_ref, ids_ref = refs
    else:
        waves_ref, out_ref, ids_ref = refs
    start = waves_ref.shape[1] - 3 * width
    wave_h = waves_ref[0:rows, start : start + width]
    wave_k = waves_ref[0:rows, start + width : start + 2 * width]
    wave_l = waves_ref[0:rows, start + 2 * width : start + 3 * width]
    flip = jnp.where(wave_l < 0.0, -1.0, 1.0)
    row_x = basis_row(wave_h * flip)
    row_y = basis_row(wave_k * flip)
    ids_ref[0] = jnp.where(row_y == float(BASIS), PAIR_ROWS + row_x, BASIS * row_x + row_y)
    ids_ref[1] = wave_l * flip + float(WEIGHT_LANE - 1)
    out_ref[...] = jnp.zeros_like(out_ref)
    row_iota = lax.broadcasted_iota(jnp.int32, (GRID_ROWS, width), 0).astype(F32)
    lane_iota = lax.broadcasted_iota(jnp.int32, (128, width), 0).astype(F32)

    def step(piece, carry):
        row_id = ids_ref[0, pl.ds(piece, 1), :]
        lane_id = ids_ref[1, pl.ds(piece, 1), :]
        row_hot = jnp.where(row_iota == row_id, 1.0, 0.0).astype(BF16)
        lane_hot = jnp.where(lane_iota == lane_id, 1.0, 0.0).astype(BF16)
        out_ref[...] += lax.dot_general(row_hot, lane_hot, NT, preferred_element_type=F32)
        return carry

    lax.fori_loop(0, rows, step, 0)
    total = out_ref[...] * weight_table()
    if has_base:
        total = total + base_ref[...]
    out_ref[...] = total


def sums_kernel(owners, first_owner, half, cap, row_count, base_ref, ions_ref, out_ref, arrive_ref, v_ref):
    block = half + 128
    slots = 2 * half
    per_pack = 64 // cap
    out_ref[...] = base_ref[...]
    device = lax.axis_index("blk") * row_count + lax.axis_index("row")
    hot_iota = lax.broadcasted_iota(jnp.int32, (64, slots), 0).astype(F32)

    def step(owner, carry):
        begin = pl.multiple_of(owner * block, 128)
        block_rows = ions_ref[:, pl.ds(begin, block)]

        def comp(index):
            return jnp.concatenate(
                [block_rows[index : index + 1, 0:half], block_rows[index + 4 : index + 5, 0:half]], axis=1
            )

        charge = comp(3)
        basis_x = [charge * rows for rows in short_basis(comp(0))]
        basis_y = jnp.concatenate(short_basis(comp(1)), axis=0)
        cos_z, sin_z = long_basis(comp(2))
        for row in range(0, BASIS, 2):
            pair = [basis_x[r // 8][r % 8 : r % 8 + 1] * basis_y for r in (row, row + 1)]
            high, low = split_two(jnp.concatenate(pair, axis=0))
            v_ref[row * BASIS : (row + 2) * BASIS] = high
            v_ref[GRID_ROWS + row * BASIS : GRID_ROWS + (row + 2) * BASIS] = low
        const_x = jnp.where(
            lax.broadcasted_iota(jnp.int32, (8, slots), 0) == 0, jnp.broadcast_to(charge, (8, slots)), 0.0
        )
        none = jnp.zeros((8, slots), F32)
        tail = jnp.concatenate([charge * basis_y] + basis_x + [const_x, none], axis=0)
        high, low = split_two(tail)
        v_ref[BASIS * BASIS : GRID_ROWS] = high
        v_ref[GRID_ROWS + BASIS * BASIS : 2 * GRID_ROWS] = low
        high, low = split_two(jnp.concatenate(cos_z + sin_z, axis=0))
        gap = jnp.zeros((128 - 2 * HARM, slots), BF16)
        table_z = jnp.concatenate([high, gap, low, gap], axis=0)
        part = lax.dot_general(v_ref[...], table_z, NT, preferred_element_type=F32)
        out_ref[...] += part[:GRID_ROWS, :128] + (part[:GRID_ROWS, 128:] + part[GRID_ROWS:, :128])

        send = jnp.concatenate([block_rows[p : p + 1, half:block] for p in range(slots // 128)], axis=1)
        place = lax.rem(first_owner + owner, per_pack) * cap
        hots = []
        for target in (device, device ^ row_count):
            rank = send - (target * cap).astype(F32)
            valid = jnp.logical_and(rank >= 0.0, rank < float(cap))
            key = jnp.where(valid, rank + place.astype(F32), -1.0)
            hots.append(jnp.where(hot_iota == key, 1.0, 0.0).astype(BF16))
        values = jnp.concatenate([comp(0), comp(1), comp(2), charge], axis=0)
        high = values.astype(BF16)
        rest = values - high.astype(F32)
        mid = rest.astype(BF16)
        low = (rest - mid.astype(F32)).astype(BF16)
        hot = jnp.concatenate(hots, axis=0)
        found = [lax.dot_general(v, hot, NT, preferred_element_type=F32) for v in (high, mid, low)]
        row = (found[0] + found[1]) + found[2]
        pack = owner // per_pack
        if per_pack == 1:
            arrive_ref[pack] = row
        else:
            arrive_ref[pack] = jnp.where(place == 0, row, arrive_ref[pack] + row)
        return carry

    lax.fori_loop(0, owners, step, 0)


def force_kernel(
    force_scale, half, mine_ref, other_ref, arrive_ref, arrived_ref, block_ref, key_ref, slot_ref, atom_ref, w_ref, z_ref
):
    slots = 2 * half
    atoms_dev = key_ref.shape[1]
    packs = arrive_ref.shape[0]
    lane = lax.broadcasted_iota(jnp.int32, (4, 128), 1)
    pieces = [jnp.where(lane < 64, arrive_ref[p], arrived_ref[p]) for p in range(packs)]
    pool = jnp.concatenate(pieces, axis=1)
    high = pool.astype(BF16)
    rest = pool - high.astype(F32)
    mid = rest.astype(BF16)
    low = (rest - mid.astype(F32)).astype(BF16)
    spot = lax.broadcasted_iota(jnp.int32, (packs * 128, atoms_dev), 0)
    hot = jnp.where(spot == key_ref[...], 1.0, 0.0).astype(BF16)
    found = [jnp.dot(v, hot, preferred_element_type=F32) for v in (high, mid, low)]
    routed = (found[0] + found[1]) + found[2]
    ions = jnp.concatenate([block_ref[0:4, 0:half], block_ref[4:8, 0:half], routed], axis=1)
    count = slots + atoms_dev
    basis_x = short_basis(ions[0:1])
    basis_y = short_basis(ions[1:2])
    cos_z, sin_z = long_basis(ions[2:3])
    table_z = jnp.concatenate(cos_z + sin_z, axis=0)
    harm = lax.broadcasted_iota(jnp.int32, (HARM, count), 0).astype(F32) + 1.0
    slope_z = jnp.concatenate(
        [-harm * jnp.concatenate(sin_z, axis=0), harm * jnp.concatenate(cos_z, axis=0)], axis=0
    )
    for spot_z, table in ((0, table_z), (count, slope_z)):
        high, low = split_two(table)
        z_ref[:, spot_z : spot_z + count] = jnp.concatenate(
            [high, low, high, jnp.zeros((256 - 6 * HARM, count), BF16)], axis=0
        )
    slope_x = short_slopes(basis_x)
    slope_y = short_slopes(basis_y)
    lane = lax.broadcasted_iota(jnp.int32, (8, 128), 1)
    is_cos = lane < HARM
    is_wave = lane < 2 * HARM
    low_rows = lax.broadcasted_iota(jnp.int32, (8, 128), 0) < 4

    def fields(row):
        tile = mine_ref[row : row + 8] + other_ref[row : row + 8]
        sums = jnp.where(is_wave, tile, 0.0)
        gain = jnp.where(is_cos, pltpu.roll(tile, 48, 1), jnp.where(is_wave, pltpu.roll(tile, 88, 1), 0.0))
        turned = jnp.where(
            is_cos, pltpu.roll(sums, 88, 1), jnp.where(is_wave, -pltpu.roll(sums, HARM, 1), 0.0)
        )
        return gain, sums, turned

    def swap(parts):
        return [parts[1], parts[0], pltpu.roll(parts[2], 4, 0)]

    def store(row, value):
        high, low = split_two(value)
        high = high.astype(F32)
        low = low.astype(F32)
        turned = pltpu.roll(high, 2 * HARM, 1)
        w_ref[row : row + 8, 0:128] = jnp.where(is_wave, high, turned)
        w_ref[row : row + 8, 128:256] = jnp.where(lane < 32, turned, pltpu.roll(low, 32, 1))

    def combine(x_rows, x_other):
        gain, sums, turned = x_rows
        swapped_gain, swapped_sums, swapped_turned = swap(gain), swap(sums), swap(turned)
        both = [a + b for a, b in zip(gain, swapped_gain)]
        odd = [a - b for a, b in zip(gain, swapped_gain)]
        if x_other is None:
            return [both[i] * sums[i] - odd[i] * swapped_turned[i] for i in range(3)]
        gain_o, sums_o, turned_o = x_other
        swapped_gain_o, swapped_sums_o = swap(gain_o), swap(sums_o)
        both_o = [a + b for a, b in zip(gain_o, swapped_gain_o)]
        odd_o = [a - b for a, b in zip(gain_o, swapped_gain_o)]
        return [
            (both[i] + both_o[i]) * sums[i]
            - (odd[i] + odd_o[i]) * swapped_turned[i]
            - (both[i] - both_o[i]) * turned_o[i]
            - (odd[i] - odd_o[i]) * swapped_sums_o[i]
            for i in range(3)
        ]

    def group(x):
        parts = [fields(BASIS * x + 8 * i) for i in range(3)]
        return [[p[j] for p in parts] for j in range(3)]

    pairs = [(x, x + 8) for x in range(8)] + [(x, x + 4) for x in range(16, 20)]
    for x, other in pairs:
        group_x, group_o = group(x), group(other)
        for i, value in enumerate(combine(group_x, group_o)):
            store(BASIS * x + 8 * i, value)
        for i, value in enumerate(combine(group_o, group_x)):
            store(BASIS * other + 8 * i, value)
    for i, value in enumerate(combine(group(BASIS), None)):
        store(BASIS * BASIS + 8 * i, value)
    last = [fields(PAIR_ROWS + 8 * i) for i in range(4)]
    gain, sums, turned = [[p[j] for p in last] for j in range(3)]
    gain_s, turned_s = swap(gain), swap(turned)
    for i in range(3):
        store(
            PAIR_ROWS + 8 * i,
            (gain[i] + gain_s[i]) * sums[i] - (gain[i] - gain_s[i]) * turned_s[i],
        )
    store(PAIR_ROWS + 24, gain[3] * sums[3])
    w_ref[PAIR_ROWS + 32 :] = jnp.zeros((GRID_ROWS - PAIR_ROWS - 32, 256), F32)
    weights = w_ref[...].astype(BF16)
    tile = 256
    for begin in range(0, count, tile):
        lanes = slice(begin, begin + tile)
        plain = jnp.dot(weights, z_ref[:, begin : begin + tile], preferred_element_type=F32)
        sloped = jnp.dot(weights, z_ref[:, count + begin : count + begin + tile], preferred_element_type=F32)
        sum_x = jnp.zeros((8, tile), F32)
        sum_y = jnp.zeros((8, tile), F32)
        sum_z = jnp.zeros((8, tile), F32)
        rows_y = [rows[:, lanes] for rows in basis_y]
        rows_dy = [rows[:, lanes] for rows in slope_y]
        for x in range(BASIS + 1):
            part_x = part_y = part_z = 0.0
            for i in range(3):
                row = BASIS * x + 8 * i
                part_x = part_x + rows_y[i] * plain[row : row + 8]
                part_y = part_y + rows_dy[i] * plain[row : row + 8]
                part_z = part_z + rows_y[i] * sloped[row : row + 8]
            if x < BASIS:
                basis = basis_x[x // 8][x % 8 : x % 8 + 1, lanes]
                sum_x = sum_x + slope_x[x // 8][x % 8 : x % 8 + 1, lanes] * part_x
                sum_y = sum_y + basis * part_y
                sum_z = sum_z + basis * part_z
            else:
                sum_y = sum_y + part_y
                sum_z = sum_z + part_z
        for i in range(3):
            row = PAIR_ROWS + 8 * i
            sum_x = sum_x + slope_x[i][:, lanes] * plain[row : row + 8]
            sum_z = sum_z + basis_x[i][:, lanes] * sloped[row : row + 8]
        sum_z = sum_z + sloped[PAIR_ROWS + 24 : PAIR_ROWS + 32]
        gain = (-DOUBLE_PI * force_scale) * ions[3:4, lanes]
        force = jnp.concatenate(
            [
                gain * jnp.sum(sum_x, axis=0, keepdims=True),
                gain * jnp.sum(sum_y, axis=0, keepdims=True),
                (gain / BOX_Z) * jnp.sum(sum_z, axis=0, keepdims=True),
            ],
            axis=0,
        )
        if begin < slots:
            slot_ref[:, begin : begin + tile] = force
        else:
            atom_ref[:, begin - slots : begin - slots + tile] = force


def params():
    return pltpu.CompilerParams(vmem_limit_bytes=VMEM_BYTES)


def whole(count):
    return [pl.BlockSpec(memory_space=pltpu.VMEM)] * count


def body(coords, charges, counts, send_slot, recv_index, wave_ints):
    slots = charges.shape[0]
    half = slots // 2
    block = half + 128
    atoms_dev = recv_index.shape[0]
    devices = lax.axis_size(("blk", "row"))
    blk_count = lax.axis_size("blk")
    row_count = lax.axis_size("row")
    k_local = wave_ints.shape[1]
    cap = 2 * atoms_dev // devices
    per_pack = 64 // cap
    wave_rows, wave_width = wave_shape(k_local)
    device = lax.axis_index(("blk", "row")).astype(jnp.int32)
    force_scale = FORCE_GAIN / math.sqrt(float(atoms_dev * devices * blk_count * k_local))

    with jax.named_scope("payload"):
        payload = pl.pallas_call(
            functools.partial(prep_kernel, cap),
            out_shape=jax.ShapeDtypeStruct((8, block + 3 * wave_width), F32),
            in_specs=whole(2) + [pl.BlockSpec(memory_space=pltpu.SMEM)] + whole(2),
            out_specs=pl.BlockSpec(memory_space=pltpu.VMEM),
            compiler_params=params(),
        )(coords, charges.reshape(1, slots), counts, send_slot.reshape(1, slots), wave_ints)

    def flip(value, axis, bit):
        size = lax.axis_size(axis)
        return lax.ppermute(value, axis, [(i, i ^ bit) for i in range(size)])

    def wave_weights(base, value, pieces):
        shape = jax.ShapeDtypeStruct((GRID_ROWS, 128), F32)
        args = (value,) if base is None else (base, value)
        return pl.pallas_call(
            functools.partial(weights_kernel, wave_rows, wave_width, base is not None),
            out_shape=shape,
            in_specs=whole(len(args)),
            out_specs=pl.BlockSpec(memory_space=pltpu.VMEM),
            scratch_shapes=[pltpu.VMEM((2, wave_rows, wave_width), F32)],
            compiler_params=params(),
            cost_estimate=pl.CostEstimate(flops=2 * GRID_ROWS * 128 * k_local, bytes_accessed=1 << 20, transcendentals=0),
        )(*args)

    bits = []
    table = wave_weights(None, payload, 1)
    waves = [payload[:, block:]]
    ions = payload[:, :block]
    bit = 2
    while bit < blk_count:
        with jax.named_scope("exchange_blk"):
            sent = jnp.concatenate([ions] + waves, axis=1)
            got = flip(sent, "blk", bit)
        width = ions.shape[1]
        ions = jnp.concatenate([ions, got[:, :width]], axis=1)
        fresh = [got[:, at : at + 3 * wave_width] for at in range(width, got.shape[1], 3 * wave_width)]
        for piece in fresh:
            table = wave_weights(table, piece, 1)
        waves = waves + fresh
        bits.append(row_count * bit)
        bit *= 2
    groups = [ions]
    bit = row_count // 2
    while bit >= 1:
        held = groups[0] if len(groups) == 1 else jnp.concatenate(groups, axis=1)
        with jax.named_scope("exchange_row"):
            groups = [held, flip(held, "row", bit)]
        bits.append(bit)
        bit //= 2

    source = (recv_index // cap) ^ device
    order = jnp.zeros_like(source)
    for place, distance in enumerate(bits):
        order = order | jnp.where((source & distance) != 0, 1 << place, 0)
    far = jnp.where((source & row_count) != 0, 64, 0)
    key = (order // per_pack) * 128 + far + (order % per_pack) * cap + recv_index % cap

    owners_half = devices // 2
    arrive_parts = []
    owner = 0
    for held in groups:
        count = held.shape[1] // block
        packs = max(1, count // per_pack)
        with jax.named_scope("structure_sums"):
            table, arrive = pl.pallas_call(
                functools.partial(sums_kernel, count, owner, half, cap, row_count),
                out_shape=(
                    jax.ShapeDtypeStruct((GRID_ROWS, 128), F32),
                    jax.ShapeDtypeStruct((packs, 4, 128), F32),
                ),
                in_specs=whole(2),
                out_specs=whole(2),
                scratch_shapes=[pltpu.VMEM((2 * GRID_ROWS, slots), BF16)],
                compiler_params=params(),
                cost_estimate=pl.CostEstimate(
                    flops=2 * count * slots * 256 * 2 * GRID_ROWS, bytes_accessed=1 << 20, transcendentals=0
                ),
            )(table, held)
        arrive_parts.append(arrive)
        owner += count
    arrive = jnp.concatenate(arrive_parts, axis=0)
    packs = arrive.shape[0]
    mine = jnp.concatenate([table, arrive.reshape(4 * packs, 128)], axis=0)
    with jax.named_scope("exchange_core"):
        other = flip(mine, "blk", 1)
    with jax.named_scope("forces"):
        return pl.pallas_call(
            functools.partial(force_kernel, force_scale, half),
            out_shape=(
                jax.ShapeDtypeStruct((3, slots), F32),
                jax.ShapeDtypeStruct((3, atoms_dev), F32),
            ),
            in_specs=whole(6),
            out_specs=tuple(whole(2)),
            scratch_shapes=[
                pltpu.VMEM((GRID_ROWS, 256), F32),
                pltpu.VMEM((256, 2 * (slots + atoms_dev)), BF16),
            ],
            compiler_params=params(),
        )(
            table,
            other[:GRID_ROWS],
            arrive,
            other[GRID_ROWS:].reshape(packs, 4, 128),
            payload[:, :block],
            key.reshape(1, atoms_dev),
        )


def solution(mesh):
    placed = (
        P(None, ("groups", "blk", "row")),
        P(("groups", "blk", "row")),
        P(("groups", "blk", "row")),
        P(("groups", "blk", "row")),
        P(("groups", "blk", "row")),
        P(None, "blk"),
    )
    return jax.shard_map(
        body,
        mesh=mesh,
        in_specs=placed,
        out_specs=(P(None, ("groups", "blk", "row")), P(None, ("groups", "blk", "row"))),
        check_vma=False,
    )
```

time: 504 us -> 31.3 us (0.06)
  other arithmetic: 431 us -> 0.05 us
  blocking collectives: 34.4 us -> 0 us
  Pallas kernels: 0 us -> 18.2 us
  local copies, waits for them, and re-layouts: 15.5 us -> 3 us
  waiting for transfers between devices: 10.4 us -> 0.94 us
    reduce_sum x3 -> x0, other arithmetic: 231 us -> none  [the longest x1 214 us: phase_sums(): jnp.sum(atom_rows[3][None, :] * jnp.cos(angles), axis=1)]
    sub x1 -> x0, other arithmetic: 193 us -> none  [pull_sum(): jnp.sin(angles) * cos_weighted[:, None]]
    pallas_call x0 -> x6, Pallas kernels: none -> 18.2 us  [the longest x2 8.22 us: wave_weights(): pl.pallas_call(functools.partial(weights_kernel, wave_rows, wave_width, b...]
    all_gather x2 -> x0, blocking collectives: 17.7 us -> none  [the longest x1 9.91 us: body(): lax.all_gather(atom_rows, 'blk', axis=1, tiled=True)]
    psum x1 -> x0, blocking collectives: 16.7 us -> none  [body(): cos_sum, sin_sum = lax.psum((cos_part, sin_part), 'row')]
    all_to_all x2 -> x0, starting transfers between devices: 11 us -> none  [the longest x1 7.39 us: body(): lax.all_to_all(outgoing.reshape(4, devices, pair_cap), ('blk', 'row'), sp...]
    all_to_all x2 -> x0, waiting for transfers between devices: 10.4 us -> none  [the longest x1 5.83 us: body(): lax.all_to_all(homeward.reshape(3, devices, pair_cap), ('blk', 'row'), sp...]
    ppermute x0 -> x4, starting transfers between devices: none -> 7.39 us  [flip(): return lax.ppermute(value, axis, [(i, i ^ bit) for i in range(size)])]
  transfers between devices with their start and end apart: 2 -> 4, of which waited for: 2 -> 1; matrix products, arithmetic and copies ran while one was open for 0% -> 0% of each run, Pallas kernels for 0% -> 39%
where the time goes in v1:
time: 31.3 us; the launch traced here: 31.1 us
  Pallas kernels  18.2 us (58%)
  starting transfers between devices  7.39 us (24%)
  local copies, waits for them, and re-layouts  3 us (10%)
  between operations  1.44 us (5%)
  waiting for transfers between devices  0.94 us (3%)
    pallas_call x2, Pallas kernels, wave_weights(): pl.pallas_call(functools.partial(weights_kernel, wave_rows, wave_width, b...  8.22 us
    pallas_call x2, Pallas kernels, body(): pl.pallas_call(functools.partial(sums_kernel, count, owner, half, cap, ro...  7.51 us
    ppermute x4, starting transfers between devices, flip(): return lax.ppermute(value, axis, [(i, i ^ bit) for i in range(size)])  7.39 us
    pallas_call x1, Pallas kernels, body(): pl.pallas_call(functools.partial(force_kernel, force_scale, half), out_sh...  2.48 us
    unnamed x7, local copies, waits for them, and re-layouts  1.57 us
    ppermute x4, waiting for transfers between devices, flip(): return lax.ppermute(value, axis, [(i, i ^ bit) for i in range(size)])  0.94 us
    reshape x1, local copies, waits for them, and re-layouts, body(): charges.reshape(1, slots)  0.7 us
    reshape x1, local copies, waits for them, and re-layouts, body(): send_slot.reshape(1, slots)  0.69 us
  transfers between devices with their start and end apart: 4, of which 1 were waited for; matrix products, arithmetic and copies ran while one was open for 0% of the time, Pallas kernels for 39%

profile of v1, /device:TPU:0, one launch (start us, length us, event | category | flops | bytes accessed | tf_op | source)
XLA Modules:
  0.0 31.1 jit_solution(14965681738168470963)
XLA Ops:
  0.6 0.0 copy-start.1
  0.6 0.7 %reshape.19.charges_ref = f32[1,768]{1,0:T(1,128)S(1)} reshape(f32[768]{0:T(1024)} %param.7) | data formatting | bytes 6144 | tf_op jit(solution)/shard_map/payload/reshape | solution.py:416
  1.3 0.7 %reshape.20.send_ref = s32[1,768]{1,0:T(1,128)S(1)} reshape(s32[768]{0:T(1024)} %param.9) | data formatting | bytes 6144 | tf_op jit(solution)/shard_map/payload/reshape | solution.py:416
  2.7 0.0 copy-done.1
  2.7 0.0 copy-start
  2.7 0.9 %copy-done = s32[3,6144]{1,0:T(4,128)S(1)} copy-done((s32[3,6144]{1,0:T(4,128)S(1)}, s32[3,6144]{1,0:T(4,128)}, u32[]{:S(2)}) %copy-start) | copy-done | bytes 73752
  3.6 3.0 %collective-permute-start = (f32[8,2816]{1,0:T(8,128)S(1)}, f32[8,2816]{1,0:T(8,128)S(1)}, u32[]{:S(2)}, u32[]{:S(2)}) collective-permute-start(f32[8,2816]{1,0:T(8,128)S(1)} %payload.1.refs_0_), channel_id=1, source_target_pairs={{0,8},{4,12},{8,0},{12,4},{1,9},{5,13},{9,1},{13,5},{2,10},{6,14},... | collective-permute-start | bytes 270344 | tf_op jit(solution)/shard_map/exchange_blk/ppermute | solution.py:420
  6.7 4.1 %shard_map.77.refs_0_ = f32[640,128]{1,0:T(8,128)S(1)} custom-call(f32[8,2816]{1,0:T(8,128)S(1)} %payload.1.refs_0_), custom_call_target="tpu_custom_call" | custom-call | flops 1006632960 | bytes 1048576 | tf_op jit(solution)/shard_map/pallas_call | solution.py:425
  10.8 0.0 collective-permute-done
  10.8 2.7 %collective-permute-start.1 = (f32[8,1024]{1,0:T(8,128)S(1)}, f32[8,1024]{1,0:T(8,128)S(1)}, u32[]{:S(2)}, u32[]{:S(2)}) collective-permute-start(f32[8,1024]{1,0:T(8,128)S(1)} %pad_maximum_fusion.2), channel_id=1, source_target_pairs={{0,2},{1,3},{2,0},{3,1},{4,6},{5,7},{6,4},{7,5},{8,10},{9,11},{10,... | collective-permute-start | bytes 98312 | tf_op jit(solution)/shard_map/exchange_row/ppermute | solution.py:420
  13.5 4.1 %shard_map.78.base_ref = f32[640,128]{1,0:T(8,128)S(1)} custom-call(f32[640,128]{1,0:T(8,128)S(1)} %shard_map.77.refs_0_, f32[8,2304]{1,0:T(8,128)S(1)} %slice.23.refs_1_), custom_call_target="tpu_custom_call" | custom-call | flops 1006632960 | bytes 1048576 | tf_op jit(solution)/shard_map/pallas_call | solution.py:425
  17.6 0.0 collective-permute-done.1
  17.6 1.6 %collective-permute-start.2 = (f32[8,2048]{1,0:T(8,128)S(1)}, f32[8,2048]{1,0:T(8,128)S(1)}, u32[]{:S(2)}, u32[]{:S(2)}) collective-permute-start(f32[8,2048]{1,0:T(8,128)S(1)} %pad_maximum_fusion.1.ions_ref), channel_id=1, source_target_pairs={{0,1},{1,0},{2,3},{3,2},{4,5},{5,4},{6,7},{7,6},{8,9},{9,8},{10,11... | collective-permute-start | bytes 196616 | tf_op jit(solution)/shard_map/exchange_row/ppermute | solution.py:420
  19.2 3.8 %structure_sums.2 = (f32[640,128]{1,0:T(8,128)S(1)}, f32[4,4,128]{2,1,0:T(4,128)S(1)}) custom-call(f32[640,128]{1,0:T(8,128)S(1)} %shard_map.78.base_ref, f32[8,2048]{1,0:T(8,128)S(1)} %pad_maximum_fusion.1.ions_ref), custom_call_target="tpu_custom_call" | custom-call | flops 2013265920 | bytes 1048576 | tf_op jit(solution)/shard_map/structure_sums/pallas_call | solution.py:475
  23.0 0.0 collective-permute-done.2.ions_ref
  23.0 3.8 %structure_sums.3 = (f32[640,128]{1,0:T(8,128)S(1)}, f32[4,4,128]{2,1,0:T(4,128)S(1)}) custom-call(f32[640,128]{1,0:T(8,128)S(1)} %get-tuple-element.6.base_ref, f32[8,2048]{1,0:T(8,128)S(1)} %collective-permute-done.2.ions_ref), custom_call_target="tpu_custom_call" | custom-call | flops 2013265920 | bytes 1048576 | tf_op jit(solution)/shard_map/structure_sums/pallas_call | solution.py:475
  26.8 0.1 collective-permute-start.3
  26.9 0.0 copy-start.2
  26.9 0.7 %copy-done.2 = s32[512]{0:T(512)S(1)} copy-done((s32[512]{0:T(512)S(1)}, s32[512]{0:T(512)}, u32[]{:S(2)}) %copy-start.2) | copy-done | bytes 2072
  27.6 0.9 %collective-permute-done.3 = f32[672,128]{1,0:T(8,128)S(1)} collective-permute-done((f32[672,128]{1,0:T(8,128)S(1)}, f32[672,128]{1,0:T(8,128)S(1)}, u32[]{:S(2)}, u32[]{:S(2)}) %collective-permute-start.3) | collective-permute-done | bytes 344096 | tf_op jit(solution)/shard_map/exchange_core/ppermute | solution.py:420
  28.6 2.5 %forces.1 = (f32[3,768]{1,0:T(4,128)}, f32[3,512]{1,0:T(4,128)}) custom-call(f32[640,128]{1,0:T(8,128)S(1)} %get-tuple-element.7.mine_ref, f32[640,128]{1,0:T(8,128)S(1)} %slice.26.other_ref, f32[8,4,128]{2,1,0:T(4,128)S(1)} %constant_dynamic-update-slice_fusion.arrive_ref, f32[8,4,128]{2,1,0:T(4,128)S(1)} %bitcast.4, f32[8,512]{1,0:T(8,128)S(1)} %slice.24.block_ref, ...), custom_call_target="tpu_custom_call" | custom-call | tf_op jit(solution)/shard_map/forces/pallas_call | solution.py:497
  (12 shorter events, 0.1 us)
Async XLA Ops:
  0.6 2.0 %copy-start.1 = (f32[3,768]{1,0:T(4,128)S(1)}, f32[3,768]{1,0:T(4,128)}, u32[]{:S(2)}) copy-start(f32[3,768]{1,0:T(4,128)} %coords_ref.1) | copy-start | bytes 27652
  2.7 0.9 %copy-start = (s32[3,6144]{1,0:T(4,128)S(1)}, s32[3,6144]{1,0:T(4,128)}, u32[]{:S(2)}) copy-start(s32[3,6144]{1,0:T(4,128)} %waves_ref.1) | copy-start | bytes 221188
  3.6 7.1 %collective-permute-start = (f32[8,2816]{1,0:T(8,128)S(1)}, f32[8,2816]{1,0:T(8,128)S(1)}, u32[]{:S(2)}, u32[]{:S(2)}) collective-permute-start(f32[8,2816]{1,0:T(8,128)S(1)} %payload.1.refs_0_), channel_id=1, source_target_pairs={{0,8},{4,12},{8,0},{12,4},{1,9},{5,13},{9,1},{13,5},{2,10},{6,14},... | collective-permute-start | bytes 270344 | tf_op jit(solution)/shard_map/exchange_blk/ppermute | solution.py:420
  10.8 6.8 %collective-permute-start.1 = (f32[8,1024]{1,0:T(8,128)S(1)}, f32[8,1024]{1,0:T(8,128)S(1)}, u32[]{:S(2)}, u32[]{:S(2)}) collective-permute-start(f32[8,1024]{1,0:T(8,128)S(1)} %pad_maximum_fusion.2), channel_id=1, source_target_pairs={{0,2},{1,3},{2,0},{3,1},{4,6},{5,7},{6,4},{7,5},{8,10},{9,11},{10,... | collective-permute-start | bytes 98312 | tf_op jit(solution)/shard_map/exchange_row/ppermute | solution.py:420
  17.6 5.4 %collective-permute-start.2 = (f32[8,2048]{1,0:T(8,128)S(1)}, f32[8,2048]{1,0:T(8,128)S(1)}, u32[]{:S(2)}, u32[]{:S(2)}) collective-permute-start(f32[8,2048]{1,0:T(8,128)S(1)} %pad_maximum_fusion.1.ions_ref), channel_id=1, source_target_pairs={{0,1},{1,0},{2,3},{3,2},{4,5},{5,4},{6,7},{7,6},{8,9},{9,8},{10,11... | collective-permute-start | bytes 196616 | tf_op jit(solution)/shard_map/exchange_row/ppermute | solution.py:420
  26.8 1.7 %collective-permute-start.3 = (f32[672,128]{1,0:T(8,128)S(1)}, f32[672,128]{1,0:T(8,128)S(1)}, u32[]{:S(2)}, u32[]{:S(2)}) collective-permute-start(f32[672,128]{1,0:T(8,128)S(1)} %pad_maximum_fusion), channel_id=1, source_target_pairs={{0,4},{4,0},{8,12},{12,8},{1,5},{5,1},{9,13},{13,9},{2,6},{6,2},{1... | collective-permute-start | bytes 1032200 | tf_op jit(solution)/shard_map/exchange_core/ppermute | solution.py:420
  26.9 0.7 %copy-start.2 = (s32[512]{0:T(512)S(1)}, s32[512]{0:T(512)}, u32[]{:S(2)}) copy-start(s32[512]{0:T(512)} %param.10) | copy-start | bytes 6148

commit v2 on v1

v2 whole, which is shorter than its diff:
```python
import functools
import math

import jax
import jax.numpy as jnp
from jax import lax
from jax.experimental import pallas as pl
from jax.experimental.pallas import tpu as pltpu
from jax.sharding import PartitionSpec as P

DOUBLE_PI = 2.0 * math.pi
EWALD_BETA = 30.0
BOX_Z = 3.0
FORCE_GAIN = 400.0
SIN_POLY = (6.283185, -41.34159, 81.599945, -76.61447, 41.342884, -12.471244)
COS_POLY = (1.0, -19.739204, 64.93912, -85.45014, 60.16763, -25.9676, 6.5286584)

BASIS = 24
PAIR_ROWS = 600
GRID_ROWS = 640
HARM = 40
WEIGHT_LANE = 80
COUNT_PAIRS = 200
COUNT_ROWS = 240
F32 = jnp.float32
BF16 = jnp.bfloat16
NT = (((1,), (1,)), ((), ()))
VMEM_BYTES = 40 * 1024 * 1024


def horner(coefs, v):
    total = jnp.full_like(v, coefs[-1])
    for coef in coefs[-2::-1]:
        total = total * v + coef
    return total


def first_harmonics(pos):
    harm = lax.broadcasted_iota(jnp.int32, (8, pos.shape[1]), 0).astype(F32) + 1.0
    turns = harm * pos
    turns = turns - jnp.floor(turns + 0.5)
    square = turns * turns
    return horner(COS_POLY, square), turns * horner(SIN_POLY, square)


def advance(first, by):
    cos_a, sin_a = first
    cos_b, sin_b = by[0][7:8], by[1][7:8]
    return cos_a * cos_b - sin_a * sin_b, sin_a * cos_b + cos_a * sin_b


def merge_last(cos_part, sin_part):
    low = lax.broadcasted_iota(jnp.int32, cos_part.shape, 0) < 4
    return jnp.where(low, cos_part, pltpu.roll(sin_part, 4, 0))


def short_basis(pos):
    first = first_harmonics(pos)
    second = advance(first, first)
    return [first[0], first[1], merge_last(*second)]


def short_slopes(basis):
    row = lax.broadcasted_iota(jnp.int32, basis[0].shape, 0)
    harm = row.astype(F32) + 1.0
    low = row < 4
    factor = jnp.where(low, -(harm + 8.0), harm + 4.0)
    return [-harm * basis[1], harm * basis[0], factor * pltpu.roll(basis[2], 4, 0)]


def long_basis(pos):
    first = first_harmonics(pos)
    second = advance(first, first)
    third = advance(first, second)
    fourth = advance(second, second)
    fifth = advance(first, fourth)
    parts = (first, second, third, fourth, fifth)
    return [p[0] for p in parts], [p[1] for p in parts]


def split_two(value):
    high = value.astype(BF16)
    return high, (value - high.astype(F32)).astype(BF16)


def key_of_rows(recv, device, cap, row_count, bits):
    per_pack = 64 // cap
    source = (recv // cap) ^ device
    order = jnp.zeros_like(source)
    for place, distance in enumerate(bits):
        order = order | jnp.where((source & distance) != 0, 1 << place, 0)
    far = jnp.where((source & row_count) != 0, 64, 0)
    return (order // per_pack) * 128 + far + (order % per_pack) * cap + recv % cap


def prep_kernel(
    coords_hbm, charges_hbm, counts_hbm, send_hbm, waves_hbm, out_ref, waves_out_ref,
    coords_ref, charges_ref, counts_ref, send_ref, waves_ref, sems,
):
    copies = [
        pltpu.make_async_copy(source, target, sems.at[i])
        for i, (source, target) in enumerate(
            (
                (waves_hbm, waves_ref),
                (counts_hbm, counts_ref),
                (send_hbm, send_ref),
                (charges_hbm, charges_ref),
                (coords_hbm, coords_ref),
            )
        )
    ]
    for copy in copies:
        copy.start()
    slots = charges_ref.shape[0]
    half = slots // 2
    out_ref[:, 0 : half + 128] = jnp.zeros((8, half + 128), F32)
    for copy in copies:
        copy.wait()
    live = lax.broadcasted_iota(jnp.int32, (1, slots), 1) < counts_ref[0]
    charge = jnp.where(live, charges_ref[...].reshape(1, slots), 0.0)
    send = jnp.where(live, send_ref[...].reshape(1, slots), -1).astype(F32)
    for part in range(2):
        lanes = slice(part * half, (part + 1) * half)
        out_ref[4 * part : 4 * part + 3, 0:half] = coords_ref[:, lanes]
        out_ref[4 * part + 3 : 4 * part + 4, 0:half] = charge[:, lanes]
    for piece in range(slots // 128):
        out_ref[piece : piece + 1, half : half + 128] = send[:, piece * 128 : (piece + 1) * 128]
    rows, width = wave_shape(waves_ref.shape[1])
    for row in range(rows):
        for comp in range(3):
            waves_out_ref[row : row + 1, comp * width : (comp + 1) * width] = waves_ref[
                comp : comp + 1, row * width : (row + 1) * width
            ].astype(F32)


def wave_shape(k_local):
    rows = 8
    while k_local % (rows * 128):
        rows //= 2
    return rows, k_local // rows


def basis_row(index):
    size = jnp.abs(index)
    sign = jnp.where(index < 0.0, 1.0, 0.0)
    row = jnp.where(size <= 8.0, size - 1.0 + 8.0 * sign, size + 7.0 + 4.0 * sign)
    return jnp.where(size == 0.0, float(BASIS), row)


def compact_weights():
    row = lax.broadcasted_iota(jnp.int32, (COUNT_ROWS, 128), 0)
    lane = lax.broadcasted_iota(jnp.int32, (COUNT_ROWS, 128), 1)
    paired = row < COUNT_PAIRS
    row_x = jnp.where(paired, row // 8, jnp.minimum(row - COUNT_PAIRS, BASIS))
    part = jnp.where(lane < HARM, 0, jnp.where(lane < 2 * HARM, 1, 2))
    row_y = jnp.where(paired, row % 8 + 8 * part, BASIS)
    phys_x = DOUBLE_PI * basis_size(row_x).astype(F32)
    phys_y = DOUBLE_PI * basis_size(row_y).astype(F32)
    phys_z = DOUBLE_PI * (lane - HARM * part + 1).astype(F32) / BOX_Z
    k_squared = phys_x * phys_x + phys_y * phys_y + phys_z * phys_z
    return jnp.exp(-k_squared / (4.0 * EWALD_BETA * EWALD_BETA)) / k_squared


def basis_size(row):
    low = jnp.where(row < 8, row, row - 8) + 1
    high = jnp.where(row < 20, row - 16, row - 20) + 9
    return jnp.where(row < 16, low, jnp.where(row < BASIS, high, 0))


def count_waves(waves, rows, width):
    wave_h = waves[0:rows, 0:width]
    wave_k = waves[0:rows, width : 2 * width]
    wave_l = waves[0:rows, 2 * width : 3 * width]
    flip = jnp.where(wave_l < 0.0, -1.0, 1.0)
    row_x = basis_row(wave_h * flip)
    row_y = basis_row(wave_k * flip)
    part = jnp.where(row_y >= 16.0, 2.0, jnp.where(row_y >= 8.0, 1.0, 0.0))
    const = row_y == float(BASIS)
    part = jnp.where(const, 0.0, part)
    row_id = jnp.where(const, COUNT_PAIRS + row_x, 8.0 * (row_x - part) + row_y)
    lane_id = wave_l * flip + (HARM * part - 1.0)
    step = lax.broadcasted_iota(jnp.int32, (16, width), 0).astype(F32)
    steps = [(step + 16.0 * i).astype(BF16) for i in range(COUNT_ROWS // 16)]
    one = jnp.ones((16, width), BF16)
    none = jnp.zeros((16, width), BF16)
    total = None
    for piece in range(rows):
        rows_at = jnp.broadcast_to(row_id[piece : piece + 1], (16, width)).astype(BF16)
        lanes_at = jnp.broadcast_to(lane_id[piece : piece + 1], (16, width)).astype(BF16)
        row_hot = jnp.concatenate([jnp.where(rows_at == at, one, none) for at in steps], axis=0)
        lane_hot = jnp.concatenate([jnp.where(lanes_at == at, one, none) for at in steps[:8]], axis=0)
        part = lax.dot_general(row_hot, lane_hot, NT, preferred_element_type=F32)
        total = part if total is None else total + part
    return total


def spread_weights(counts, table_ref):
    weights = counts * compact_weights()
    lane = lax.broadcasted_iota(jnp.int32, (8, 128), 1)
    inside = jnp.logical_and(lane >= WEIGHT_LANE, lane < WEIGHT_LANE + HARM)
    for x in range(BASIS + 1):
        tile = weights[8 * x : 8 * x + 8]
        for part in range(3):
            row = BASIS * x + 8 * part
            moved = tile if part == 2 else pltpu.roll(tile, WEIGHT_LANE - HARM * part, 1)
            table_ref[row : row + 8] += jnp.where(inside, moved, 0.0)
    for block in range(4):
        moved = pltpu.roll(weights[COUNT_PAIRS + 8 * block : COUNT_PAIRS + 8 * block + 8], WEIGHT_LANE, 1)
        table_ref[PAIR_ROWS + 8 * block : PAIR_ROWS + 8 * block + 8] += jnp.where(inside, moved, 0.0)


def add_owner(block_rows, half, cap, place, pack, targets, table_ref, v_ref):
    block = half + 128
    slots = 2 * half

    def comp(index):
        return jnp.concatenate(
            [block_rows[index : index + 1, 0:half], block_rows[index + 4 : index + 5, 0:half]], axis=1
        )

    charge = comp(3)
    basis_x = [charge * rows for rows in short_basis(comp(0))]
    basis_y = jnp.concatenate(short_basis(comp(1)), axis=0)
    cos_z, sin_z = long_basis(comp(2))
    for row in range(0, BASIS, 2):
        pair = [basis_x[r // 8][r % 8 : r % 8 + 1] * basis_y for r in (row, row + 1)]
        high, low = split_two(jnp.concatenate(pair, axis=0))
        v_ref[row * BASIS : (row + 2) * BASIS] = high
        v_ref[GRID_ROWS + row * BASIS : GRID_ROWS + (row + 2) * BASIS] = low
    first_row = lax.broadcasted_iota(jnp.int32, (8, slots), 0) == 0
    const_x = jnp.where(first_row, jnp.broadcast_to(charge, (8, slots)), 0.0)
    none = jnp.zeros((8, slots), F32)
    tail = jnp.concatenate([charge * basis_y] + basis_x + [const_x, none], axis=0)
    high, low = split_two(tail)
    v_ref[BASIS * BASIS : GRID_ROWS] = high
    v_ref[GRID_ROWS + BASIS * BASIS : 2 * GRID_ROWS] = low
    high, low = split_two(jnp.concatenate(cos_z + sin_z, axis=0))
    gap = jnp.zeros((128 - 2 * HARM, slots), BF16)
    table_z = jnp.concatenate([high, gap, low, gap], axis=0)
    part = lax.dot_general(v_ref[...], table_z, NT, preferred_element_type=F32)
    table_ref[:GRID_ROWS] += part[:GRID_ROWS, :128] + (part[:GRID_ROWS, 128:] + part[GRID_ROWS:, :128])

    send = jnp.concatenate([block_rows[p : p + 1, half:block] for p in range(slots // 128)], axis=1)
    hot_iota = lax.broadcasted_iota(jnp.int32, (64, slots), 0).astype(F32)
    hots = []
    for target in targets:
        rank = send - (target * cap).astype(F32)
        valid = jnp.logical_and(rank >= 0.0, rank < float(cap))
        key = jnp.where(valid, rank + place, -1.0)
        hots.append(jnp.where(hot_iota == key, 1.0, 0.0).astype(BF16))
    values = jnp.concatenate([comp(0), comp(1), comp(2), charge, jnp.zeros((4, slots), F32)], axis=0)
    found = lax.dot_general(split_three(values), jnp.concatenate(hots, axis=0), NT, preferred_element_type=F32)
    row = GRID_ROWS + 8 * pack
    if not isinstance(row, int):
        row = pl.multiple_of(row, 8)
    table_ref[pl.ds(row, 8)] += (found[0:8] + found[8:16]) + found[16:24]


def split_three(value):
    high = value.astype(BF16).astype(F32)
    rest = value - high
    mid = rest.astype(BF16).astype(F32)
    return jnp.concatenate([high, mid, rest - mid], axis=0).astype(BF16)


def sums_kernel(plan, *refs):
    refs = list(refs)
    base_ref = refs.pop(0) if plan["has_base"] else None
    counts_ref = refs.pop(0) if plan["has_counts"] else None
    wave_refs = [refs.pop(0) for _ in plan["pieces"]]
    ion_refs = [refs.pop(0) for _ in plan["chunks"]]
    table_ref = refs.pop(0) if plan["table"] else None
    counts_out_ref = refs.pop(0) if plan["pieces"] else None
    v_ref = refs.pop(0)
    half, cap, row_count = plan["half"], plan["cap"], plan["row_count"]
    rows, width = plan["wave_shape"]
    block = half + 128
    per_pack = 64 // cap
    counts = None if counts_ref is None else counts_ref[...]
    for ref, pieces in zip(wave_refs, plan["pieces"]):
        for piece in range(pieces):
            part = count_waves(ref[:, 3 * width * piece : 3 * width * (piece + 1)], rows, width)
            counts = part if counts is None else counts + part
    if counts_out_ref is not None:
        counts_out_ref[...] = counts
    if table_ref is None:
        return
    device = lax.axis_index("blk") * row_count + lax.axis_index("row")
    targets = (device, device ^ row_count)
    table_ref[...] = jnp.zeros_like(table_ref) if base_ref is None else base_ref[...]
    if plan["spread"]:
        spread_weights(counts, table_ref)
    turn = 0
    for ref, (owners, first_owner) in zip(ion_refs, plan["chunks"]):
        if owners <= 4 and per_pack == 1:
            for owner in range(owners):
                add_owner(
                    ref[:, owner * block : (owner + 1) * block], half, cap, 0.0, first_owner + owner, targets,
                    table_ref, v_ref.at[turn % 2],
                )
                turn += 1
        else:

            def step(owner, carry, ref=ref, first_owner=first_owner):
                begin = pl.multiple_of(owner * block, 128)
                index = first_owner + owner
                add_owner(
                    ref[:, pl.ds(begin, block)], half, cap, (lax.rem(index, per_pack) * cap).astype(F32),
                    index // per_pack, targets, table_ref, v_ref.at[0],
                )
                return carry

            lax.fori_loop(0, owners, step, 0)


def store_bases(ions, basis_ref, z_ref):
    count = ions.shape[1]
    basis_x = short_basis(ions[0:1])
    basis_y = short_basis(ions[1:2])
    parts = basis_x + basis_y + short_slopes(basis_x) + short_slopes(basis_y)
    for i, part in enumerate(parts):
        basis_ref[8 * i : 8 * i + 8] = part
    cos_z, sin_z = (jnp.concatenate(rows, axis=0) for rows in long_basis(ions[2:3]))
    harm = lax.broadcasted_iota(jnp.int32, (HARM, count), 0).astype(F32) + 1.0
    plain = jnp.concatenate([cos_z, sin_z], axis=0)
    slope = jnp.concatenate([-harm * sin_z, harm * cos_z], axis=0)
    for i, table in enumerate((plain, slope)):
        high, low = split_two(table)
        z_ref[:, i * count : (i + 1) * count] = jnp.concatenate(
            [high, low, high, jnp.zeros((256 - 6 * HARM, count), BF16)], axis=0
        )


def own_kernel(half, cap, row_count, bits, data_ref, recv_ref, basis_ref, z_ref, hot_ref):
    store_bases(jnp.concatenate([data_ref[0:4, 0:half], data_ref[4:8, 0:half]], axis=1), basis_ref, z_ref)
    atoms_dev = recv_ref.shape[0]
    device = lax.axis_index("blk") * row_count + lax.axis_index("row")
    key = key_of_rows(recv_ref[...].reshape(1, atoms_dev), device, cap, row_count, bits)
    spot = lax.broadcasted_iota(jnp.int32, hot_ref.shape, 0)
    hot_ref[...] = jnp.where(spot == key, 1.0, 0.0).astype(BF16)


def force_kernel(
    force_scale, half, mine_ref, other_ref, data_ref, basis_ref, z_ref, hot_ref, slot_ref, atom_ref,
    w_ref, atom_basis_ref, atom_z_ref,
):
    slots = 2 * half
    atoms_dev = hot_ref.shape[1]
    packs = (mine_ref.shape[0] - GRID_ROWS) // 8
    lane = lax.broadcasted_iota(jnp.int32, (8, 128), 1)
    starts = [GRID_ROWS + 8 * p for p in range(packs)]
    pool = jnp.concatenate([jnp.where(lane < 64, mine_ref[r : r + 8], other_ref[r : r + 8]) for r in starts], axis=1)
    found = jnp.dot(split_three(pool), hot_ref[...], preferred_element_type=F32)
    routed = ((found[0:8] + found[8:16]) + found[16:24])[0:4]
    store_bases(routed, atom_basis_ref, atom_z_ref)
    lane = lax.broadcasted_iota(jnp.int32, (8, 128), 1)
    is_cos = lane < HARM
    is_wave = lane < 2 * HARM
    low_rows = lax.broadcasted_iota(jnp.int32, (8, 128), 0) < 4

    def fields(row):
        tile = mine_ref[row : row + 8] + other_ref[row : row + 8]
        sums = jnp.where(is_wave, tile, 0.0)
        gain = jnp.where(is_cos, pltpu.roll(tile, 48, 1), jnp.where(is_wave, pltpu.roll(tile, 88, 1), 0.0))
        turned = jnp.where(
            is_cos, pltpu.roll(sums, 88, 1), jnp.where(is_wave, -pltpu.roll(sums, HARM, 1), 0.0)
        )
        return gain, sums, turned

    def swap(parts):
        return [parts[1], parts[0], pltpu.roll(parts[2], 4, 0)]

    def store(row, value):
        high, low = split_two(value)
        high = high.astype(F32)
        low = low.astype(F32)
        turned = pltpu.roll(high, 2 * HARM, 1)
        w_ref[row : row + 8, 0:128] = jnp.where(is_wave, high, turned)
        w_ref[row : row + 8, 128:256] = jnp.where(lane < 32, turned, pltpu.roll(low, 32, 1))

    def combine(x_rows, x_other):
        gain, sums, turned = x_rows
        swapped_gain, swapped_sums, swapped_turned = swap(gain), swap(sums), swap(turned)
        both = [a + b for a, b in zip(gain, swapped_gain)]
        odd = [a - b for a, b in zip(gain, swapped_gain)]
        if x_other is None:
            return [both[i] * sums[i] - odd[i] * swapped_turned[i] for i in range(3)]
        gain_o, sums_o, turned_o = x_other
        swapped_gain_o, swapped_sums_o = swap(gain_o), swap(sums_o)
        both_o = [a + b for a, b in zip(gain_o, swapped_gain_o)]
        odd_o = [a - b for a, b in zip(gain_o, swapped_gain_o)]
        return [
            (both[i] + both_o[i]) * sums[i]
            - (odd[i] + odd_o[i]) * swapped_turned[i]
            - (both[i] - both_o[i]) * turned_o[i]
            - (odd[i] - odd_o[i]) * swapped_sums_o[i]
            for i in range(3)
        ]

    def group(x):
        parts = [fields(BASIS * x + 8 * i) for i in range(3)]
        return [[p[j] for p in parts] for j in range(3)]

    pairs = [(x, x + 8) for x in range(8)] + [(x, x + 4) for x in range(16, 20)]
    for x, other in pairs:
        group_x, group_o = group(x), group(other)
        for i, value in enumerate(combine(group_x, group_o)):
            store(BASIS * x + 8 * i, value)
        for i, value in enumerate(combine(group_o, group_x)):
            store(BASIS * other + 8 * i, value)
    for i, value in enumerate(combine(group(BASIS), None)):
        store(BASIS * BASIS + 8 * i, value)
    last = [fields(PAIR_ROWS + 8 * i) for i in range(4)]
    gain, sums, turned = [[p[j] for p in last] for j in range(3)]
    gain_s, turned_s = swap(gain), swap(turned)
    for i in range(3):
        store(
            PAIR_ROWS + 8 * i,
            (gain[i] + gain_s[i]) * sums[i] - (gain[i] - gain_s[i]) * turned_s[i],
        )
    store(PAIR_ROWS + 24, gain[3] * sums[3])
    w_ref[PAIR_ROWS + 32 :] = jnp.zeros((GRID_ROWS - PAIR_ROWS - 32, 256), F32)
    weights = w_ref[...].astype(BF16)
    tile = 256
    charge = jnp.concatenate([data_ref[3:4, 0:half], data_ref[7:8, 0:half]], axis=1)
    jobs = [(basis_ref, z_ref, charge, slot_ref, slots, begin) for begin in range(0, slots, tile)]
    jobs += [(atom_basis_ref, atom_z_ref, routed[3:4], atom_ref, atoms_dev, begin) for begin in range(0, atoms_dev, tile)]
    for rows_ref, table_ref, charges, out_ref, count, begin in jobs:
        lanes = slice(begin, begin + tile)
        plain = jnp.dot(weights, table_ref[:, begin : begin + tile], preferred_element_type=F32)
        sloped = jnp.dot(weights, table_ref[:, count + begin : count + begin + tile], preferred_element_type=F32)
        sum_x = jnp.zeros((8, tile), F32)
        sum_y = jnp.zeros((8, tile), F32)
        sum_z = jnp.zeros((8, tile), F32)
        rows_y = [rows_ref[24 + 8 * i : 32 + 8 * i, lanes] for i in range(3)]
        rows_dy = [rows_ref[72 + 8 * i : 80 + 8 * i, lanes] for i in range(3)]
        for x in range(BASIS + 1):
            part_x = part_y = part_z = 0.0
            for i in range(3):
                row = BASIS * x + 8 * i
                part_x = part_x + rows_y[i] * plain[row : row + 8]
                part_y = part_y + rows_dy[i] * plain[row : row + 8]
                part_z = part_z + rows_y[i] * sloped[row : row + 8]
            if x < BASIS:
                basis = rows_ref[x : x + 1, lanes]
                sum_x = sum_x + rows_ref[48 + x : 49 + x, lanes] * part_x
                sum_y = sum_y + basis * part_y
                sum_z = sum_z + basis * part_z
            else:
                sum_y = sum_y + part_y
                sum_z = sum_z + part_z
        for i in range(3):
            row = PAIR_ROWS + 8 * i
            sum_x = sum_x + rows_ref[48 + 8 * i : 56 + 8 * i, lanes] * plain[row : row + 8]
            sum_z = sum_z + rows_ref[8 * i : 8 * i + 8, lanes] * sloped[row : row + 8]
        sum_z = sum_z + sloped[PAIR_ROWS + 24 : PAIR_ROWS + 32]
        gain = (-DOUBLE_PI * force_scale) * charges[:, lanes]
        out_ref[:, lanes] = jnp.concatenate(
            [
                gain * jnp.sum(sum_x, axis=0, keepdims=True),
                gain * jnp.sum(sum_y, axis=0, keepdims=True),
                (gain / BOX_Z) * jnp.sum(sum_z, axis=0, keepdims=True),
            ],
            axis=0,
        )


def params():
    return pltpu.CompilerParams(vmem_limit_bytes=VMEM_BYTES)


def stay(value):
    return pltpu.with_memory_space_constraint(value, pltpu.HBM)


def whole(count):
    return [pl.BlockSpec(memory_space=pltpu.VMEM)] * count


def body(coords, charges, counts, send_slot, recv_index, wave_ints):
    slots = charges.shape[0]
    half = slots // 2
    block = half + 128
    atoms_dev = recv_index.shape[0]
    devices = lax.axis_size(("blk", "row"))
    blk_count = lax.axis_size("blk")
    row_count = lax.axis_size("row")
    k_local = wave_ints.shape[1]
    cap = 2 * atoms_dev // devices
    packs = max(1, devices // 2 * cap // 64)
    wave_rows, wave_width = wave_shape(k_local)
    force_scale = FORCE_GAIN / math.sqrt(float(atoms_dev * devices * blk_count * k_local))
    table_shape = jax.ShapeDtypeStruct((GRID_ROWS + 8 * packs, 128), F32)
    count_shape = jax.ShapeDtypeStruct((COUNT_ROWS, 128), F32)

    with jax.named_scope("payload"):
        own_ions, own_waves = pl.pallas_call(
            prep_kernel,
            out_shape=(
                jax.ShapeDtypeStruct((8, block), F32),
                jax.ShapeDtypeStruct((wave_rows, 3 * wave_width), F32),
            ),
            in_specs=[pl.BlockSpec(memory_space=pltpu.HBM)] * 5,
            out_specs=tuple(whole(2)),
            scratch_shapes=[
                pltpu.VMEM(coords.shape, F32),
                pltpu.VMEM(charges.shape, F32),
                pltpu.SMEM(counts.shape, jnp.int32),
                pltpu.VMEM(send_slot.shape, jnp.int32),
                pltpu.VMEM(wave_ints.shape, jnp.int32),
                pltpu.SemaphoreType.DMA((5,)),
            ],
            compiler_params=params(),
        )(stay(coords), stay(charges), counts, stay(send_slot), stay(wave_ints))

    def flip(value, axis, bit):
        size = lax.axis_size(axis)
        return lax.ppermute(value, axis, [(i, i ^ bit) for i in range(size)])

    def accumulate(table, counted, pieces, chunks, spread):
        plan = {
            "has_base": table is not None and bool(chunks),
            "has_counts": counted is not None and (bool(pieces) or spread),
            "pieces": [count for _, count in pieces],
            "chunks": [tuple(chunk[1:]) for chunk in chunks],
            "table": bool(chunks),
            "spread": spread,
            "half": half,
            "cap": cap,
            "row_count": row_count,
            "wave_shape": (wave_rows, wave_width),
        }
        args = [table] * plan["has_base"] + [counted] * plan["has_counts"]
        args += [piece[0] for piece in pieces] + [chunk[0] for chunk in chunks]
        shapes = (table_shape,) * plan["table"] + (count_shape,) * bool(pieces)
        flops = sum(2 * chunk[1] * slots * 256 * 2 * GRID_ROWS for chunk in chunks)
        flops += sum(2 * piece[1] * k_local * COUNT_ROWS * 256 for piece in pieces)
        with jax.named_scope("structure_sums"):
            out = pl.pallas_call(
                functools.partial(sums_kernel, plan),
                out_shape=shapes,
                in_specs=whole(len(args)),
                out_specs=tuple(whole(len(shapes))),
                scratch_shapes=[pltpu.VMEM((2, 2 * GRID_ROWS, slots), BF16)],
                compiler_params=params(),
                cost_estimate=pl.CostEstimate(flops=flops, bytes_accessed=1 << 20, transcendentals=0),
            )(*args)
        return (out[0] if chunks else table), (out[-1] if pieces else counted)

    steps = []
    bit = 2
    while bit < blk_count:
        steps.append(("blk", bit, row_count * bit))
        bit *= 2
    bit = row_count // 2
    while bit >= 1:
        steps.append(("row", bit, bit))
        bit //= 2
    bits = [distance for _, _, distance in steps]
    with jax.named_scope("own_ions"):
        basis, table_z, hot = pl.pallas_call(
            functools.partial(own_kernel, half, cap, row_count, bits),
            out_shape=(
                jax.ShapeDtypeStruct((96, slots), F32),
                jax.ShapeDtypeStruct((256, 2 * slots), BF16),
                jax.ShapeDtypeStruct((128 * packs, atoms_dev), BF16),
            ),
            in_specs=whole(2),
            out_specs=tuple(whole(3)),
            compiler_params=params(),
            cost_estimate=pl.CostEstimate(flops=1 << 30, bytes_accessed=1 << 20, transcendentals=0),
        )(own_ions, recv_index)
    table, counted = None, None
    ions, waves = [own_ions], [own_waves]
    pieces, chunks = [(own_waves, 1)], [(own_ions, 1, 0)]
    held, counted_sets, spread_done = 1, 0, False
    for axis, bit, _ in steps:
        with jax.named_scope("exchange_" + axis):
            got = flip(ions[0] if len(ions) == 1 else jnp.concatenate(ions, axis=1), axis, bit)
            if axis == "blk":
                got_waves = flip(waves[0] if len(waves) == 1 else jnp.concatenate(waves, axis=1), axis, bit)
        spread = not spread_done and counted_sets == max(1, blk_count // 2)
        table, counted = accumulate(table, counted, pieces, chunks, spread)
        got, table, counted = lax.optimization_barrier((got, table, counted))
        spread_done = spread_done or spread
        counted_sets += sum(piece[1] for piece in pieces)
        chunks = [(got, held, held)]
        pieces = []
        if axis == "blk":
            pieces = [(got_waves, held)]
            waves = waves + [got_waves]
        ions = ions + [got]
        held *= 2
    table, counted = accumulate(table, counted, pieces, chunks, not spread_done)
    with jax.named_scope("exchange_core"):
        other = flip(table, "blk", 1)
    with jax.named_scope("forces"):
        return pl.pallas_call(
            functools.partial(force_kernel, force_scale, half),
            out_shape=(
                jax.ShapeDtypeStruct((3, slots), F32),
                jax.ShapeDtypeStruct((3, atoms_dev), F32),
            ),
            in_specs=whole(6),
            out_specs=tuple(whole(2)),
            scratch_shapes=[
                pltpu.VMEM((GRID_ROWS, 256), F32),
                pltpu.VMEM((96, atoms_dev), F32),
                pltpu.VMEM((256, 2 * atoms_dev), BF16),
            ],
            compiler_params=params(),
        )(table, other, own_ions, basis, table_z, hot)


def solution(mesh):
    placed = (
        P(None, ("groups", "blk", "row")),
        P(("groups", "blk", "row")),
        P(("groups", "blk", "row")),
        P(("groups", "blk", "row")),
        P(("groups", "blk", "row")),
        P(None, "blk"),
    )
    return jax.shard_map(
        body,
        mesh=mesh,
        in_specs=placed,
        out_specs=(P(None, ("groups", "blk", "row")), P(None, ("groups", "blk", "row"))),
        check_vma=False,
    )
```

time: 31.3 us -> 23.1 us (0.74)
  Pallas kernels: 18.2 us -> 10.7 us
  local copies, waits for them, and re-layouts: 3 us -> 0.01 us
  waiting for transfers between devices: 0.94 us -> 2.56 us
  starting transfers between devices: 7.39 us -> 8.25 us
    pallas_call x5 -> x6, Pallas kernels: 15.8 us -> 8.53 us  [the longest x4 7.15 us: accumulate(): pl.pallas_call(functools.partial(sums_kernel, plan), out_shape=shapes, in...]
    ppermute x4 -> x5, waiting for transfers between devices: 0.94 us -> 2.56 us  [flip(): return lax.ppermute(value, axis, [(i, i ^ bit) for i in range(size)])]
    unnamed x7 -> x2, local copies, waits for them, and re-layouts: 1.57 us -> 0.01 us
    reshape x2 -> x0, local copies, waits for them, and re-layouts: 1.38 us -> none  [the longest x1 0.7 us: body(): charges.reshape(1, slots)]
    ppermute x4 -> x5, starting transfers between devices: 7.39 us -> 8.25 us  [flip(): return lax.ppermute(value, axis, [(i, i ^ bit) for i in range(size)])]
  transfers between devices with their start and end apart: 4 -> 5, of which waited for: 1 -> 4; matrix products, arithmetic and copies ran while one was open for 0% -> 0% of each run, Pallas kernels for 39% -> 22%
where the time goes in v2:
time: 23.1 us; the launch traced here: 22.9 us
  Pallas kernels  10.7 us (46%)
  starting transfers between devices  8.25 us (36%)
  waiting for transfers between devices  2.56 us (11%)
  between operations  1.34 us (6%)
    ppermute x5, starting transfers between devices, flip(): return lax.ppermute(value, axis, [(i, i ^ bit) for i in range(size)])  8.25 us
    pallas_call x4, Pallas kernels, accumulate(): pl.pallas_call(functools.partial(sums_kernel, plan), out_shape=shapes, in...  7.15 us
    ppermute x5, waiting for transfers between devices, flip(): return lax.ppermute(value, axis, [(i, i ^ bit) for i in range(size)])  2.56 us
    pallas_call x1, Pallas kernels, body(): pl.pallas_call(functools.partial(force_kernel, force_scale, half), out_sh...  2.21 us
    pallas_call x1, Pallas kernels, body(): pl.pallas_call(prep_kernel, out_shape=(jax.ShapeDtypeStruct((8, block), F...  0.98 us
  transfers between devices with their start and end apart: 5, of which 4 were waited for; matrix products, arithmetic and copies ran while one was open for 0% of the time, Pallas kernels for 22%

profile of v2, /device:TPU:0, one launch (start us, length us, event | category | flops | bytes accessed | tf_op | source)
XLA Modules:
  0.0 22.9 jit_solution(7193863297827561850)
XLA Ops:
  1.3 1.0 %payload.1 = (f32[8,512]{1,0:T(8,128)S(1)}, f32[8,2304]{1,0:T(8,128)S(1)}) custom-call(f32[3,768]{1,0:T(4,128)} %coords_hbm.1, f32[768]{0:T(1024)} %charges_hbm.1, s32[1]{0:T(128)S(6)} %copy.8.counts_hbm, s32[768]{0:T(1024)} %send_hbm.1, s32[3,6144]{1,0:T(4,128)} %waves_hbm.1), custom_call_target="tpu_custom_call" | custom-call | tf_op jit(solution)/shard_map/payload/pallas_call | solution.py:497
  2.3 3.0 %collective-permute-start = (f32[8,512]{1,0:T(8,128)S(1)}, f32[8,512]{1,0:T(8,128)S(1)}, u32[]{:S(2)}, u32[]{:S(2)}) collective-permute-start(f32[8,512]{1,0:T(8,128)S(1)} %get-tuple-element.19.refs_1_.data_ref), channel_id=1, source_target_pairs={{0,8},{4,12},{8,0},{12,4},{1,9},{5,13},{9,1},{13,5},{2,10},{6,14},... | collective-permute-start | bytes 49160 | tf_op jit(solution)/shard_map/exchange_blk/ppermute | solution.py:518
  5.3 0.1 collective-permute-start.2
  5.4 1.5 %structure_sums.4 = (f32[704,128]{1,0:T(8,128)S(1)}, f32[240,128]{1,0:T(8,128)S(1)}) custom-call(f32[8,2304]{1,0:T(8,128)S(1)} %get-tuple-element.20.refs_0_, f32[8,512]{1,0:T(8,128)S(1)} %get-tuple-element.19.refs_1_.data_ref), custom_call_target="tpu_custom_call" | custom-call | flops 1258291200 | bytes 1048576 | tf_op jit(solution)/shard_map/structure_sums/pallas_call | solution.py:539
  6.9 0.1 collective-permute-done.refs_3_
  7.0 3.2 %collective-permute-start.1 = (f32[8,1024]{1,0:T(8,128)S(1)}, f32[8,1024]{1,0:T(8,128)S(1)}, u32[]{:S(2)}, u32[]{:S(2)}) collective-permute-start(f32[8,1024]{1,0:T(8,128)S(1)} %pad_maximum_fusion.1), channel_id=1, source_target_pairs={{0,2},{1,3},{2,0},{3,1},{4,6},{5,7},{6,4},{7,5},{8,10},{9,11},{10,... | collective-permute-start | bytes 98312 | tf_op jit(solution)/shard_map/exchange_row/ppermute | solution.py:518
  10.2 0.0 collective-permute-done.2.refs_2_
  10.2 1.5 %structure_sums.5 = (f32[704,128]{1,0:T(8,128)S(1)}, f32[240,128]{1,0:T(8,128)S(1)}) custom-call(f32[704,128]{1,0:T(8,128)S(1)} %get-tuple-element.24.refs_0_, f32[240,128]{1,0:T(8,128)S(1)} %get-tuple-element.25.refs_1_, f32[8,2304]{1,0:T(8,128)S(1)} %collective-permute-done.2.refs_2_, f32[8,512]{1,0:T(8,128)S(1)} %collective-permute-done.refs_3_), custom_call_target="tpu_custom_call" | custom-call | flops 1258291200 | bytes 1048576 | tf_op jit(solution)/shard_map/structure_sums/pallas_call | solution.py:539
  11.7 0.3 %collective-permute-done.1.refs_2_ = f32[8,1024]{1,0:T(8,128)S(1)} collective-permute-done((f32[8,1024]{1,0:T(8,128)S(1)}, f32[8,1024]{1,0:T(8,128)S(1)}, u32[]{:S(2)}, u32[]{:S(2)}) %collective-permute-start.1) | collective-permute-done | bytes 32800 | tf_op jit(solution)/shard_map/exchange_row/ppermute | solution.py:518
  12.1 1.9 %collective-permute-start.3 = (f32[8,2048]{1,0:T(8,128)S(1)}, f32[8,2048]{1,0:T(8,128)S(1)}, u32[]{:S(2)}, u32[]{:S(2)}) collective-permute-start(f32[8,2048]{1,0:T(8,128)S(1)} %pad_maximum_fusion), channel_id=1, source_target_pairs={{0,1},{1,0},{2,3},{3,2},{4,5},{5,4},{6,7},{7,6},{8,9},{9,8},{10,11... | collective-permute-start | bytes 196616 | tf_op jit(solution)/shard_map/exchange_row/ppermute | solution.py:518
  14.0 1.5 %structure_sums.6.refs_0_ = f32[704,128]{1,0:T(8,128)S(1)} custom-call(f32[704,128]{1,0:T(8,128)S(1)} %get-tuple-element.29.refs_0_, f32[240,128]{1,0:T(8,128)S(1)} %get-tuple-element.30.refs_1_, f32[8,1024]{1,0:T(8,128)S(1)} %collective-permute-done.1.refs_2_), custom_call_target="tpu_custom_call" | custom-call | flops 1006632960 | bytes 1048576 | tf_op jit(solution)/shard_map/structure_sums/pallas_call | solution.py:539
  15.5 0.0 copy-start
  15.5 0.9 %collective-permute-done.3.refs_1_ = f32[8,2048]{1,0:T(8,128)S(1)} collective-permute-done((f32[8,2048]{1,0:T(8,128)S(1)}, f32[8,2048]{1,0:T(8,128)S(1)}, u32[]{:S(2)}, u32[]{:S(2)}) %collective-permute-start.3) | collective-permute-done | bytes 65568 | tf_op jit(solution)/shard_map/exchange_row/ppermute | solution.py:518
  16.3 2.6 %structure_sums.7.mine_ref = f32[704,128]{1,0:T(8,128)S(1)} custom-call(f32[704,128]{1,0:T(8,128)S(1)} %structure_sums.6.refs_0_, f32[8,2048]{1,0:T(8,128)S(1)} %collective-permute-done.3.refs_1_), custom_call_target="tpu_custom_call" | custom-call | flops 2013265920 | bytes 1048576 | tf_op jit(solution)/shard_map/structure_sums/pallas_call | solution.py:539
  18.9 0.1 collective-permute-start.4
  19.0 0.0 copy-done
  19.0 0.4 %own_ions.1 = (f32[96,768]{1,0:T(8,128)S(1)}, bf16[256,1536]{1,0:T(8,128)(2,1)S(1)}, bf16[1024,512]{1,0:T(8,128)(2,1)S(1)}) custom-call(f32[8,512]{1,0:T(8,128)S(1)} %get-tuple-element.19.refs_1_.data_ref, s32[512]{0:T(512)S(1)} %copy-done), custom_call_target="tpu_custom_call" | custom-call | flops 1073741824 | bytes 1048576 | tf_op jit(solution)/shard_map/own_ions/pallas_call | solution.py:561
  19.4 1.2 %collective-permute-done.4.other_ref = f32[704,128]{1,0:T(8,128)S(1)} collective-permute-done((f32[704,128]{1,0:T(8,128)S(1)}, f32[704,128]{1,0:T(8,128)S(1)}, u32[]{:S(2)}, u32[]{:S(2)}) %collective-permute-start.4) | collective-permute-done | bytes 360480 | tf_op jit(solution)/shard_map/exchange_core/ppermute | solution.py:518
  20.7 2.2 %forces.1 = (f32[3,768]{1,0:T(4,128)}, f32[3,512]{1,0:T(4,128)}) custom-call(f32[704,128]{1,0:T(8,128)S(1)} %structure_sums.7.mine_ref, f32[704,128]{1,0:T(8,128)S(1)} %collective-permute-done.4.other_ref, f32[8,512]{1,0:T(8,128)S(1)} %get-tuple-element.19.refs_1_.data_ref, f32[96,768]{1,0:T(8,128)S(1)} %get-tuple-element.33.basis_ref, ...), custom_call_target="tpu_custom_call" | custom-call | tf_op jit(solution)/shard_map/forces/pallas_call | solution.py:598
  (2 shorter events, 0.0 us)
Async XLA Ops:
  2.3 4.8 %collective-permute-start = (f32[8,512]{1,0:T(8,128)S(1)}, f32[8,512]{1,0:T(8,128)S(1)}, u32[]{:S(2)}, u32[]{:S(2)}) collective-permute-start(f32[8,512]{1,0:T(8,128)S(1)} %get-tuple-element.19.refs_1_.data_ref), channel_id=1, source_target_pairs={{0,8},{4,12},{8,0},{12,4},{1,9},{5,13},{9,1},{13,5},{2,10},{6,14},... | collective-permute-start | bytes 49160 | tf_op jit(solution)/shard_map/exchange_blk/ppermute | solution.py:518
  5.3 4.9 %collective-permute-start.2 = (f32[8,2304]{1,0:T(8,128)S(1)}, f32[8,2304]{1,0:T(8,128)S(1)}, u32[]{:S(2)}, u32[]{:S(2)}) collective-permute-start(f32[8,2304]{1,0:T(8,128)S(1)} %get-tuple-element.20.refs_0_), channel_id=1, source_target_pairs={{0,8},{4,12},{8,0},{12,4},{1,9},{5,13},{9,1},{13,5},{2,10},{6,14},... | collective-permute-start | bytes 221192 | tf_op jit(solution)/shard_map/exchange_blk/ppermute | solution.py:518
  7.0 5.0 %collective-permute-start.1 = (f32[8,1024]{1,0:T(8,128)S(1)}, f32[8,1024]{1,0:T(8,128)S(1)}, u32[]{:S(2)}, u32[]{:S(2)}) collective-permute-start(f32[8,1024]{1,0:T(8,128)S(1)} %pad_maximum_fusion.1), channel_id=1, source_target_pairs={{0,2},{1,3},{2,0},{3,1},{4,6},{5,7},{6,4},{7,5},{8,10},{9,11},{10,... | collective-permute-start | bytes 98312 | tf_op jit(solution)/shard_map/exchange_row/ppermute | solution.py:518
  12.1 4.3 %collective-permute-start.3 = (f32[8,2048]{1,0:T(8,128)S(1)}, f32[8,2048]{1,0:T(8,128)S(1)}, u32[]{:S(2)}, u32[]{:S(2)}) collective-permute-start(f32[8,2048]{1,0:T(8,128)S(1)} %pad_maximum_fusion), channel_id=1, source_target_pairs={{0,1},{1,0},{2,3},{3,2},{4,5},{5,4},{6,7},{7,6},{8,9},{9,8},{10,11... | collective-permute-start | bytes 196616 | tf_op jit(solution)/shard_map/exchange_row/ppermute | solution.py:518
  15.5 3.6 %copy-start = (s32[512]{0:T(512)S(1)}, s32[512]{0:T(512)}, u32[]{:S(2)}) copy-start(s32[512]{0:T(512)} %recv_ref.1) | copy-start | bytes 6148
  18.9 1.7 %collective-permute-start.4 = (f32[704,128]{1,0:T(8,128)S(1)}, f32[704,128]{1,0:T(8,128)S(1)}, u32[]{:S(2)}, u32[]{:S(2)}) collective-permute-start(f32[704,128]{1,0:T(8,128)S(1)} %structure_sums.7.mine_ref), channel_id=1, source_target_pairs={{0,4},{4,0},{8,12},{12,8},{1,5},{5,1},{9,13},{13,9},{2,6},{6,2},{1... | collective-permute-start | bytes 1081352 | tf_op jit(solution)/shard_map/exchange_core/ppermute | solution.py:518

commit v3 on v2

v3 whole, which is shorter than its diff:
```python
import functools
import math

import jax
import jax.numpy as jnp
from jax import lax
from jax.experimental import pallas as pl
from jax.experimental.pallas import tpu as pltpu
from jax.sharding import PartitionSpec as P

DOUBLE_PI = 2.0 * math.pi
EWALD_BETA = 30.0
BOX_Z = 3.0
FORCE_GAIN = 400.0
SIN_POLY = (6.283185, -41.34159, 81.599945, -76.61447, 41.342884, -12.471244)
COS_POLY = (1.0, -19.739204, 64.93912, -85.45014, 60.16763, -25.9676, 6.5286584)

BASIS = 24
HARM = 40
STEMS = (((0, 0), (3, 0), (3, 1), (6, 0), (6, 1)), ((9, 0), (9, 1), (12, 0), (12, 1)))
SUM_ROWS = (144, 112)
ORDERS = (
    tuple((k, 0) for k in range(8)) + tuple((k, 1) for k in range(1, 8)),
    tuple((k, 0) for k in range(8, 13)) + tuple((k, 1) for k in range(8, 13)),
)
COUNT_ROWS = 240
COUNT_AT = (0, 136)
COUNT_LEN = (136, 96)
FORCE_ROWS = (384, 256)
FORCE_AT = (0, 384)
PART_AT = (0, 2 * SUM_ROWS[0])
ARRIVE_AT = PART_AT[1] + 2 * SUM_ROWS[1]
F32 = jnp.float32
BF16 = jnp.bfloat16
NT = (((1,), (1,)), ((), ()))
VMEM_BYTES = 40 * 1024 * 1024


def horner(coefs, v):
    total = jnp.full_like(v, coefs[-1])
    for coef in coefs[-2::-1]:
        total = total * v + coef
    return total


def harmonics(pos, first):
    harm = lax.broadcasted_iota(jnp.int32, (8, pos.shape[1]), 0).astype(F32) + float(first)
    turns = harm * pos
    turns = turns - jnp.floor(turns + 0.5)
    square = turns * turns
    return horner(COS_POLY, square), turns * horner(SIN_POLY, square)


def advance(first, by):
    cos_a, sin_a = first
    cos_b, sin_b = by
    return cos_a * cos_b - sin_a * sin_b, sin_a * cos_b + cos_a * sin_b


def row_of(pair, row):
    return pair[0][row : row + 1], pair[1][row : row + 1]


def merge_last(cos_part, sin_part):
    low = lax.broadcasted_iota(jnp.int32, cos_part.shape, 0) < 4
    return jnp.where(low, cos_part, pltpu.roll(sin_part, 4, 0))


def first_basis(pos):
    first = harmonics(pos, 1)
    second = advance(first, row_of(first, 7))
    return [first[0], first[1], merge_last(*second)]


def first_slopes(basis):
    row = lax.broadcasted_iota(jnp.int32, basis[0].shape, 0)
    harm = row.astype(F32) + 1.0
    low = row < 4
    factor = jnp.where(low, -(harm + 8.0), harm + 4.0)
    return [-harm * basis[1], harm * basis[0], factor * pltpu.roll(basis[2], 4, 0)]


def second_basis(pos):
    first = harmonics(pos, 0)
    fourth = row_of(first, 4)
    second = advance(first, advance(fourth, fourth))
    return [first[0], first[1], second[0], second[1]]


def second_slopes(basis):
    harm = lax.broadcasted_iota(jnp.int32, basis[0].shape, 0).astype(F32)
    high = harm + 8.0
    return [-harm * basis[1], harm * basis[0], -high * basis[3], high * basis[2]]


def second_row(basis, harmonic, sine):
    return basis[2 * (harmonic // 8) + sine][harmonic % 8 : harmonic % 8 + 1]


def third_basis(pos):
    first = harmonics(pos, 1)
    second = advance(first, row_of(first, 7))
    third = advance(first, row_of(second, 7))
    fourth = advance(second, row_of(second, 7))
    fifth = advance(first, row_of(fourth, 7))
    parts = (first, second, third, fourth, fifth)
    return jnp.concatenate([p[0] for p in parts] + [p[1] for p in parts], axis=0)


def split_two(value):
    high = value.astype(BF16)
    return high, (value - high.astype(F32)).astype(BF16)


def key_of_rows(recv, device, cap, row_count, bits):
    per_pack = 64 // cap
    source = (recv // cap) ^ device
    order = jnp.zeros_like(source)
    for place, distance in enumerate(bits):
        order = order | jnp.where((source & distance) != 0, 1 << place, 0)
    far = jnp.where((source & row_count) != 0, 64, 0)
    return (order // per_pack) * 128 + far + (order % per_pack) * cap + recv % cap


def prep_kernel(
    coords_hbm, charges_hbm, counts_hbm, send_hbm, waves_hbm, out_ref, waves_out_ref,
    coords_ref, charges_ref, counts_ref, send_ref, waves_ref, sems,
):
    copies = [
        pltpu.make_async_copy(source, target, sems.at[i])
        for i, (source, target) in enumerate(
            (
                (waves_hbm, waves_ref),
                (counts_hbm, counts_ref),
                (send_hbm, send_ref),
                (charges_hbm, charges_ref),
                (coords_hbm, coords_ref),
            )
        )
    ]
    for copy in copies:
        copy.start()
    slots = charges_ref.shape[0]
    half = slots // 2
    out_ref[:, 0 : half + 128] = jnp.zeros((8, half + 128), F32)
    for copy in copies:
        copy.wait()
    live = lax.broadcasted_iota(jnp.int32, (1, slots), 1) < counts_ref[0]
    charge = jnp.where(live, charges_ref[...].reshape(1, slots), 0.0)
    send = jnp.where(live, send_ref[...].reshape(1, slots), -1).astype(F32)
    for part in range(2):
        lanes = slice(part * half, (part + 1) * half)
        out_ref[4 * part : 4 * part + 3, 0:half] = coords_ref[:, lanes]
        out_ref[4 * part + 3 : 4 * part + 4, 0:half] = charge[:, lanes]
    for piece in range(slots // 128):
        out_ref[piece : piece + 1, half : half + 128] = send[:, piece * 128 : (piece + 1) * 128]
    rows, width = wave_shape(waves_ref.shape[1])
    for row in range(rows):
        for comp in range(3):
            waves_out_ref[row : row + 1, comp * width : (comp + 1) * width] = waves_ref[
                comp : comp + 1, row * width : (row + 1) * width
            ].astype(F32)


def wave_shape(k_local):
    rows = 8
    while k_local % (rows * 128):
        rows //= 2
    return rows, k_local // rows


def basis_row(index):
    size = jnp.abs(index)
    sign = jnp.where(index < 0.0, 1.0, 0.0)
    row = jnp.where(size <= 8.0, size - 1.0 + 8.0 * sign, size + 7.0 + 4.0 * sign)
    return jnp.where(size == 0.0, float(BASIS), row)


def basis_size(row):
    low = jnp.where(row < 8, row, row - 8) + 1
    high = jnp.where(row < 20, row - 16, row - 20) + 9
    return jnp.where(row < 16, low, jnp.where(row < BASIS, high, 0))


def dense_weights():
    row = lax.broadcasted_iota(jnp.int32, (COUNT_ROWS, 128), 0)
    lane = lax.broadcasted_iota(jnp.int32, (COUNT_ROWS, 128), 1)
    early = row < COUNT_AT[1]
    own = jnp.where(early, row, row - COUNT_AT[1])
    paired = own < jnp.where(early, COUNT_LEN[0] - 16, COUNT_LEN[1] - 16)
    group = own // 8
    size_y = jnp.where(early, jnp.where(group < 8, group, group - 7), 8 + jnp.where(group < 5, group, group - 5))
    size_y = jnp.where(paired, size_y, jnp.where(early, own % 8, 8 + own % 8))
    part = jnp.where(lane < HARM, 0, jnp.where(lane < 2 * HARM, 1, 2))
    size_x = jnp.where(paired, basis_size(own % 8 + 8 * part), 0)
    phys_x = DOUBLE_PI * size_x.astype(F32)
    phys_y = DOUBLE_PI * size_y.astype(F32)
    phys_z = DOUBLE_PI * (lane - HARM * part + 1).astype(F32) / BOX_Z
    k_squared = phys_x * phys_x + phys_y * phys_y + phys_z * phys_z
    return jnp.exp(-k_squared / (4.0 * EWALD_BETA * EWALD_BETA)) / k_squared


def count_waves(waves, rows, width):
    wave_h = waves[0:rows, 0:width]
    wave_k = waves[0:rows, width : 2 * width]
    wave_l = waves[0:rows, 2 * width : 3 * width]
    flip = jnp.where(wave_l < 0.0, -1.0, 1.0)
    row_x = basis_row(wave_h * flip)
    wave_k = wave_k * flip
    size_y = jnp.abs(wave_k)
    sine = jnp.where(wave_k < 0.0, 1.0, 0.0)
    const = row_x == float(BASIS)
    part = jnp.where(row_x >= 16.0, 2.0, jnp.where(row_x >= 8.0, 1.0, 0.0))
    part = jnp.where(const, 0.0, part)
    late = size_y >= 8.0
    group = jnp.where(late, size_y - 8.0 + 5.0 * sine, size_y + 7.0 * sine)
    paired_id = 8.0 * group + (row_x - 8.0 * part) + jnp.where(late, float(COUNT_AT[1]), 0.0)
    tail = jnp.where(late, size_y - 8.0 + float(COUNT_AT[1] + COUNT_LEN[1] - 16), size_y + float(COUNT_LEN[0] - 16))
    row_id = jnp.where(const, tail + 8.0 * sine, paired_id)
    lane_id = wave_l * flip + (HARM * part - 1.0)
    step = lax.broadcasted_iota(jnp.int32, (16, width), 0).astype(F32)
    steps = [(step + 16.0 * i).astype(BF16) for i in range(COUNT_ROWS // 16)]
    one = jnp.ones((16, width), BF16)
    none = jnp.zeros((16, width), BF16)
    total = None
    for piece in range(rows):
        rows_at = jnp.broadcast_to(row_id[piece : piece + 1], (16, width)).astype(BF16)
        lanes_at = jnp.broadcast_to(lane_id[piece : piece + 1], (16, width)).astype(BF16)
        row_hot = jnp.concatenate([jnp.where(rows_at == at, one, none) for at in steps], axis=0)
        lane_hot = jnp.concatenate([jnp.where(lanes_at == at, one, none) for at in steps[:8]], axis=0)
        found = lax.dot_general(row_hot, lane_hot, NT, preferred_element_type=F32)
        total = found if total is None else total + found
    return total


def owner_rows(block_rows, half):
    return [
        jnp.concatenate([block_rows[i : i + 1, 0:half], block_rows[i + 4 : i + 5, 0:half]], axis=1) for i in range(4)
    ]


def owner_tables(rows):
    pos_x, pos_y, pos_z, charge = rows
    basis_x = jnp.concatenate([charge * part for part in first_basis(pos_x)], axis=0)
    basis_y = second_basis(pos_y)
    third = third_basis(pos_z)
    lanes = jnp.concatenate([third, third * basis_y[0][1:2], third * basis_y[1][1:2]], axis=0)
    high, low = split_two(lanes)
    gap = jnp.zeros((256 - 6 * HARM, third.shape[1]), BF16)
    high = jnp.concatenate([high, gap], axis=0)
    low = jnp.concatenate([low, gap], axis=0)
    return basis_x, basis_y, high, low


def stem_rows(part, basis_y):
    return [second_row(basis_y, harmonic, sine) for harmonic, sine in STEMS[part]]


def add_sums(basis_x, basis_y, charge, high, low, table_ref, v_ref):
    slots = charge.shape[1]
    all_rows = sum(SUM_ROWS)
    at = 0
    for part in range(2):
        stems = stem_rows(part, basis_y)
        rows = [stem * basis_x for stem in stems] + [charge * rows for rows in basis_y[2 * part : 2 * part + 2]]
        fill = SUM_ROWS[part] - BASIS * len(stems) - 16
        if fill:
            rows.append(jnp.zeros((fill, slots), F32))
        rows = jnp.concatenate(rows, axis=0)
        for begin in range(0, SUM_ROWS[part], 16):
            v_high, v_low = split_two(rows[begin : begin + 16])
            v_ref[at : at + 16] = v_high
            v_ref[all_rows + at : all_rows + at + 16] = v_low
            at += 16
    both = lax.dot_general(v_ref[...], high, NT, preferred_element_type=F32)
    rest = lax.dot_general(v_ref[0:all_rows], low, NT, preferred_element_type=F32)
    total = (both[:all_rows] + both[all_rows:]) + rest
    at = 0
    for part in range(2):
        count, begin = SUM_ROWS[part], PART_AT[part]
        table_ref[begin : begin + count] += total[at : at + count, :128]
        table_ref[begin + count : begin + 2 * count] += total[at : at + count, 128:]
        at += count


def add_arrivals(block_rows, rows, half, cap, place, pack, targets, table_ref):
    block = half + 128
    slots = 2 * half
    send = jnp.concatenate([block_rows[p : p + 1, half:block] for p in range(slots // 128)], axis=1)
    step = lax.broadcasted_iota(jnp.int32, (16, slots), 0).astype(F32)
    one, none = jnp.ones((16, slots), BF16), jnp.zeros((16, slots), BF16)
    hots = []
    for target in targets:
        rank = send - (target * cap).astype(F32)
        valid = jnp.logical_and(rank >= 0.0, rank < float(cap))
        key = jnp.broadcast_to(jnp.where(valid, rank + place, -1.0), (16, slots)).astype(BF16)
        hots += [jnp.where(key == (step + 16.0 * i).astype(BF16), one, none) for i in range(4)]
    values = jnp.concatenate(rows + [jnp.zeros((4, slots), F32)], axis=0)
    found = lax.dot_general(split_three(values), jnp.concatenate(hots, axis=0), NT, preferred_element_type=F32)
    row = ARRIVE_AT + 8 * pack
    if not isinstance(row, int):
        row = pl.multiple_of(row, 8)
    table_ref[pl.ds(row, 8)] += (found[0:8] + found[8:16]) + found[16:24]


def split_three(value):
    high = value.astype(BF16).astype(F32)
    rest = value - high
    mid = rest.astype(BF16).astype(F32)
    return jnp.concatenate([high, mid, rest - mid], axis=0).astype(BF16)


def count_kernel(rows, width, waves_ref, out_ref):
    counts = count_waves(waves_ref, rows, width)
    for row in range(0, COUNT_ROWS, 8):
        out_ref[:, 16 * row : 16 * row + 128] = counts[row : row + 8]


def sums_kernel(plan, *refs):
    refs = list(refs)
    base_ref = refs.pop(0) if plan["has_base"] else None
    ion_refs = [refs.pop(0) for _ in plan["chunks"]]
    table_ref = refs.pop(0)
    v_ref = refs.pop(0)
    half, cap, row_count = plan["half"], plan["cap"], plan["row_count"]
    block = half + 128
    per_pack = 64 // cap
    device = lax.axis_index("blk") * row_count + lax.axis_index("row")
    targets = (device, device ^ row_count)
    table_ref[...] = jnp.zeros_like(table_ref) if base_ref is None else base_ref[...]

    def add(block_rows, place, pack, v_ref):
        ions = owner_rows(block_rows, half)
        basis_x, basis_y, high, low = owner_tables(ions)
        add_sums(basis_x, basis_y, ions[3], high, low, table_ref, v_ref)
        add_arrivals(block_rows, ions, half, cap, place, pack, targets, table_ref)

    turn = 0
    for ions_ref, (owners, first_owner) in zip(ion_refs, plan["chunks"]):
        if owners <= 4 and per_pack == 1:
            for owner in range(owners):
                ions = ions_ref[:, owner * block : (owner + 1) * block]
                add(ions, 0.0, first_owner + owner, v_ref.at[turn % 2])
                turn += 1
        else:

            def step(owner, carry, ions_ref=ions_ref, first_owner=first_owner):
                begin = pl.multiple_of(owner * block, 128)
                index = first_owner + owner
                place = (lax.rem(index, per_pack) * cap).astype(F32)
                add(ions_ref[:, pl.ds(begin, block)], place, index // per_pack, v_ref.at[0])
                return carry

            lax.fori_loop(0, owners, step, 0)


SLOPE_X, BASIS_Y, SLOPE_Y, BASIS_ROWS = 24, 48, 80, 112


def store_bases(ions, basis_ref, z_ref):
    count = ions.shape[1]
    basis_x = first_basis(ions[0:1])
    basis_y = second_basis(ions[1:2])
    parts = basis_x + first_slopes(basis_x) + basis_y + second_slopes(basis_y)
    for i, part in enumerate(parts):
        basis_ref[8 * i : 8 * i + 8] = part
    plain = third_basis(ions[2:3])
    harm = lax.broadcasted_iota(jnp.int32, (HARM, count), 0).astype(F32) + 1.0
    slope = jnp.concatenate([-harm * plain[HARM:], harm * plain[:HARM]], axis=0)
    for i, table in enumerate((plain, slope)):
        high, low = split_two(table)
        z_ref[:, i * count : (i + 1) * count] = jnp.concatenate(
            [high, low, high, jnp.zeros((256 - 6 * HARM, count), BF16)], axis=0
        )


def own_kernel(half, cap, row_count, bits, data_ref, recv_ref, basis_ref, z_ref, hot_ref, gain_ref):
    store_bases(jnp.concatenate([data_ref[0:4, 0:half], data_ref[4:8, 0:half]], axis=1), basis_ref, z_ref)
    atoms_dev = recv_ref.shape[0]
    device = lax.axis_index("blk") * row_count + lax.axis_index("row")
    key = key_of_rows(recv_ref[...].reshape(1, atoms_dev), device, cap, row_count, bits)
    spot = lax.broadcasted_iota(jnp.int32, hot_ref.shape, 0)
    hot_ref[...] = jnp.where(spot == key, 1.0, 0.0).astype(BF16)
    gain_ref[...] = dense_weights()


def swap(parts):
    return [parts[1], parts[0], pltpu.roll(parts[2], 4, 0)]


def combine(own, other):
    gain, sums, turned = own
    gain_s, sums_s, turned_s = swap(gain), swap(sums), swap(turned)
    both = [a + b for a, b in zip(gain, gain_s)]
    odd = [a - b for a, b in zip(gain, gain_s)]
    if other is None:
        return [both[i] * sums[i] - odd[i] * turned_s[i] for i in range(3)]
    gain_o, sums_o, turned_o = other
    gain_os, sums_os = swap(gain_o), swap(sums_o)
    both_o = [a + b for a, b in zip(gain_o, gain_os)]
    odd_o = [a - b for a, b in zip(gain_o, gain_os)]
    return [
        (both[i] + both_o[i]) * sums[i]
        - (odd[i] + odd_o[i]) * turned_s[i]
        - (both[i] - both_o[i]) * turned_o[i]
        - (odd[i] - odd_o[i]) * sums_os[i]
        for i in range(3)
    ]


def weighted_sums(part, mine_ref, other_ref, count_refs, gain_ref, w_ref):
    lane = lax.broadcasted_iota(jnp.int32, (8, 128), 1)
    is_cos = lane < HARM
    is_wave = lane < 2 * HARM
    count = SUM_ROWS[part]

    def both(row):
        row = PART_AT[part] + row
        return mine_ref[row : row + 8] + other_ref[row : row + 8]

    def blocks(row):
        near, far = both(row), both(count + row)
        middle = jnp.where(lane < 48, pltpu.roll(near, 48, 1), pltpu.roll(far, 48, 1))
        return [jnp.where(is_wave, value, 0.0) for value in (near, middle, pltpu.roll(far, 96, 1))]

    def turn(sums):
        return jnp.where(is_cos, pltpu.roll(sums, 88, 1), -pltpu.roll(sums, HARM, 1))

    def harmonics_of(stem):
        found = {}
        for harmonic, _ in STEMS[part]:
            if harmonic == 0:
                plain, cos_1, sin_1 = stem[(0, 0)]
                found.update({(0, 0): plain, (1, 0): cos_1, (1, 1): sin_1})
                continue
            cos, sin = stem[(harmonic, 0)], stem[(harmonic, 1)]
            found[(harmonic, 0)], found[(harmonic, 1)] = cos[0], sin[0]
            found[(harmonic - 1, 0)] = cos[1] + sin[2]
            found[(harmonic - 1, 1)] = sin[1] - cos[2]
            found[(harmonic + 1, 0)] = cos[1] - sin[2]
            found[(harmonic + 1, 1)] = sin[1] + cos[2]
        return found

    def gains(row):
        at = COUNT_AT[part] + row
        lanes = slice(16 * at, 16 * at + 128)
        tile = (count_refs[0][:, lanes] + count_refs[1][:, lanes]) * gain_ref[at : at + 8]
        back, far = pltpu.roll(tile, 88, 1), pltpu.roll(tile, 48, 1)
        pairs = ((tile, pltpu.roll(tile, HARM, 1)), (back, tile), (far, back))
        return [jnp.where(is_cos, a, jnp.where(is_wave, b, 0.0)) for a, b in pairs]

    def store(row, value):
        high, low = split_two(value)
        high = high.astype(F32)
        low = low.astype(F32)
        turned = pltpu.roll(high, 2 * HARM, 1)
        row = FORCE_AT[part] + row
        w_ref[row : row + 8, 0:128] = jnp.where(is_wave, high, turned)
        w_ref[row : row + 8, 128:256] = jnp.where(lane < 32, turned, pltpu.roll(low, 32, 1))

    by_block = [
        harmonics_of({stem: blocks(BASIS * i + 8 * x) for i, stem in enumerate(STEMS[part])}) for x in range(3)
    ]
    order = ORDERS[part]
    groups = {}
    for i, name in enumerate(order):
        sums = [by_block[x][name] for x in range(3)]
        groups[name] = (gains(8 * i), sums, [turn(value) for value in sums])
    for i, (harmonic, sine) in enumerate(order):
        other = None if harmonic == 0 else groups[(harmonic, 1 - sine)]
        for x, value in enumerate(combine(groups[(harmonic, sine)], other)):
            store(BASIS * i + 8 * x, value)
    tails = [blocks(BASIS * len(STEMS[part]) + 8 * sine) for sine in range(2)]
    found = harmonics_of({(h, sine): [b[h % 8 : h % 8 + 1] for b in tails[sine]] for h, sine in STEMS[part]})
    index = lax.broadcasted_iota(jnp.int32, (8, 128), 0)
    kinds = []
    for sine in range(2):
        rows = jnp.zeros((8, 128), F32)
        for harmonic, kind in order:
            if kind == sine:
                rows = jnp.where(index == harmonic % 8, found[(harmonic, kind)], rows)
        at = COUNT_LEN[part] - 16 + 8 * sine
        kinds.append((gains(at)[0], rows, turn(rows)))
    at = BASIS * len(order)
    for sine in range(2):
        (gain, sums, _), (gain_o, _, turned_o) = kinds[sine], kinds[1 - sine]
        store(at + 8 * sine, (gain + gain_o) * sums - (gain - gain_o) * turned_o)
    if at + 16 < FORCE_ROWS[part]:
        fill = FORCE_ROWS[part] - at - 16
        w_ref[FORCE_AT[part] + at + 16 : FORCE_AT[part] + FORCE_ROWS[part]] = jnp.zeros((fill, 256), F32)


def pull(weights, basis_ref, z_ref, count, begin, tile):
    lanes = slice(begin, begin + tile)
    plain = jnp.dot(weights, z_ref[:, begin : begin + tile], preferred_element_type=F32)
    sloped = jnp.dot(weights, z_ref[:, count + begin : count + begin + tile], preferred_element_type=F32)
    zero = jnp.zeros((8, tile), F32)
    even, slope, third = [zero] * 3, [zero] * 3, [zero] * 3
    sum_y = sum_z = zero
    for part in range(2):
        for place, (harmonic, sine) in enumerate(ORDERS[part]):
            at = 16 * (harmonic // 8) + 8 * sine + harmonic % 8
            basis = basis_ref[BASIS_Y + at : BASIS_Y + at + 1, lanes]
            basis_slope = basis_ref[SLOPE_Y + at : SLOPE_Y + at + 1, lanes]
            for i in range(3):
                row = FORCE_AT[part] + BASIS * place + 8 * i
                plain_rows, sloped_rows = plain[row : row + 8], sloped[row : row + 8]
                if harmonic == 0:
                    even[i] = even[i] + plain_rows
                    third[i] = third[i] + sloped_rows
                else:
                    even[i] = even[i] + basis * plain_rows
                    slope[i] = slope[i] + basis_slope * plain_rows
                    third[i] = third[i] + basis * sloped_rows
        for sine in range(2):
            row = FORCE_AT[part] + BASIS * len(ORDERS[part]) + 8 * sine
            at = 16 * part + 8 * sine
            sum_y = sum_y + basis_ref[SLOPE_Y + at : SLOPE_Y + at + 8, lanes] * plain[row : row + 8]
            sum_z = sum_z + basis_ref[BASIS_Y + at : BASIS_Y + at + 8, lanes] * sloped[row : row + 8]
    sum_x = zero
    for i in range(3):
        rows_x = basis_ref[8 * i : 8 * i + 8, lanes]
        sum_x = sum_x + basis_ref[SLOPE_X + 8 * i : SLOPE_X + 8 * i + 8, lanes] * even[i]
        sum_y = sum_y + rows_x * slope[i]
        sum_z = sum_z + rows_x * third[i]
    return [jnp.sum(value, axis=0, keepdims=True) for value in (sum_x, sum_y, sum_z)]


TILE = 256


def force_kernel(
    force_scale, half, mine_ref, other_ref, count_ref, other_count_ref, data_ref, basis_ref, z_ref, hot_ref, gain_ref,
    slot_ref, atom_ref, w_ref, atom_basis_ref, atom_z_ref,
):
    packs = hot_ref.shape[0] // 128
    lane = lax.broadcasted_iota(jnp.int32, (8, 128), 1)
    starts = [ARRIVE_AT + 8 * p for p in range(packs)]
    pool = jnp.concatenate([jnp.where(lane < 64, mine_ref[r : r + 8], other_ref[r : r + 8]) for r in starts], axis=1)
    found = jnp.dot(split_three(pool), hot_ref[...], preferred_element_type=F32)
    routed = ((found[0:8] + found[8:16]) + found[16:24])[0:4]
    for part in range(2):
        weighted_sums(part, mine_ref, other_ref, (count_ref, other_count_ref), gain_ref, w_ref)
    weights = w_ref[...].astype(BF16)
    store_bases(routed, atom_basis_ref, atom_z_ref)
    charge = jnp.concatenate([data_ref[3:4, 0:half], data_ref[7:8, 0:half]], axis=1)
    jobs = ((basis_ref, z_ref, charge, slot_ref), (atom_basis_ref, atom_z_ref, routed[3:4], atom_ref))
    for rows_ref, table_ref, charges, out_ref in jobs:
        count = out_ref.shape[1]
        for begin in range(0, count, TILE):
            lanes = slice(begin, begin + TILE)
            gain = (-DOUBLE_PI * force_scale) * charges[:, lanes]
            gains = (gain, gain, gain / BOX_Z)
            found = pull(weights, rows_ref, table_ref, count, begin, TILE)
            out_ref[:, lanes] = jnp.concatenate([gains[i] * found[i] for i in range(3)], axis=0)


def params():
    return pltpu.CompilerParams(vmem_limit_bytes=VMEM_BYTES)


def stay(value):
    return pltpu.with_memory_space_constraint(value, pltpu.HBM)


def whole(count):
    return [pl.BlockSpec(memory_space=pltpu.VMEM)] * count


def body(coords, charges, counts, send_slot, recv_index, wave_ints):
    slots = charges.shape[0]
    half = slots // 2
    block = half + 128
    atoms_dev = recv_index.shape[0]
    devices = lax.axis_size(("blk", "row"))
    blk_count = lax.axis_size("blk")
    row_count = lax.axis_size("row")
    k_local = wave_ints.shape[1]
    cap = 2 * atoms_dev // devices
    packs = max(1, devices // 2 * cap // 64)
    wave_rows, wave_width = wave_shape(k_local)
    force_scale = FORCE_GAIN / math.sqrt(float(atoms_dev * devices * blk_count * k_local))
    table_shape = jax.ShapeDtypeStruct((ARRIVE_AT + 8 * packs, 128), F32)
    count_shape = jax.ShapeDtypeStruct((8, 16 * COUNT_ROWS), F32)

    with jax.named_scope("payload"):
        own_ions, own_waves = pl.pallas_call(
            prep_kernel,
            out_shape=(
                jax.ShapeDtypeStruct((8, block), F32),
                jax.ShapeDtypeStruct((wave_rows, 3 * wave_width), F32),
            ),
            in_specs=[pl.BlockSpec(memory_space=pltpu.HBM)] * 5,
            out_specs=tuple(whole(2)),
            scratch_shapes=[
                pltpu.VMEM(coords.shape, F32),
                pltpu.VMEM(charges.shape, F32),
                pltpu.SMEM(counts.shape, jnp.int32),
                pltpu.VMEM(send_slot.shape, jnp.int32),
                pltpu.VMEM(wave_ints.shape, jnp.int32),
                pltpu.SemaphoreType.DMA((5,)),
            ],
            compiler_params=params(),
        )(stay(coords), stay(charges), counts, stay(send_slot), stay(wave_ints))

    def flip(value, blk_bit, row_bit):
        if not row_bit:
            return lax.ppermute(value, "blk", [(i, i ^ blk_bit) for i in range(blk_count)])
        if not blk_bit:
            return lax.ppermute(value, "row", [(i, i ^ row_bit) for i in range(row_count)])
        distance = row_count * blk_bit + row_bit
        return lax.ppermute(value, ("blk", "row"), [(i, i ^ distance) for i in range(devices)])

    def joined(values):
        return values[0] if len(values) == 1 else jnp.concatenate(values, axis=1)

    def accumulate(table, chunks):
        plan = {
            "has_base": table is not None,
            "chunks": [chunk[1:] for chunk in chunks],
            "half": half,
            "cap": cap,
            "row_count": row_count,
        }
        args = [table] * plan["has_base"] + [chunk[0] for chunk in chunks]
        flops = 2 * sum(chunk[1] for chunk in chunks) * slots * 256 * 720
        with jax.named_scope("structure_sums"):
            return pl.pallas_call(
                functools.partial(sums_kernel, plan),
                out_shape=table_shape,
                in_specs=whole(len(args)),
                out_specs=whole(1)[0],
                scratch_shapes=[pltpu.VMEM((2, 2 * sum(SUM_ROWS), slots), BF16)],
                compiler_params=params(),
                cost_estimate=pl.CostEstimate(flops=flops, bytes_accessed=1 << 20, transcendentals=0),
            )(*args)

    steps = []
    bit = row_count // 2
    while bit >= 2:
        steps.append((0, bit))
        bit //= 2
    bit = 4
    while bit < blk_count:
        steps.append((bit, 0))
        bit *= 2
    bits = [row_count * blk_bit + row_bit for blk_bit, row_bit in steps] + [2 * row_count, 1]
    table, counted = None, None
    ions, held, chunks = [own_ions], 1, [(own_ions, 1, 0)]
    for blk_bit, row_bit in steps:
        with jax.named_scope("exchange_ions"):
            got = flip(joined(ions), blk_bit, row_bit)
        if blk_bit:
            with jax.named_scope("exchange_counts"):
                counted = counted + flip(counted, blk_bit, 0)
        if counted is None:
            with jax.named_scope("counts"):
                counted = pl.pallas_call(
                    functools.partial(count_kernel, wave_rows, wave_width),
                    out_shape=count_shape,
                    in_specs=whole(1),
                    out_specs=whole(1)[0],
                    compiler_params=params(),
                    cost_estimate=pl.CostEstimate(
                        flops=2 * k_local * COUNT_ROWS * 128, bytes_accessed=1 << 20, transcendentals=0
                    ),
                )(own_waves)
            got, counted = lax.optimization_barrier((got, counted))
        else:
            table, chunks = accumulate(table, chunks), []
            got, table = lax.optimization_barrier((got, table))
        chunks = chunks + [(got, held, held)]
        ions = ions + [got]
        held *= 2
    with jax.named_scope("exchange_ions"):
        sent = joined(ions)
        across = flip(jnp.concatenate([sent, counted], axis=1), 2, 0)
        along = flip(sent, 0, 1)
        corner = flip(sent, 2, 1)
    table = accumulate(table, chunks)
    table = accumulate(table, [(along, held, 2 * held)])
    table, across = lax.optimization_barrier((table, across))
    counted = counted + across[:, held * block :]
    with jax.named_scope("exchange_core"):
        other_counted = flip(counted, 1, 0)
    table = accumulate(table, [(across, held, held)])
    corner, table, counted = lax.optimization_barrier((corner, table, counted))
    table = accumulate(table, [(corner, held, 3 * held)])
    with jax.named_scope("exchange_core"):
        other = flip(table, 1, 0)
    own_ions, recv_index, table = lax.optimization_barrier((own_ions, recv_index, table))
    with jax.named_scope("own_ions"):
        basis, table_z, hot, gain = pl.pallas_call(
            functools.partial(own_kernel, half, cap, row_count, bits),
            out_shape=(
                jax.ShapeDtypeStruct((BASIS_ROWS, slots), F32),
                jax.ShapeDtypeStruct((256, 2 * slots), BF16),
                jax.ShapeDtypeStruct((128 * packs, atoms_dev), BF16),
                jax.ShapeDtypeStruct((COUNT_ROWS, 128), F32),
            ),
            in_specs=whole(2),
            out_specs=tuple(whole(4)),
            compiler_params=params(),
            cost_estimate=pl.CostEstimate(flops=1 << 30, bytes_accessed=1 << 20, transcendentals=0),
        )(own_ions, recv_index)
    with jax.named_scope("forces"):
        return pl.pallas_call(
            functools.partial(force_kernel, force_scale, half),
            out_shape=(
                jax.ShapeDtypeStruct((3, slots), F32),
                jax.ShapeDtypeStruct((3, atoms_dev), F32),
            ),
            in_specs=whole(9),
            out_specs=tuple(whole(2)),
            scratch_shapes=[
                pltpu.VMEM((sum(FORCE_ROWS), 256), F32),
                pltpu.VMEM((BASIS_ROWS, atoms_dev), F32),
                pltpu.VMEM((256, 2 * atoms_dev), BF16),
            ],
            compiler_params=params(),
        )(table, other, counted, other_counted, own_ions, basis, table_z, hot, gain)


def solution(mesh):
    placed = (
        P(None, ("groups", "blk", "row")),
        P(("groups", "blk", "row")),
        P(("groups", "blk", "row")),
        P(("groups", "blk", "row")),
        P(("groups", "blk", "row")),
        P(None, "blk"),
    )
    return jax.shard_map(
        body,
        mesh=mesh,
        in_specs=placed,
        out_specs=(P(None, ("groups", "blk", "row")), P(None, ("groups", "blk", "row"))),
        check_vma=False,
    )
```

time: 23.1 us -> 21.7 us (0.939)
  Pallas kernels: 10.7 us -> 8.92 us
  waiting for transfers between devices: 2.56 us -> 2.96 us
    pallas_call x4 -> x5, Pallas kernels: 7.15 us -> 5.23 us  [the longest x4 4.29 us: accumulate(): pl.pallas_call(functools.partial(sums_kernel, plan), out_shape=table_shap...]
    ppermute x5 -> x6, waiting for transfers between devices: 2.56 us -> 2.96 us  [the longest x2 2.02 us: flip(): lax.ppermute(value, 'row', [(i, i ^ row_bit) for i in range(row_count)])]
    ppermute x5 -> x6, starting transfers between devices: 8.25 us -> 8.22 us  [the longest x2 5.62 us: flip(): lax.ppermute(value, 'row', [(i, i ^ row_bit) for i in range(row_count)])]
  transfers between devices with their start and end apart: 5 -> 6, of which waited for: 4 -> 4; matrix products, arithmetic and copies ran while one was open for 0% -> 0% of each run, Pallas kernels for 22% -> 22%
where the time goes in v3:
time: 21.7 us; the launch traced here: 21.5 us
  Pallas kernels  8.92 us (41%)
  starting transfers between devices  8.22 us (38%)
  waiting for transfers between devices  2.96 us (14%)
  between operations  1.36 us (6%)
    ppermute x2, starting transfers between devices, flip(): lax.ppermute(value, 'row', [(i, i ^ row_bit) for i in range(row_count)])  5.62 us
    pallas_call x4, Pallas kernels, accumulate(): pl.pallas_call(functools.partial(sums_kernel, plan), out_shape=table_shap...  4.29 us
    ppermute x3, starting transfers between devices, flip(): lax.ppermute(value, 'blk', [(i, i ^ blk_bit) for i in range(blk_count)])  2.54 us
    pallas_call x1, Pallas kernels, body(): pl.pallas_call(functools.partial(force_kernel, force_scale, half), out_sh...  2.2 us
    ppermute x2, waiting for transfers between devices, flip(): lax.ppermute(value, 'row', [(i, i ^ row_bit) for i in range(row_count)])  2.02 us
    pallas_call x1, Pallas kernels, body(): pl.pallas_call(prep_kernel, out_shape=(jax.ShapeDtypeStruct((8, block), F...  0.98 us
    pallas_call x1, Pallas kernels, body(): pl.pallas_call(functools.partial(count_kernel, wave_rows, wave_width), ou...  0.94 us
    ppermute x3, waiting for transfers between devices, flip(): lax.ppermute(value, 'blk', [(i, i ^ blk_bit) for i in range(blk_count)])  0.73 us
  transfers between devices with their start and end apart: 6, of which 4 were waited for; matrix products, arithmetic and copies ran while one was open for 0% of the time, Pallas kernels for 22%

profile of v3, /device:TPU:0, one launch (start us, length us, event | category | flops | bytes accessed | tf_op | source)
XLA Modules:
  0.0 21.5 jit_solution(17095642084821120831)
XLA Ops:
  1.3 1.0 %payload.1 = (f32[8,512]{1,0:T(8,128)S(1)}, f32[8,2304]{1,0:T(8,128)S(1)}) custom-call(f32[3,768]{1,0:T(4,128)} %coords_hbm.1, f32[768]{0:T(1024)} %charges_hbm.1, s32[1]{0:T(128)S(6)} %copy.9.counts_hbm, s32[768]{0:T(1024)} %send_hbm.1, s32[3,6144]{1,0:T(4,128)} %waves_hbm.1), custom_call_target="tpu_custom_call" | custom-call | tf_op jit(solution)/shard_map/payload/pallas_call | solution.py:587
  2.3 4.1 %collective-permute-start = (f32[8,512]{1,0:T(8,128)S(1)}, f32[8,512]{1,0:T(8,128)S(1)}, u32[]{:S(2)}, u32[]{:S(2)}) collective-permute-start(f32[8,512]{1,0:T(8,128)S(1)} %get-tuple-element.28.refs_0_.data_ref), channel_id=1, source_target_pairs={{0,2},{1,3},{2,0},{3,1},{4,6},{5,7},{6,4},{7,5},{8,10},{9,11},{10,... | collective-permute-start | bytes 49160 | tf_op jit(solution)/shard_map/exchange_ions/ppermute | solution.py:610
  6.4 0.9 %counts.1 = f32[8,3840]{1,0:T(8,128)S(1)} custom-call(f32[8,2304]{1,0:T(8,128)S(1)} %get-tuple-element.19.waves_ref), custom_call_target="tpu_custom_call" | custom-call | flops 377487360 | bytes 1048576 | tf_op jit(solution)/shard_map/counts/pallas_call | solution.py:658
  7.3 0.8 %collective-permute-done.refs_1_ = f32[8,512]{1,0:T(8,128)S(1)} collective-permute-done((f32[8,512]{1,0:T(8,128)S(1)}, f32[8,512]{1,0:T(8,128)S(1)}, u32[]{:S(2)}, u32[]{:S(2)}) %collective-permute-start) | collective-permute-done | bytes 16416 | tf_op jit(solution)/shard_map/exchange_ions/ppermute | solution.py:610
  8.1 2.0 %collective-permute-start.3 = (f32[8,4864]{1,0:T(8,128)S(1)}, f32[8,4864]{1,0:T(8,128)S(1)}, u32[]{:S(2)}, u32[]{:S(2)}) collective-permute-start(f32[8,4864]{1,0:T(8,128)S(1)} %pad_maximum_fusion), channel_id=1, source_target_pairs={{0,8},{4,12},{8,0},{12,4},{1,9},{5,13},{9,1},{13,5},{2,10},{6,14},... | collective-permute-start | bytes 466952 | tf_op jit(solution)/shard_map/exchange_ions/ppermute | solution.py:608
  10.1 1.5 %collective-permute-start.2 = (f32[8,1024]{1,0:T(8,128)S(1)}, f32[8,1024]{1,0:T(8,128)S(1)}, u32[]{:S(2)}, u32[]{:S(2)}) collective-permute-start(f32[8,1024]{1,0:T(8,128)S(1)} %constant_dynamic-update-slice_fusion), channel_id=1, source_target_pairs={{0,1},{1,0},{2,3},{3,2},{4,5},{5,4},{6,7},{7,6},{8,9},{9,8},{10,11... | collective-permute-start | bytes 98312 | tf_op jit(solution)/shard_map/exchange_ions/ppermute | solution.py:610
  11.6 0.1 collective-permute-start.1
  11.7 1.1 %structure_sums.4.refs_0_ = f32[576,128]{1,0:T(8,128)S(1)} custom-call(f32[8,512]{1,0:T(8,128)S(1)} %get-tuple-element.28.refs_0_.data_ref, f32[8,512]{1,0:T(8,128)S(1)} %collective-permute-done.refs_1_), custom_call_target="tpu_custom_call" | custom-call | flops 566231040 | bytes 1048576 | tf_op jit(solution)/shard_map/structure_sums/pallas_call | solution.py:628
  12.7 1.2 %collective-permute-done.2.refs_1_ = f32[8,1024]{1,0:T(8,128)S(1)} collective-permute-done((f32[8,1024]{1,0:T(8,128)S(1)}, f32[8,1024]{1,0:T(8,128)S(1)}, u32[]{:S(2)}, u32[]{:S(2)}) %collective-permute-start.2) | collective-permute-done | bytes 32800 | tf_op jit(solution)/shard_map/exchange_ions/ppermute | solution.py:610
  14.0 1.1 %structure_sums.5.refs_0_ = f32[576,128]{1,0:T(8,128)S(1)} custom-call(f32[576,128]{1,0:T(8,128)S(1)} %structure_sums.4.refs_0_, f32[8,1024]{1,0:T(8,128)S(1)} %collective-permute-done.2.refs_1_), custom_call_target="tpu_custom_call" | custom-call | flops 566231040 | bytes 1048576 | tf_op jit(solution)/shard_map/structure_sums/pallas_call | solution.py:628
  15.1 0.0 collective-permute-done.3.refs_1_
  15.1 1.1 %structure_sums.6.refs_0_ = f32[576,128]{1,0:T(8,128)S(1)} custom-call(f32[576,128]{1,0:T(8,128)S(1)} %structure_sums.5.refs_0_, f32[8,4864]{1,0:T(8,128)S(1)} %collective-permute-done.3.refs_1_), custom_call_target="tpu_custom_call" | custom-call | flops 566231040 | bytes 1048576 | tf_op jit(solution)/shard_map/structure_sums/pallas_call | solution.py:628
  16.2 0.0 copy-start
  16.2 0.2 collective-permute-done.1.refs_1_
  16.4 1.1 %structure_sums.7.mine_ref = f32[576,128]{1,0:T(8,128)S(1)} custom-call(f32[576,128]{1,0:T(8,128)S(1)} %structure_sums.6.refs_0_, f32[8,1024]{1,0:T(8,128)S(1)} %collective-permute-done.1.refs_1_), custom_call_target="tpu_custom_call" | custom-call | flops 566231040 | bytes 1048576 | tf_op jit(solution)/shard_map/structure_sums/pallas_call | solution.py:628
  17.5 0.1 collective-permute-start.4
  17.6 0.5 %collective-permute-start.5 = (f32[8,3840]{1,0:T(8,128)S(1)}, f32[8,3840]{1,0:T(8,128)S(1)}, u32[]{:S(2)}, u32[]{:S(2)}) collective-permute-start(f32[8,3840]{1,0:T(8,128)S(1)} %slice_add_fusion.count_ref), channel_id=1, source_target_pairs={{0,4},{4,0},{8,12},{12,8},{1,5},{5,1},{9,13},{13,9},{2,6},{6,2},{1... | collective-permute-start | bytes 368648 | tf_op jit(solution)/shard_map/exchange_core/ppermute | solution.py:608
  18.1 0.0 copy-done
  18.1 0.5 %own_ions.1 = (f32[112,768]{1,0:T(8,128)S(1)}, bf16[256,1536]{1,0:T(8,128)(2,1)S(1)}, bf16[1024,512]{1,0:T(8,128)(2,1)S(1)}, f32[240,128]{1,0:T(8,128)S(1)}) custom-call(f32[8,512]{1,0:T(8,128)S(1)} %get-tuple-element.28.refs_0_.data_ref, s32[512]{0:T(512)S(1)} %copy-done), custom_call_target="tpu_custom_call" | custom-call | flops 1073741824 | bytes 1048576 | tf_op jit(solution)/shard_map/own_ions/pallas_call | solution.py:693
  18.6 0.7 %collective-permute-done.5.other_count_ref = f32[8,3840]{1,0:T(8,128)S(1)} collective-permute-done((f32[8,3840]{1,0:T(8,128)S(1)}, f32[8,3840]{1,0:T(8,128)S(1)}, u32[]{:S(2)}, u32[]{:S(2)}) %collective-permute-start.5) | collective-permute-done | bytes 122912 | tf_op jit(solution)/shard_map/exchange_core/ppermute | solution.py:608
  19.3 0.0 collective-permute-done.4.other_ref
  19.3 2.2 %forces.1 = (f32[3,768]{1,0:T(4,128)}, f32[3,512]{1,0:T(4,128)}) custom-call(f32[576,128]{1,0:T(8,128)S(1)} %structure_sums.7.mine_ref, f32[576,128]{1,0:T(8,128)S(1)} %collective-permute-done.4.other_ref, f32[8,3840]{1,0:T(8,128)S(1)} %slice_add_fusion.count_ref, f32[8,3840]{1,0:T(8,128)S(1)} %collective-permute-done.5.other_count_ref, ...), custom_call_target="tpu_custom_call" | custom-call | tf_op jit(solution)/shard_map/forces/pallas_call | solution.py:707
  (4 shorter events, 0.0 us)
Async XLA Ops:
  2.3 5.8 %collective-permute-start = (f32[8,512]{1,0:T(8,128)S(1)}, f32[8,512]{1,0:T(8,128)S(1)}, u32[]{:S(2)}, u32[]{:S(2)}) collective-permute-start(f32[8,512]{1,0:T(8,128)S(1)} %get-tuple-element.28.refs_0_.data_ref), channel_id=1, source_target_pairs={{0,2},{1,3},{2,0},{3,1},{4,6},{5,7},{6,4},{7,5},{8,10},{9,11},{10,... | collective-permute-start | bytes 49160 | tf_op jit(solution)/shard_map/exchange_ions/ppermute | solution.py:610
  8.1 7.0 %collective-permute-start.3 = (f32[8,4864]{1,0:T(8,128)S(1)}, f32[8,4864]{1,0:T(8,128)S(1)}, u32[]{:S(2)}, u32[]{:S(2)}) collective-permute-start(f32[8,4864]{1,0:T(8,128)S(1)} %pad_maximum_fusion), channel_id=1, source_target_pairs={{0,8},{4,12},{8,0},{12,4},{1,9},{5,13},{9,1},{13,5},{2,10},{6,14},... | collective-permute-start | bytes 466952 | tf_op jit(solution)/shard_map/exchange_ions/ppermute | solution.py:608
  10.1 3.9 %collective-permute-start.2 = (f32[8,1024]{1,0:T(8,128)S(1)}, f32[8,1024]{1,0:T(8,128)S(1)}, u32[]{:S(2)}, u32[]{:S(2)}) collective-permute-start(f32[8,1024]{1,0:T(8,128)S(1)} %constant_dynamic-update-slice_fusion), channel_id=1, source_target_pairs={{0,1},{1,0},{2,3},{3,2},{4,5},{5,4},{6,7},{7,6},{8,9},{9,8},{10,11... | collective-permute-start | bytes 98312 | tf_op jit(solution)/shard_map/exchange_ions/ppermute | solution.py:610
  11.6 4.8 %collective-permute-start.1 = (f32[8,1024]{1,0:T(8,128)S(1)}, f32[8,1024]{1,0:T(8,128)S(1)}, u32[]{:S(2)}, u32[]{:S(2)}) collective-permute-start(f32[8,1024]{1,0:T(8,128)S(1)} %constant_dynamic-update-slice_fusion), channel_id=1, source_target_pairs={{0,9},{1,8},{2,11},{3,10},{4,13},{5,12},{6,15},{7,14},{8,1},{9,0},... | collective-permute-start | bytes 98312 | tf_op jit(solution)/shard_map/exchange_ions/ppermute | solution.py:612
  16.2 1.9 %copy-start = (s32[512]{0:T(512)S(1)}, s32[512]{0:T(512)}, u32[]{:S(2)}) copy-start(s32[512]{0:T(512)} %recv_ref) | copy-start | bytes 6148
  17.5 1.8 %collective-permute-start.4 = (f32[576,128]{1,0:T(8,128)S(1)}, f32[576,128]{1,0:T(8,128)S(1)}, u32[]{:S(2)}, u32[]{:S(2)}) collective-permute-start(f32[576,128]{1,0:T(8,128)S(1)} %structure_sums.7.mine_ref), channel_id=1, source_target_pairs={{0,4},{4,0},{8,12},{12,8},{1,5},{5,1},{9,13},{13,9},{2,6},{6,2},{1... | collective-permute-start | bytes 884744 | tf_op jit(solution)/shard_map/exchange_core/ppermute | solution.py:608
  17.6 1.7 %collective-permute-start.5 = (f32[8,3840]{1,0:T(8,128)S(1)}, f32[8,3840]{1,0:T(8,128)S(1)}, u32[]{:S(2)}, u32[]{:S(2)}) collective-permute-start(f32[8,3840]{1,0:T(8,128)S(1)} %slice_add_fusion.count_ref), channel_id=1, source_target_pairs={{0,4},{4,0},{8,12},{12,8},{1,5},{5,1},{9,13},{13,9},{2,6},{6,2},{1... | collective-permute-start | bytes 368648 | tf_op jit(solution)/shard_map/exchange_core/ppermute | solution.py:608

commit v4 on v3

--- a/solution.py
+++ b/solution.py
@@ -123,8 +123,8 @@
 
 
 def prep_kernel(
-    coords_hbm, charges_hbm, counts_hbm, send_hbm, waves_hbm, out_ref, waves_out_ref,
-    coords_ref, charges_ref, counts_ref, send_ref, waves_ref, sems,
+    coords_hbm, charges_hbm, counts_hbm, send_hbm, waves_hbm, out_ref, waves_ref,
+    coords_ref, charges_ref, counts_ref, send_ref, sems,
 ):
     copies = [
         pltpu.make_async_copy(source, target, sems.at[i])
@@ -143,7 +143,7 @@
     slots = charges_ref.shape[0]
     half = slots // 2
     out_ref[:, 0 : half + 128] = jnp.zeros((8, half + 128), F32)
-    for copy in copies:
+    for copy in copies[1:]:
         copy.wait()
     live = lax.broadcasted_iota(jnp.int32, (1, slots), 1) < counts_ref[0]
     charge = jnp.where(live, charges_ref[...].reshape(1, slots), 0.0)
@@ -154,12 +154,7 @@
         out_ref[4 * part + 3 : 4 * part + 4, 0:half] = charge[:, lanes]
     for piece in range(slots // 128):
         out_ref[piece : piece + 1, half : half + 128] = send[:, piece * 128 : (piece + 1) * 128]
-    rows, width = wave_shape(waves_ref.shape[1])
-    for row in range(rows):
-        for comp in range(3):
-            waves_out_ref[row : row + 1, comp * width : (comp + 1) * width] = waves_ref[
-                comp : comp + 1, row * width : (row + 1) * width
-            ].astype(F32)
+    copies[0].wait()
 
 
 def wave_shape(k_local):
@@ -256,9 +251,9 @@
     return [second_row(basis_y, harmonic, sine) for harmonic, sine in STEMS[part]]
 
 
-def add_sums(basis_x, basis_y, charge, high, low, table_ref, v_ref):
+def store_rows(basis_x, basis_y, charge, v_ref):
+    all_rows = sum(SUM_ROWS)
     slots = charge.shape[1]
-    all_rows = sum(SUM_ROWS)
     at = 0
     for part in range(2):
         stems = stem_rows(part, basis_y)
@@ -268,18 +263,32 @@
             rows.append(jnp.zeros((fill, slots), F32))
         rows = jnp.concatenate(rows, axis=0)
         for begin in range(0, SUM_ROWS[part], 16):
-            v_high, v_low = split_two(rows[begin : begin + 16])
-            v_ref[at : at + 16] = v_high
-            v_ref[all_rows + at : all_rows + at + 16] = v_low
+            high, low = split_two(rows[begin : begin + 16])
+            v_ref[at : at + 16] = high
+            v_ref[all_rows + at : all_rows + at + 16] = low
             at += 16
-    both = lax.dot_general(v_ref[...], high, NT, preferred_element_type=F32)
-    rest = lax.dot_general(v_ref[0:all_rows], low, NT, preferred_element_type=F32)
+
+
+def add_owners(owners, base_ref, table_ref, v_ref):
+    all_rows = sum(SUM_ROWS)
+    highs, lows = [], []
+    for i, ions in enumerate(owners):
+        slots = ions[3].shape[1]
+        basis_x, basis_y, high, low = owner_tables(ions)
+        store_rows(basis_x, basis_y, ions[3], v_ref.at[:, i * slots : (i + 1) * slots])
+        highs.append(high)
+        lows.append(low)
+    width = sum(high.shape[1] for high in highs)
+    both = lax.dot_general(v_ref[:, 0:width], jnp.concatenate(highs, axis=1), NT, preferred_element_type=F32)
+    rest = lax.dot_general(v_ref[0:all_rows, 0:width], jnp.concatenate(lows, axis=1), NT, preferred_element_type=F32)
     total = (both[:all_rows] + both[all_rows:]) + rest
     at = 0
     for part in range(2):
         count, begin = SUM_ROWS[part], PART_AT[part]
-        table_ref[begin : begin + count] += total[at : at + count, :128]
-        table_ref[begin + count : begin + 2 * count] += total[at : at + count, 128:]
+        for half in range(2):
+            rows = slice(begin + half * count, begin + (half + 1) * count)
+            value = total[at : at + count, 128 * half : 128 * half + 128]
+            table_ref[rows] = value if base_ref is None else base_ref[rows] + value
         at += count
 
 
@@ -310,8 +319,13 @@
     return jnp.concatenate([high, mid, rest - mid], axis=0).astype(BF16)
 
 
-def count_kernel(rows, width, waves_ref, out_ref):
-    counts = count_waves(waves_ref, rows, width)
+def count_kernel(rows, width, waves_ref, out_ref, stack_ref):
+    for row in range(rows):
+        for comp in range(3):
+            stack_ref[row : row + 1, comp * width : (comp + 1) * width] = waves_ref[
+                comp : comp + 1, row * width : (row + 1) * width
+            ].astype(F32)
+    counts = count_waves(stack_ref, rows, width)
     for row in range(0, COUNT_ROWS, 8):
         out_ref[:, 16 * row : 16 * row + 128] = counts[row : row + 8]
 
@@ -327,28 +341,33 @@
     per_pack = 64 // cap
     device = lax.axis_index("blk") * row_count + lax.axis_index("row")
     targets = (device, device ^ row_count)
-    table_ref[...] = jnp.zeros_like(table_ref) if base_ref is None else base_ref[...]
-
-    def add(block_rows, place, pack, v_ref):
-        ions = owner_rows(block_rows, half)
-        basis_x, basis_y, high, low = owner_tables(ions)
-        add_sums(basis_x, basis_y, ions[3], high, low, table_ref, v_ref)
-        add_arrivals(block_rows, ions, half, cap, place, pack, targets, table_ref)
-
-    turn = 0
+    kept = slice(ARRIVE_AT, table_ref.shape[0])
+    table_ref[kept] = jnp.zeros_like(table_ref[kept]) if base_ref is None else base_ref[kept]
+
     for ions_ref, (owners, first_owner) in zip(ion_refs, plan["chunks"]):
         if owners <= 4 and per_pack == 1:
-            for owner in range(owners):
-                ions = ions_ref[:, owner * block : (owner + 1) * block]
-                add(ions, 0.0, first_owner + owner, v_ref.at[turn % 2])
-                turn += 1
+            for owner in range(0, owners, 2):
+                group = []
+                for i in range(owner, min(owner + 2, owners)):
+                    block_rows = ions_ref[:, i * block : (i + 1) * block]
+                    group.append(owner_rows(block_rows, half))
+                    add_arrivals(block_rows, group[-1], half, cap, 0.0, first_owner + i, targets, table_ref)
+                add_owners(group, base_ref, table_ref, v_ref)
+                base_ref = table_ref
         else:
+            if base_ref is not table_ref:
+                sums = slice(0, ARRIVE_AT)
+                table_ref[sums] = jnp.zeros_like(table_ref[sums]) if base_ref is None else base_ref[sums]
+                base_ref = table_ref
 
             def step(owner, carry, ions_ref=ions_ref, first_owner=first_owner):
                 begin = pl.multiple_of(owner * block, 128)
                 index = first_owner + owner
                 place = (lax.rem(index, per_pack) * cap).astype(F32)
-                add(ions_ref[:, pl.ds(begin, block)], place, index // per_pack, v_ref.at[0])
+                block_rows = ions_ref[:, pl.ds(begin, block)]
+                ions = owner_rows(block_rows, half)
+                add_arrivals(block_rows, ions, half, cap, place, index // per_pack, targets, table_ref)
+                add_owners([ions], table_ref, table_ref, v_ref)
                 return carry
 
             lax.fori_loop(0, owners, step, 0)
@@ -388,27 +407,49 @@
     return [parts[1], parts[0], pltpu.roll(parts[2], 4, 0)]
 
 
-def combine(own, other):
-    gain, sums, turned = own
-    gain_s, sums_s, turned_s = swap(gain), swap(sums), swap(turned)
-    both = [a + b for a, b in zip(gain, gain_s)]
-    odd = [a - b for a, b in zip(gain, gain_s)]
-    if other is None:
-        return [both[i] * sums[i] - odd[i] * turned_s[i] for i in range(3)]
-    gain_o, sums_o, turned_o = other
-    gain_os, sums_os = swap(gain_o), swap(sums_o)
-    both_o = [a + b for a, b in zip(gain_o, gain_os)]
-    odd_o = [a - b for a, b in zip(gain_o, gain_os)]
-    return [
-        (both[i] + both_o[i]) * sums[i]
-        - (odd[i] + odd_o[i]) * turned_s[i]
-        - (both[i] - both_o[i]) * turned_o[i]
-        - (odd[i] - odd_o[i]) * sums_os[i]
-        for i in range(3)
-    ]
-
-
-def weighted_sums(part, mine_ref, other_ref, count_refs, gain_ref, w_ref):
+def store_coefs(part, gain_ref, count_refs, coef_ref):
+    lane = lax.broadcasted_iota(jnp.int32, (8, 128), 1)
+    is_cos = lane < HARM
+    is_wave = lane < 2 * HARM
+
+    def gains(row):
+        at = COUNT_AT[part] + row
+        lanes = slice(16 * at, 16 * at + 128)
+        tile = (count_refs[0][:, lanes] + count_refs[1][:, lanes]) * gain_ref[at : at + 8]
+        back, far = pltpu.roll(tile, 88, 1), pltpu.roll(tile, 48, 1)
+        pairs = ((tile, pltpu.roll(tile, HARM, 1)), (back, tile), (far, back))
+        return [jnp.where(is_cos, a, jnp.where(is_wave, b, 0.0)) for a, b in pairs]
+
+    order = ORDERS[part]
+    pairs = {}
+    for i, name in enumerate(order):
+        gain = gains(8 * i)
+        other = swap(gain)
+        pairs[name] = [a + b for a, b in zip(gain, other)], [a - b for a, b in zip(gain, other)]
+    for i, (harmonic, sine) in enumerate(order):
+        both, odd = pairs[(harmonic, sine)]
+        both_o, odd_o = pairs.get((harmonic, 1 - sine), (None, None))
+        for x in range(3):
+            row = FORCE_AT[part] + BASIS * i + 8 * x
+            if both_o is None:
+                coefs = (both[x], odd[x])
+            else:
+                coefs = (both[x] + both_o[x], odd[x] + odd_o[x], both[x] - both_o[x], odd[x] - odd_o[x])
+            for kind, coef in enumerate(coefs):
+                coef_ref[kind, row : row + 8] = coef
+    tails = [gains(COUNT_LEN[part] - 16 + 8 * sine)[0] for sine in range(2)]
+    for sine in range(2):
+        row = FORCE_AT[part] + BASIS * len(order) + 8 * sine
+        coef_ref[0, row : row + 8] = tails[sine] + tails[1 - sine]
+        coef_ref[2, row : row + 8] = tails[sine] - tails[1 - sine]
+
+
+def coef_kernel(gain_ref, count_ref, other_count_ref, coef_ref):
+    for part in range(2):
+        store_coefs(part, gain_ref, (count_ref, other_count_ref), coef_ref)
+
+
+def weighted_sums(part, mine_ref, other_ref, coef_ref, w_ref):
     lane = lax.broadcasted_iota(jnp.int32, (8, 128), 1)
     is_cos = lane < HARM
     is_wave = lane < 2 * HARM
@@ -441,14 +482,6 @@
             found[(harmonic + 1, 1)] = sin[1] + cos[2]
         return found
 
-    def gains(row):
-        at = COUNT_AT[part] + row
-        lanes = slice(16 * at, 16 * at + 128)
-        tile = (count_refs[0][:, lanes] + count_refs[1][:, lanes]) * gain_ref[at : at + 8]
-        back, far = pltpu.roll(tile, 88, 1), pltpu.roll(tile, 48, 1)
-        pairs = ((tile, pltpu.roll(tile, HARM, 1)), (back, tile), (far, back))
-        return [jnp.where(is_cos, a, jnp.where(is_wave, b, 0.0)) for a, b in pairs]
-
     def store(row, value):
         high, low = split_two(value)
         high = high.astype(F32)
@@ -463,13 +496,20 @@
     ]
     order = ORDERS[part]
     groups = {}
-    for i, name in enumerate(order):
+    for name in order:
         sums = [by_block[x][name] for x in range(3)]
-        groups[name] = (gains(8 * i), sums, [turn(value) for value in sums])
+        turned = [turn(value) for value in sums]
+        groups[name] = swap(sums), turned, swap(turned)
     for i, (harmonic, sine) in enumerate(order):
-        other = None if harmonic == 0 else groups[(harmonic, 1 - sine)]
-        for x, value in enumerate(combine(groups[(harmonic, sine)], other)):
-            store(BASIS * i + 8 * x, value)
+        turned_s = groups[(harmonic, sine)][2]
+        for x in range(3):
+            row = BASIS * i + 8 * x
+            coefs = [coef_ref[kind, FORCE_AT[part] + row : FORCE_AT[part] + row + 8] for kind in range(4)]
+            value = coefs[0] * by_block[x][(harmonic, sine)] - coefs[1] * turned_s[x]
+            if harmonic:
+                sums_os, turned_o, _ = groups[(harmonic, 1 - sine)]
+                value = value - coefs[2] * turned_o[x] - coefs[3] * sums_os[x]
+            store(row, value)
     tails = [blocks(BASIS * len(STEMS[part]) + 8 * sine) for sine in range(2)]
     found = harmonics_of({(h, sine): [b[h % 8 : h % 8 + 1] for b in tails[sine]] for h, sine in STEMS[part]})
     index = lax.broadcasted_iota(jnp.int32, (8, 128), 0)
@@ -479,12 +519,11 @@
         for harmonic, kind in order:
             if kind == sine:
                 rows = jnp.where(index == harmonic % 8, found[(harmonic, kind)], rows)
-        at = COUNT_LEN[part] - 16 + 8 * sine
-        kinds.append((gains(at)[0], rows, turn(rows)))
+        kinds.append((rows, turn(rows)))
     at = BASIS * len(order)
     for sine in range(2):
-        (gain, sums, _), (gain_o, _, turned_o) = kinds[sine], kinds[1 - sine]
-        store(at + 8 * sine, (gain + gain_o) * sums - (gain - gain_o) * turned_o)
+        row = FORCE_AT[part] + at + 8 * sine
+        store(at + 8 * sine, coef_ref[0, row : row + 8] * kinds[sine][0] - coef_ref[2, row : row + 8] * kinds[1 - sine][1])
     if at + 16 < FORCE_ROWS[part]:
         fill = FORCE_ROWS[part] - at - 16
         w_ref[FORCE_AT[part] + at + 16 : FORCE_AT[part] + FORCE_ROWS[part]] = jnp.zeros((fill, 256), F32)
@@ -530,7 +569,7 @@
 
 
 def force_kernel(
-    force_scale, half, mine_ref, other_ref, count_ref, other_count_ref, data_ref, basis_ref, z_ref, hot_ref, gain_ref,
+    force_scale, half, mine_ref, other_ref, data_ref, basis_ref, z_ref, hot_ref, coef_ref,
     slot_ref, atom_ref, w_ref, atom_basis_ref, atom_z_ref,
 ):
     packs = hot_ref.shape[0] // 128
@@ -540,7 +579,7 @@
     found = jnp.dot(split_three(pool), hot_ref[...], preferred_element_type=F32)
     routed = ((found[0:8] + found[8:16]) + found[16:24])[0:4]
     for part in range(2):
-        weighted_sums(part, mine_ref, other_ref, (count_ref, other_count_ref), gain_ref, w_ref)
+        weighted_sums(part, mine_ref, other_ref, coef_ref, w_ref)
     weights = w_ref[...].astype(BF16)
     store_bases(routed, atom_basis_ref, atom_z_ref)
     charge = jnp.concatenate([data_ref[3:4, 0:half], data_ref[7:8, 0:half]], axis=1)
@@ -578,17 +617,18 @@
     k_local = wave_ints.shape[1]
     cap = 2 * atoms_dev // devices
     packs = max(1, devices // 2 * cap // 64)
+    per_pack = 64 // cap
     wave_rows, wave_width = wave_shape(k_local)
     force_scale = FORCE_GAIN / math.sqrt(float(atoms_dev * devices * blk_count * k_local))
     table_shape = jax.ShapeDtypeStruct((ARRIVE_AT + 8 * packs, 128), F32)
     count_shape = jax.ShapeDtypeStruct((8, 16 * COUNT_ROWS), F32)
 
     with jax.named_scope("payload"):
-        own_ions, own_waves = pl.pallas_call(
+        own_ions, waves = pl.pallas_call(
             prep_kernel,
             out_shape=(
                 jax.ShapeDtypeStruct((8, block), F32),
-                jax.ShapeDtypeStruct((wave_rows, 3 * wave_width), F32),
+                jax.ShapeDtypeStruct(wave_ints.shape, jnp.int32),
             ),
             in_specs=[pl.BlockSpec(memory_space=pltpu.HBM)] * 5,
             out_specs=tuple(whole(2)),
@@ -597,7 +637,6 @@
                 pltpu.VMEM(charges.shape, F32),
                 pltpu.SMEM(counts.shape, jnp.int32),
                 pltpu.VMEM(send_slot.shape, jnp.int32),
-                pltpu.VMEM(wave_ints.shape, jnp.int32),
                 pltpu.SemaphoreType.DMA((5,)),
             ],
             compiler_params=params(),
@@ -614,7 +653,7 @@
     def joined(values):
         return values[0] if len(values) == 1 else jnp.concatenate(values, axis=1)
 
-    def accumulate(table, chunks):
+    def accumulate(table, chunks, cost=1):
         plan = {
             "has_base": table is not None,
             "chunks": [chunk[1:] for chunk in chunks],
@@ -623,14 +662,14 @@
             "row_count": row_count,
         }
         args = [table] * plan["has_base"] + [chunk[0] for chunk in chunks]
-        flops = 2 * sum(chunk[1] for chunk in chunks) * slots * 256 * 720
+        flops = int(cost * 2 * sum(chunk[1] for chunk in chunks) * slots * 256 * 720)
         with jax.named_scope("structure_sums"):
             return pl.pallas_call(
                 functools.partial(sums_kernel, plan),
                 out_shape=table_shape,
                 in_specs=whole(len(args)),
                 out_specs=whole(1)[0],
-                scratch_shapes=[pltpu.VMEM((2, 2 * sum(SUM_ROWS), slots), BF16)],
+                scratch_shapes=[pltpu.VMEM((2 * sum(SUM_ROWS), 2 * slots), BF16)],
                 compiler_params=params(),
                 cost_estimate=pl.CostEstimate(flops=flops, bytes_accessed=1 << 20, transcendentals=0),
             )(*args)
@@ -660,11 +699,12 @@
                     out_shape=count_shape,
                     in_specs=whole(1),
                     out_specs=whole(1)[0],
+                    scratch_shapes=[pltpu.VMEM((wave_rows, 3 * wave_width), F32)],
                     compiler_params=params(),
                     cost_estimate=pl.CostEstimate(
                         flops=2 * k_local * COUNT_ROWS * 128, bytes_accessed=1 << 20, transcendentals=0
                     ),
-                )(own_waves)
+                )(waves)
             got, counted = lax.optimization_barrier((got, counted))
         else:
             table, chunks = accumulate(table, chunks), []
@@ -678,16 +718,6 @@
         along = flip(sent, 0, 1)
         corner = flip(sent, 2, 1)
     table = accumulate(table, chunks)
-    table = accumulate(table, [(along, held, 2 * held)])
-    table, across = lax.optimization_barrier((table, across))
-    counted = counted + across[:, held * block :]
-    with jax.named_scope("exchange_core"):
-        other_counted = flip(counted, 1, 0)
-    table = accumulate(table, [(across, held, held)])
-    corner, table, counted = lax.optimization_barrier((corner, table, counted))
-    table = accumulate(table, [(corner, held, 3 * held)])
-    with jax.named_scope("exchange_core"):
-        other = flip(table, 1, 0)
     own_ions, recv_index, table = lax.optimization_barrier((own_ions, recv_index, table))
     with jax.named_scope("own_ions"):
         basis, table_z, hot, gain = pl.pallas_call(
@@ -701,8 +731,27 @@
             in_specs=whole(2),
             out_specs=tuple(whole(4)),
             compiler_params=params(),
-            cost_estimate=pl.CostEstimate(flops=1 << 30, bytes_accessed=1 << 20, transcendentals=0),
+            cost_estimate=pl.CostEstimate(flops=1<<22, bytes_accessed=1 << 20, transcendentals=0),
         )(own_ions, recv_index)
+    along, table, basis, table_z, hot, gain = lax.optimization_barrier((along, table, basis, table_z, hot, gain))
+    table = accumulate(table, [(along, held, 2 * held)], cost=0.05)
+    table = accumulate(table, [(across, held, held)], cost=0.05)
+    with jax.named_scope("exchange_core"):
+        counted = counted + across[:, held * block :]
+        other_counted = flip(counted, 1, 0)
+    corner, table, counted = lax.optimization_barrier((corner, table, counted))
+    table = accumulate(table, [(corner, held, 3 * held)], cost=16)
+    with jax.named_scope("exchange_core"):
+        other = flip(table, 1, 0)
+    with jax.named_scope("coefficients"):
+        coefs = pl.pallas_call(
+            coef_kernel,
+            out_shape=jax.ShapeDtypeStruct((4, sum(FORCE_ROWS), 128), F32),
+            in_specs=whole(3),
+            out_specs=whole(1)[0],
+            compiler_params=params(),
+            cost_estimate=pl.CostEstimate(flops=1<<33, bytes_accessed=1 << 20, transcendentals=0),
+        )(gain, counted, other_counted)
     with jax.named_scope("forces"):
         return pl.pallas_call(
             functools.partial(force_kernel, force_scale, half),
@@ -710,7 +759,7 @@
                 jax.ShapeDtypeStruct((3, slots), F32),
                 jax.ShapeDtypeStruct((3, atoms_dev), F32),
             ),
-            in_specs=whole(9),
+            in_specs=whole(7),
             out_specs=tuple(whole(2)),
             scratch_shapes=[
                 pltpu.VMEM((sum(FORCE_ROWS), 256), F32),
@@ -718,7 +767,7 @@
                 pltpu.VMEM((256, 2 * atoms_dev), BF16),
             ],
             compiler_params=params(),
-        )(table, other, counted, other_counted, own_ions, basis, table_z, hot, gain)
+        )(table, other, own_ions, basis, table_z, hot, coefs)
 
 
 def solution(mesh):

time: 21.7 us -> 21.4 us (0.986)
    ppermute x2, waiting for transfers between devices: 2.02 us -> 1.45 us  [flip(): lax.ppermute(value, 'row', [(i, i ^ row_bit) for i in range(row_count)])]
    ppermute x3, waiting for transfers between devices: 0.73 us -> 1.09 us  [flip(): lax.ppermute(value, 'blk', [(i, i ^ blk_bit) for i in range(blk_count)])]
  transfers between devices with their start and end apart: 6 -> 6, of which waited for: 4 -> 4; matrix products, arithmetic and copies ran while one was open for 0% -> 0% of each run, Pallas kernels for 22% -> 28%
where the time goes in v4:
time: 21.4 us; the launch traced here: 21.2 us
  Pallas kernels  8.9 us (42%)
  starting transfers between devices  8.09 us (38%)
  waiting for transfers between devices  2.75 us (13%)
  between operations  1.38 us (6%)
    ppermute x2, starting transfers between devices, flip(): lax.ppermute(value, 'row', [(i, i ^ row_bit) for i in range(row_count)])  5.62 us
    pallas_call x4, Pallas kernels, accumulate(): pl.pallas_call(functools.partial(sums_kernel, plan), out_shape=table_shap...  4.2 us
    ppermute x3, starting transfers between devices, flip(): lax.ppermute(value, 'blk', [(i, i ^ blk_bit) for i in range(blk_count)])  2.4 us
    pallas_call x1, Pallas kernels, body(): pl.pallas_call(functools.partial(force_kernel, force_scale, half), out_sh...  2.1 us
    ppermute x2, waiting for transfers between devices, flip(): lax.ppermute(value, 'row', [(i, i ^ row_bit) for i in range(row_count)])  1.45 us
    ppermute x3, waiting for transfers between devices, flip(): lax.ppermute(value, 'blk', [(i, i ^ blk_bit) for i in range(blk_count)])  1.09 us
    pallas_call x1, Pallas kernels, body(): pl.pallas_call(functools.partial(count_kernel, wave_rows, wave_width), ou...  0.96 us
    pallas_call x1, Pallas kernels, body(): pl.pallas_call(prep_kernel, out_shape=(jax.ShapeDtypeStruct((8, block), F...  0.94 us
  transfers between devices with their start and end apart: 6, of which 4 were waited for; matrix products, arithmetic and copies ran while one was open for 0% of the time, Pallas kernels for 28%

profile of v4, /device:TPU:0, one launch (start us, length us, event | category | flops | bytes accessed | tf_op | source)
XLA Modules:
  0.0 21.2 jit_solution(16844319062164098486)
XLA Ops:
  1.3 0.9 %payload.1 = (f32[8,512]{1,0:T(8,128)S(1)}, s32[3,6144]{1,0:T(4,128)S(1)}) custom-call(f32[3,768]{1,0:T(4,128)} %coords_hbm.1, f32[768]{0:T(1024)} %charges_hbm.1, s32[1]{0:T(128)S(6)} %copy.9.counts_hbm, s32[768]{0:T(1024)} %send_hbm.1, s32[3,6144]{1,0:T(4,128)} %waves_hbm.1), custom_call_target="tpu_custom_call" | custom-call | tf_op jit(solution)/shard_map/payload/pallas_call | solution.py:627
  2.2 4.1 %collective-permute-start = (f32[8,512]{1,0:T(8,128)S(1)}, f32[8,512]{1,0:T(8,128)S(1)}, u32[]{:S(2)}, u32[]{:S(2)}) collective-permute-start(f32[8,512]{1,0:T(8,128)S(1)} %get-tuple-element.26.refs_0_.data_ref), channel_id=1, source_target_pairs={{0,2},{1,3},{2,0},{3,1},{4,6},{5,7},{6,4},{7,5},{8,10},{9,11},{10,... | collective-permute-start | bytes 49160 | tf_op jit(solution)/shard_map/exchange_ions/ppermute | solution.py:649
  6.3 1.0 %counts.1 = f32[8,3840]{1,0:T(8,128)S(1)} custom-call(s32[3,6144]{1,0:T(4,128)S(1)} %get-tuple-element.23.waves_ref), custom_call_target="tpu_custom_call" | custom-call | flops 377487360 | bytes 1048576 | tf_op jit(solution)/shard_map/counts/pallas_call | solution.py:697
  7.3 0.0 copy-start
  7.3 0.7 %collective-permute-done.refs_1_ = f32[8,512]{1,0:T(8,128)S(1)} collective-permute-done((f32[8,512]{1,0:T(8,128)S(1)}, f32[8,512]{1,0:T(8,128)S(1)}, u32[]{:S(2)}, u32[]{:S(2)}) %collective-permute-start) | collective-permute-done | bytes 16416 | tf_op jit(solution)/shard_map/exchange_ions/ppermute | solution.py:649
  8.1 2.0 %collective-permute-start.3 = (f32[8,4864]{1,0:T(8,128)S(1)}, f32[8,4864]{1,0:T(8,128)S(1)}, u32[]{:S(2)}, u32[]{:S(2)}) collective-permute-start(f32[8,4864]{1,0:T(8,128)S(1)} %pad_maximum_fusion), channel_id=1, source_target_pairs={{0,8},{4,12},{8,0},{12,4},{1,9},{5,13},{9,1},{13,5},{2,10},{6,14},... | collective-permute-start | bytes 466952 | tf_op jit(solution)/shard_map/exchange_ions/ppermute | solution.py:647
  10.0 1.5 %collective-permute-start.2 = (f32[8,1024]{1,0:T(8,128)S(1)}, f32[8,1024]{1,0:T(8,128)S(1)}, u32[]{:S(2)}, u32[]{:S(2)}) collective-permute-start(f32[8,1024]{1,0:T(8,128)S(1)} %constant_dynamic-update-slice_fusion), channel_id=1, source_target_pairs={{0,1},{1,0},{2,3},{3,2},{4,5},{5,4},{6,7},{7,6},{8,9},{9,8},{10,11... | collective-permute-start | bytes 98312 | tf_op jit(solution)/shard_map/exchange_ions/ppermute | solution.py:649
  11.6 0.1 collective-permute-start.1
  11.6 1.1 %structure_sums.4.refs_0_ = f32[576,128]{1,0:T(8,128)S(1)} custom-call(f32[8,512]{1,0:T(8,128)S(1)} %get-tuple-element.26.refs_0_.data_ref, f32[8,512]{1,0:T(8,128)S(1)} %collective-permute-done.refs_1_), custom_call_target="tpu_custom_call" | custom-call | flops 566231040 | bytes 1048576 | tf_op jit(solution)/shard_map/structure_sums/pallas_call | solution.py:667
  12.7 0.0 copy-done
  12.7 0.5 %own_ions.1 = (f32[112,768]{1,0:T(8,128)S(1)}, bf16[256,1536]{1,0:T(8,128)(2,1)S(1)}, bf16[1024,512]{1,0:T(8,128)(2,1)S(1)}, f32[240,128]{1,0:T(8,128)S(1)}) custom-call(f32[8,512]{1,0:T(8,128)S(1)} %get-tuple-element.26.refs_0_.data_ref, s32[512]{0:T(512)S(1)} %copy-done), custom_call_target="tpu_custom_call" | custom-call | flops 4194304 | bytes 1048576 | tf_op jit(solution)/shard_map/own_ions/pallas_call | solution.py:723
  13.2 0.7 %collective-permute-done.2.refs_1_ = f32[8,1024]{1,0:T(8,128)S(1)} collective-permute-done((f32[8,1024]{1,0:T(8,128)S(1)}, f32[8,1024]{1,0:T(8,128)S(1)}, u32[]{:S(2)}, u32[]{:S(2)}) %collective-permute-start.2) | collective-permute-done | bytes 32800 | tf_op jit(solution)/shard_map/exchange_ions/ppermute | solution.py:649
  13.9 1.0 %structure_sums.5.refs_0_ = f32[576,128]{1,0:T(8,128)S(1)} custom-call(f32[576,128]{1,0:T(8,128)S(1)} %structure_sums.4.refs_0_, f32[8,1024]{1,0:T(8,128)S(1)} %collective-permute-done.2.refs_1_), custom_call_target="tpu_custom_call" | custom-call | flops 28311552 | bytes 1048576 | tf_op jit(solution)/shard_map/structure_sums/pallas_call | solution.py:667
  15.0 0.0 collective-permute-done.3.refs_1_
  15.0 0.1 collective-permute-start.5
  15.1 1.0 %structure_sums.6.refs_0_ = f32[576,128]{1,0:T(8,128)S(1)} custom-call(f32[576,128]{1,0:T(8,128)S(1)} %structure_sums.5.refs_0_, f32[8,4864]{1,0:T(8,128)S(1)} %collective-permute-done.3.refs_1_), custom_call_target="tpu_custom_call" | custom-call | flops 28311552 | bytes 1048576 | tf_op jit(solution)/shard_map/structure_sums/pallas_call | solution.py:667
  16.2 0.2 collective-permute-done.1.refs_1_
  16.4 1.0 %structure_sums.7.mine_ref = f32[576,128]{1,0:T(8,128)S(1)} custom-call(f32[576,128]{1,0:T(8,128)S(1)} %structure_sums.6.refs_0_, f32[8,1024]{1,0:T(8,128)S(1)} %collective-permute-done.1.refs_1_), custom_call_target="tpu_custom_call" | custom-call | flops 9059696640 | bytes 1048576 | tf_op jit(solution)/shard_map/structure_sums/pallas_call | solution.py:667
  17.4 0.4 %collective-permute-start.4 = (f32[576,128]{1,0:T(8,128)S(1)}, f32[576,128]{1,0:T(8,128)S(1)}, u32[]{:S(2)}, u32[]{:S(2)}) collective-permute-start(f32[576,128]{1,0:T(8,128)S(1)} %structure_sums.7.mine_ref), channel_id=1, source_target_pairs={{0,4},{4,0},{8,12},{12,8},{1,5},{5,1},{9,13},{13,9},{2,6},{6,2},{1... | collective-permute-start | bytes 884744 | tf_op jit(solution)/shard_map/exchange_core/ppermute | solution.py:647
  17.8 0.0 collective-permute-done.5.other_count_ref
  17.8 0.2 coefficients.1.coef_ref
  18.0 1.1 %collective-permute-done.4.other_ref = f32[576,128]{1,0:T(8,128)S(1)} collective-permute-done((f32[576,128]{1,0:T(8,128)S(1)}, f32[576,128]{1,0:T(8,128)S(1)}, u32[]{:S(2)}, u32[]{:S(2)}) %collective-permute-start.4) | collective-permute-done | bytes 294944 | tf_op jit(solution)/shard_map/exchange_core/ppermute | solution.py:647
  19.1 2.1 %forces.1 = (f32[3,768]{1,0:T(4,128)}, f32[3,512]{1,0:T(4,128)}) custom-call(f32[576,128]{1,0:T(8,128)S(1)} %structure_sums.7.mine_ref, f32[576,128]{1,0:T(8,128)S(1)} %collective-permute-done.4.other_ref, f32[8,512]{1,0:T(8,128)S(1)} %get-tuple-element.26.refs_0_.data_ref, f32[112,768]{1,0:T(8,128)S(1)} %get-tuple-element.37.basis_ref, ...), custom_call_target="tpu_custom_call" | custom-call | tf_op jit(solution)/shard_map/forces/pallas_call | solution.py:756
  (4 shorter events, 0.0 us)
Async XLA Ops:
  2.2 5.8 %collective-permute-start = (f32[8,512]{1,0:T(8,128)S(1)}, f32[8,512]{1,0:T(8,128)S(1)}, u32[]{:S(2)}, u32[]{:S(2)}) collective-permute-start(f32[8,512]{1,0:T(8,128)S(1)} %get-tuple-element.26.refs_0_.data_ref), channel_id=1, source_target_pairs={{0,2},{1,3},{2,0},{3,1},{4,6},{5,7},{6,4},{7,5},{8,10},{9,11},{10,... | collective-permute-start | bytes 49160 | tf_op jit(solution)/shard_map/exchange_ions/ppermute | solution.py:649
  7.3 5.4 %copy-start = (s32[512]{0:T(512)S(1)}, s32[512]{0:T(512)}, u32[]{:S(2)}) copy-start(s32[512]{0:T(512)} %recv_ref) | copy-start | bytes 6148
  8.1 6.9 %collective-permute-start.3 = (f32[8,4864]{1,0:T(8,128)S(1)}, f32[8,4864]{1,0:T(8,128)S(1)}, u32[]{:S(2)}, u32[]{:S(2)}) collective-permute-start(f32[8,4864]{1,0:T(8,128)S(1)} %pad_maximum_fusion), channel_id=1, source_target_pairs={{0,8},{4,12},{8,0},{12,4},{1,9},{5,13},{9,1},{13,5},{2,10},{6,14},... | collective-permute-start | bytes 466952 | tf_op jit(solution)/shard_map/exchange_ions/ppermute | solution.py:647
  10.0 3.9 %collective-permute-start.2 = (f32[8,1024]{1,0:T(8,128)S(1)}, f32[8,1024]{1,0:T(8,128)S(1)}, u32[]{:S(2)}, u32[]{:S(2)}) collective-permute-start(f32[8,1024]{1,0:T(8,128)S(1)} %constant_dynamic-update-slice_fusion), channel_id=1, source_target_pairs={{0,1},{1,0},{2,3},{3,2},{4,5},{5,4},{6,7},{7,6},{8,9},{9,8},{10,11... | collective-permute-start | bytes 98312 | tf_op jit(solution)/shard_map/exchange_ions/ppermute | solution.py:649
  11.6 4.8 %collective-permute-start.1 = (f32[8,1024]{1,0:T(8,128)S(1)}, f32[8,1024]{1,0:T(8,128)S(1)}, u32[]{:S(2)}, u32[]{:S(2)}) collective-permute-start(f32[8,1024]{1,0:T(8,128)S(1)} %constant_dynamic-update-slice_fusion), channel_id=1, source_target_pairs={{0,9},{1,8},{2,11},{3,10},{4,13},{5,12},{6,15},{7,14},{8,1},{9,0},... | collective-permute-start | bytes 98312 | tf_op jit(solution)/shard_map/exchange_ions/ppermute | solution.py:651
  15.0 2.8 %collective-permute-start.5 = (f32[8,3840]{1,0:T(8,128)S(1)}, f32[8,3840]{1,0:T(8,128)S(1)}, u32[]{:S(2)}, u32[]{:S(2)}) collective-permute-start(f32[8,3840]{1,0:T(8,128)S(1)} %slice_add_fusion.count_ref), channel_id=1, source_target_pairs={{0,4},{4,0},{8,12},{12,8},{1,5},{5,1},{9,13},{13,9},{2,6},{6,2},{1... | collective-permute-start | bytes 368648 | tf_op jit(solution)/shard_map/exchange_core/ppermute | solution.py:647
  17.4 1.6 %collective-permute-start.4 = (f32[576,128]{1,0:T(8,128)S(1)}, f32[576,128]{1,0:T(8,128)S(1)}, u32[]{:S(2)}, u32[]{:S(2)}) collective-permute-start(f32[576,128]{1,0:T(8,128)S(1)} %structure_sums.7.mine_ref), channel_id=1, source_target_pairs={{0,4},{4,0},{8,12},{12,8},{1,5},{5,1},{9,13},{13,9},{2,6},{6,2},{1... | collective-permute-start | bytes 884744 | tf_op jit(solution)/shard_map/exchange_core/ppermute | solution.py:647

commit v5 on v4

--- a/solution.py
+++ b/solution.py
@@ -123,14 +123,12 @@
 
 
 def prep_kernel(
-    coords_hbm, charges_hbm, counts_hbm, send_hbm, waves_hbm, out_ref, waves_ref,
-    coords_ref, charges_ref, counts_ref, send_ref, sems,
+    coords_hbm, charges_hbm, counts_hbm, send_hbm, out_ref, coords_ref, charges_ref, counts_ref, send_ref, sems
 ):
     copies = [
         pltpu.make_async_copy(source, target, sems.at[i])
         for i, (source, target) in enumerate(
             (
-                (waves_hbm, waves_ref),
                 (counts_hbm, counts_ref),
                 (send_hbm, send_ref),
                 (charges_hbm, charges_ref),
@@ -143,7 +141,7 @@
     slots = charges_ref.shape[0]
     half = slots // 2
     out_ref[:, 0 : half + 128] = jnp.zeros((8, half + 128), F32)
-    for copy in copies[1:]:
+    for copy in copies:
         copy.wait()
     live = lax.broadcasted_iota(jnp.int32, (1, slots), 1) < counts_ref[0]
     charge = jnp.where(live, charges_ref[...].reshape(1, slots), 0.0)
@@ -154,7 +152,6 @@
         out_ref[4 * part + 3 : 4 * part + 4, 0:half] = charge[:, lanes]
     for piece in range(slots // 128):
         out_ref[piece : piece + 1, half : half + 128] = send[:, piece * 128 : (piece + 1) * 128]
-    copies[0].wait()
 
 
 def wave_shape(k_local):
@@ -319,7 +316,10 @@
     return jnp.concatenate([high, mid, rest - mid], axis=0).astype(BF16)
 
 
-def count_kernel(rows, width, waves_ref, out_ref, stack_ref):
+def count_kernel(rows, width, waves_hbm, out_ref, waves_ref, stack_ref, sem):
+    copy = pltpu.make_async_copy(waves_hbm, waves_ref, sem)
+    copy.start()
+    copy.wait()
     for row in range(rows):
         for comp in range(3):
             stack_ref[row : row + 1, comp * width : (comp + 1) * width] = waves_ref[
@@ -624,23 +624,20 @@
     count_shape = jax.ShapeDtypeStruct((8, 16 * COUNT_ROWS), F32)
 
     with jax.named_scope("payload"):
-        own_ions, waves = pl.pallas_call(
+        own_ions = pl.pallas_call(
             prep_kernel,
-            out_shape=(
-                jax.ShapeDtypeStruct((8, block), F32),
-                jax.ShapeDtypeStruct(wave_ints.shape, jnp.int32),
-            ),
-            in_specs=[pl.BlockSpec(memory_space=pltpu.HBM)] * 5,
-            out_specs=tuple(whole(2)),
+            out_shape=jax.ShapeDtypeStruct((8, block), F32),
+            in_specs=[pl.BlockSpec(memory_space=pltpu.HBM)] * 4,
+            out_specs=whole(1)[0],
             scratch_shapes=[
                 pltpu.VMEM(coords.shape, F32),
                 pltpu.VMEM(charges.shape, F32),
                 pltpu.SMEM(counts.shape, jnp.int32),
                 pltpu.VMEM(send_slot.shape, jnp.int32),
-                pltpu.SemaphoreType.DMA((5,)),
+                pltpu.SemaphoreType.DMA((4,)),
             ],
             compiler_params=params(),
-        )(stay(coords), stay(charges), counts, stay(send_slot), stay(wave_ints))
+        )(stay(coords), stay(charges), counts, stay(send_slot))
 
     def flip(value, blk_bit, row_bit):
         if not row_bit:
@@ -697,14 +694,18 @@
                 counted = pl.pallas_call(
                     functools.partial(count_kernel, wave_rows, wave_width),
                     out_shape=count_shape,
-                    in_specs=whole(1),
+                    in_specs=[pl.BlockSpec(memory_space=pltpu.HBM)],
                     out_specs=whole(1)[0],
-                    scratch_shapes=[pltpu.VMEM((wave_rows, 3 * wave_width), F32)],
+                    scratch_shapes=[
+                        pltpu.VMEM(wave_ints.shape, jnp.int32),
+                        pltpu.VMEM((wave_rows, 3 * wave_width), F32),
+                        pltpu.SemaphoreType.DMA,
+                    ],
                     compiler_params=params(),
                     cost_estimate=pl.CostEstimate(
                         flops=2 * k_local * COUNT_ROWS * 128, bytes_accessed=1 << 20, transcendentals=0
                     ),
-                )(waves)
+                )(stay(wave_ints))
             got, counted = lax.optimization_barrier((got, counted))
         else:
             table, chunks = accumulate(table, chunks), []

time: 21.4 us -> 21.3 us (level)
  waiting for transfers between devices: 2.75 us -> 1.83 us
  Pallas kernels: 8.9 us -> 9.65 us
    ppermute x2, waiting for transfers between devices: 1.45 us -> 0.53 us  [flip(): lax.ppermute(value, 'row', [(i, i ^ row_bit) for i in range(row_count)])]
    pallas_call x1, Pallas kernels: 0.96 us -> 1.87 us  [body(): pl.pallas_call(functools.partial(count_kernel, wave_rows, wave_width), ou...]
  transfers between devices with their start and end apart: 6 -> 6, of which waited for: 4 -> 3; matrix products, arithmetic and copies ran while one was open for 0% -> 0% of each run, Pallas kernels for 28% -> 32%
where the time goes in v5:
time: 21.3 us; the launch traced here: 21 us
  Pallas kernels  9.65 us (45%)
  starting transfers between devices  8.09 us (38%)
  waiting for transfers between devices  1.83 us (9%)
  between operations  1.39 us (7%)
    ppermute x2, starting transfers between devices, flip(): lax.ppermute(value, 'row', [(i, i ^ row_bit) for i in range(row_count)])  5.62 us
    pallas_call x4, Pallas kernels, accumulate(): pl.pallas_call(functools.partial(sums_kernel, plan), out_shape=table_shap...  4.2 us
    ppermute x3, starting transfers between devices, flip(): lax.ppermute(value, 'blk', [(i, i ^ blk_bit) for i in range(blk_count)])  2.22 us
    pallas_call x1, Pallas kernels, body(): pl.pallas_call(functools.partial(force_kernel, force_scale, half), out_sh...  2.1 us
    pallas_call x1, Pallas kernels, body(): pl.pallas_call(functools.partial(count_kernel, wave_rows, wave_width), ou...  1.87 us
    ppermute x3, waiting for transfers between devices, flip(): lax.ppermute(value, 'blk', [(i, i ^ blk_bit) for i in range(blk_count)])  1.09 us
    pallas_call x1, Pallas kernels, body(): pl.pallas_call(prep_kernel, out_shape=jax.ShapeDtypeStruct((8, block), F3...  0.79 us
    ppermute x2, waiting for transfers between devices, flip(): lax.ppermute(value, 'row', [(i, i ^ row_bit) for i in range(row_count)])  0.53 us
  transfers between devices with their start and end apart: 6, of which 3 were waited for; matrix products, arithmetic and copies ran while one was open for 0% of the time, Pallas kernels for 32%

profile of v5, /device:TPU:0, one launch (start us, length us, event | category | flops | bytes accessed | tf_op | source)
XLA Modules:
  0.0 21.0 jit_solution(449388521283562122)
XLA Ops:
  1.3 0.8 %payload.1.refs_0_.data_ref = f32[8,512]{1,0:T(8,128)S(1)} custom-call(f32[3,768]{1,0:T(4,128)} %coords_hbm.1, f32[768]{0:T(1024)} %charges_hbm.1, s32[1]{0:T(128)S(6)} %copy.8.counts_hbm, s32[768]{0:T(1024)} %send_hbm.1), custom_call_target="tpu_custom_call" | custom-call | tf_op jit(solution)/shard_map/payload/pallas_call | solution.py:627
  2.1 4.1 %collective-permute-start = (f32[8,512]{1,0:T(8,128)S(1)}, f32[8,512]{1,0:T(8,128)S(1)}, u32[]{:S(2)}, u32[]{:S(2)}) collective-permute-start(f32[8,512]{1,0:T(8,128)S(1)} %payload.1.refs_0_.data_ref), channel_id=1, source_target_pairs={{0,2},{1,3},{2,0},{3,1},{4,6},{5,7},{6,4},{7,5},{8,10},{9,11},{10,... | collective-permute-start | bytes 49160 | tf_op jit(solution)/shard_map/exchange_ions/ppermute | solution.py:646
  6.2 1.9 %counts.1 = f32[8,3840]{1,0:T(8,128)S(1)} custom-call(s32[3,6144]{1,0:T(4,128)} %waves_hbm.1), custom_call_target="tpu_custom_call" | custom-call | flops 377487360 | bytes 1048576 | tf_op jit(solution)/shard_map/counts/pallas_call | solution.py:694
  8.0 0.0 copy-start
  8.1 0.0 collective-permute-done.refs_1_
  8.1 1.8 %collective-permute-start.3 = (f32[8,4864]{1,0:T(8,128)S(1)}, f32[8,4864]{1,0:T(8,128)S(1)}, u32[]{:S(2)}, u32[]{:S(2)}) collective-permute-start(f32[8,4864]{1,0:T(8,128)S(1)} %pad_maximum_fusion), channel_id=1, source_target_pairs={{0,8},{4,12},{8,0},{12,4},{1,9},{5,13},{9,1},{13,5},{2,10},{6,14},... | collective-permute-start | bytes 466952 | tf_op jit(solution)/shard_map/exchange_ions/ppermute | solution.py:644
  9.9 1.5 %collective-permute-start.2 = (f32[8,1024]{1,0:T(8,128)S(1)}, f32[8,1024]{1,0:T(8,128)S(1)}, u32[]{:S(2)}, u32[]{:S(2)}) collective-permute-start(f32[8,1024]{1,0:T(8,128)S(1)} %pad_maximum_fusion.1), channel_id=1, source_target_pairs={{0,1},{1,0},{2,3},{3,2},{4,5},{5,4},{6,7},{7,6},{8,9},{9,8},{10,11... | collective-permute-start | bytes 98312 | tf_op jit(solution)/shard_map/exchange_ions/ppermute | solution.py:646
  11.4 0.2 %collective-permute-start.1 = (f32[8,1024]{1,0:T(8,128)S(1)}, f32[8,1024]{1,0:T(8,128)S(1)}, u32[]{:S(2)}, u32[]{:S(2)}) collective-permute-start(f32[8,1024]{1,0:T(8,128)S(1)} %pad_maximum_fusion.1), channel_id=1, source_target_pairs={{0,9},{1,8},{2,11},{3,10},{4,13},{5,12},{6,15},{7,14},{8,1},{9,0},... | collective-permute-start | bytes 98312 | tf_op jit(solution)/shard_map/exchange_ions/ppermute | solution.py:648
  11.6 1.1 %structure_sums.4.refs_0_ = f32[576,128]{1,0:T(8,128)S(1)} custom-call(f32[8,512]{1,0:T(8,128)S(1)} %payload.1.refs_0_.data_ref, f32[8,512]{1,0:T(8,128)S(1)} %collective-permute-done.refs_1_), custom_call_target="tpu_custom_call" | custom-call | flops 566231040 | bytes 1048576 | tf_op jit(solution)/shard_map/structure_sums/pallas_call | solution.py:664
  12.7 0.0 copy-done
  12.7 0.5 %own_ions.1 = (f32[112,768]{1,0:T(8,128)S(1)}, bf16[256,1536]{1,0:T(8,128)(2,1)S(1)}, bf16[1024,512]{1,0:T(8,128)(2,1)S(1)}, f32[240,128]{1,0:T(8,128)S(1)}) custom-call(f32[8,512]{1,0:T(8,128)S(1)} %payload.1.refs_0_.data_ref, s32[512]{0:T(512)S(1)} %copy-done), custom_call_target="tpu_custom_call" | custom-call | flops 4194304 | bytes 1048576 | tf_op jit(solution)/shard_map/own_ions/pallas_call | solution.py:724
  13.3 0.5 %collective-permute-done.2.refs_1_ = f32[8,1024]{1,0:T(8,128)S(1)} collective-permute-done((f32[8,1024]{1,0:T(8,128)S(1)}, f32[8,1024]{1,0:T(8,128)S(1)}, u32[]{:S(2)}, u32[]{:S(2)}) %collective-permute-start.2) | collective-permute-done | bytes 32800 | tf_op jit(solution)/shard_map/exchange_ions/ppermute | solution.py:646
  13.8 1.0 %structure_sums.5.refs_0_ = f32[576,128]{1,0:T(8,128)S(1)} custom-call(f32[576,128]{1,0:T(8,128)S(1)} %structure_sums.4.refs_0_, f32[8,1024]{1,0:T(8,128)S(1)} %collective-permute-done.2.refs_1_), custom_call_target="tpu_custom_call" | custom-call | flops 28311552 | bytes 1048576 | tf_op jit(solution)/shard_map/structure_sums/pallas_call | solution.py:664
  14.8 0.0 collective-permute-done.3.refs_1_
  14.9 0.1 collective-permute-start.5
  15.0 1.0 %structure_sums.6.refs_0_ = f32[576,128]{1,0:T(8,128)S(1)} custom-call(f32[576,128]{1,0:T(8,128)S(1)} %structure_sums.5.refs_0_, f32[8,4864]{1,0:T(8,128)S(1)} %collective-permute-done.3.refs_1_), custom_call_target="tpu_custom_call" | custom-call | flops 28311552 | bytes 1048576 | tf_op jit(solution)/shard_map/structure_sums/pallas_call | solution.py:664
  16.0 0.2 collective-permute-done.1.refs_1_
  16.2 1.0 %structure_sums.7.mine_ref = f32[576,128]{1,0:T(8,128)S(1)} custom-call(f32[576,128]{1,0:T(8,128)S(1)} %structure_sums.6.refs_0_, f32[8,1024]{1,0:T(8,128)S(1)} %collective-permute-done.1.refs_1_), custom_call_target="tpu_custom_call" | custom-call | flops 9059696640 | bytes 1048576 | tf_op jit(solution)/shard_map/structure_sums/pallas_call | solution.py:664
  17.3 0.4 %collective-permute-start.4 = (f32[576,128]{1,0:T(8,128)S(1)}, f32[576,128]{1,0:T(8,128)S(1)}, u32[]{:S(2)}, u32[]{:S(2)}) collective-permute-start(f32[576,128]{1,0:T(8,128)S(1)} %structure_sums.7.mine_ref), channel_id=1, source_target_pairs={{0,4},{4,0},{8,12},{12,8},{1,5},{5,1},{9,13},{13,9},{2,6},{6,2},{1... | collective-permute-start | bytes 884744 | tf_op jit(solution)/shard_map/exchange_core/ppermute | solution.py:644
  17.6 0.0 collective-permute-done.5.other_count_ref
  17.6 0.2 coefficients.1.coef_ref
  17.8 1.1 %collective-permute-done.4.other_ref = f32[576,128]{1,0:T(8,128)S(1)} collective-permute-done((f32[576,128]{1,0:T(8,128)S(1)}, f32[576,128]{1,0:T(8,128)S(1)}, u32[]{:S(2)}, u32[]{:S(2)}) %collective-permute-start.4) | collective-permute-done | bytes 294944 | tf_op jit(solution)/shard_map/exchange_core/ppermute | solution.py:644
  18.9 2.1 %forces.1 = (f32[3,768]{1,0:T(4,128)}, f32[3,512]{1,0:T(4,128)}) custom-call(f32[576,128]{1,0:T(8,128)S(1)} %structure_sums.7.mine_ref, f32[576,128]{1,0:T(8,128)S(1)} %collective-permute-done.4.other_ref, f32[8,512]{1,0:T(8,128)S(1)} %payload.1.refs_0_.data_ref, f32[112,768]{1,0:T(8,128)S(1)} %get-tuple-element.33.basis_ref, ...), custom_call_target="tpu_custom_call" | custom-call | tf_op jit(solution)/shard_map/forces/pallas_call | solution.py:757
  (3 shorter events, 0.0 us)
Async XLA Ops:
  2.1 6.0 %collective-permute-start = (f32[8,512]{1,0:T(8,128)S(1)}, f32[8,512]{1,0:T(8,128)S(1)}, u32[]{:S(2)}, u32[]{:S(2)}) collective-permute-start(f32[8,512]{1,0:T(8,128)S(1)} %payload.1.refs_0_.data_ref), channel_id=1, source_target_pairs={{0,2},{1,3},{2,0},{3,1},{4,6},{5,7},{6,4},{7,5},{8,10},{9,11},{10,... | collective-permute-start | bytes 49160 | tf_op jit(solution)/shard_map/exchange_ions/ppermute | solution.py:646
  8.0 4.7 %copy-start = (s32[512]{0:T(512)S(1)}, s32[512]{0:T(512)}, u32[]{:S(2)}) copy-start(s32[512]{0:T(512)} %recv_ref) | copy-start | bytes 6148
  8.1 6.8 %collective-permute-start.3 = (f32[8,4864]{1,0:T(8,128)S(1)}, f32[8,4864]{1,0:T(8,128)S(1)}, u32[]{:S(2)}, u32[]{:S(2)}) collective-permute-start(f32[8,4864]{1,0:T(8,128)S(1)} %pad_maximum_fusion), channel_id=1, source_target_pairs={{0,8},{4,12},{8,0},{12,4},{1,9},{5,13},{9,1},{13,5},{2,10},{6,14},... | collective-permute-start | bytes 466952 | tf_op jit(solution)/shard_map/exchange_ions/ppermute | solution.py:644
  9.9 3.9 %collective-permute-start.2 = (f32[8,1024]{1,0:T(8,128)S(1)}, f32[8,1024]{1,0:T(8,128)S(1)}, u32[]{:S(2)}, u32[]{:S(2)}) collective-permute-start(f32[8,1024]{1,0:T(8,128)S(1)} %pad_maximum_fusion.1), channel_id=1, source_target_pairs={{0,1},{1,0},{2,3},{3,2},{4,5},{5,4},{6,7},{7,6},{8,9},{9,8},{10,11... | collective-permute-start | bytes 98312 | tf_op jit(solution)/shard_map/exchange_ions/ppermute | solution.py:646
  11.4 4.8 %collective-permute-start.1 = (f32[8,1024]{1,0:T(8,128)S(1)}, f32[8,1024]{1,0:T(8,128)S(1)}, u32[]{:S(2)}, u32[]{:S(2)}) collective-permute-start(f32[8,1024]{1,0:T(8,128)S(1)} %pad_maximum_fusion.1), channel_id=1, source_target_pairs={{0,9},{1,8},{2,11},{3,10},{4,13},{5,12},{6,15},{7,14},{8,1},{9,0},... | collective-permute-start | bytes 98312 | tf_op jit(solution)/shard_map/exchange_ions/ppermute | solution.py:648
  14.9 2.8 %collective-permute-start.5 = (f32[8,3840]{1,0:T(8,128)S(1)}, f32[8,3840]{1,0:T(8,128)S(1)}, u32[]{:S(2)}, u32[]{:S(2)}) collective-permute-start(f32[8,3840]{1,0:T(8,128)S(1)} %slice_add_fusion.count_ref), channel_id=1, source_target_pairs={{0,4},{4,0},{8,12},{12,8},{1,5},{5,1},{9,13},{13,9},{2,6},{6,2},{1... | collective-permute-start | bytes 368648 | tf_op jit(solution)/shard_map/exchange_core/ppermute | solution.py:644
  17.3 1.6 %collective-permute-start.4 = (f32[576,128]{1,0:T(8,128)S(1)}, f32[576,128]{1,0:T(8,128)S(1)}, u32[]{:S(2)}, u32[]{:S(2)}) collective-permute-start(f32[576,128]{1,0:T(8,128)S(1)} %structure_sums.7.mine_ref), channel_id=1, source_target_pairs={{0,4},{4,0},{8,12},{12,8},{1,5},{5,1},{9,13},{13,9},{2,6},{6,2},{1... | collective-permute-start | bytes 884744 | tf_op jit(solution)/shard_map/exchange_core/ppermute | solution.py:644

commit v6 on v5

--- a/solution.py
+++ b/solution.py
@@ -18,7 +18,7 @@
 BASIS = 24
 HARM = 40
 STEMS = (((0, 0), (3, 0), (3, 1), (6, 0), (6, 1)), ((9, 0), (9, 1), (12, 0), (12, 1)))
-SUM_ROWS = (144, 112)
+SUM_ROWS = (128, 112)
 ORDERS = (
     tuple((k, 0) for k in range(8)) + tuple((k, 1) for k in range(1, 8)),
     tuple((k, 0) for k in range(8, 13)) + tuple((k, 1) for k in range(8, 13)),
@@ -254,8 +254,11 @@
     at = 0
     for part in range(2):
         stems = stem_rows(part, basis_y)
-        rows = [stem * basis_x for stem in stems] + [charge * rows for rows in basis_y[2 * part : 2 * part + 2]]
-        fill = SUM_ROWS[part] - BASIS * len(stems) - 16
+        index = lax.broadcasted_iota(jnp.int32, (8, slots), 0)
+        sines = [index == harmonic % 8 + 1 for harmonic, sine in STEMS[part] if sine]
+        tail = jnp.where(jnp.logical_or(*sines), pltpu.roll(basis_y[2 * part + 1], 1, 0), basis_y[2 * part])
+        rows = [stem * basis_x for stem in stems] + [charge * tail]
+        fill = SUM_ROWS[part] - BASIS * len(stems) - 8
         if fill:
             rows.append(jnp.zeros((fill, slots), F32))
         rows = jnp.concatenate(rows, axis=0)
@@ -510,8 +513,8 @@
                 sums_os, turned_o, _ = groups[(harmonic, 1 - sine)]
                 value = value - coefs[2] * turned_o[x] - coefs[3] * sums_os[x]
             store(row, value)
-    tails = [blocks(BASIS * len(STEMS[part]) + 8 * sine) for sine in range(2)]
-    found = harmonics_of({(h, sine): [b[h % 8 : h % 8 + 1] for b in tails[sine]] for h, sine in STEMS[part]})
+    tail = blocks(BASIS * len(STEMS[part]))
+    found = harmonics_of({(h, sine): [b[h % 8 + sine : h % 8 + sine + 1] for b in tail] for h, sine in STEMS[part]})
     index = lax.broadcasted_iota(jnp.int32, (8, 128), 0)
     kinds = []
     for sine in range(2):

time: 21.3 us -> 21.2 us (level)
  no operation moved by 1% of the time
where the time goes in v6:
time: 21.2 us; the launch traced here: 21 us
  Pallas kernels  9.58 us (45%)
  starting transfers between devices  8.06 us (38%)
  waiting for transfers between devices  1.91 us (9%)
  between operations  1.39 us (7%)
    ppermute x2, starting transfers between devices, flip(): lax.ppermute(value, 'row', [(i, i ^ row_bit) for i in range(row_count)])  5.62 us
    pallas_call x4, Pallas kernels, accumulate(): pl.pallas_call(functools.partial(sums_kernel, plan), out_shape=table_shap...  4.11 us
    ppermute x3, starting transfers between devices, flip(): lax.ppermute(value, 'blk', [(i, i ^ blk_bit) for i in range(blk_count)])  2.19 us
    pallas_call x1, Pallas kernels, body(): pl.pallas_call(functools.partial(force_kernel, force_scale, half), out_sh...  2.11 us
    pallas_call x1, Pallas kernels, body(): pl.pallas_call(functools.partial(count_kernel, wave_rows, wave_width), ou...  1.87 us
    ppermute x3, waiting for transfers between devices, flip(): lax.ppermute(value, 'blk', [(i, i ^ blk_bit) for i in range(blk_count)])  1.1 us
    pallas_call x1, Pallas kernels, body(): pl.pallas_call(prep_kernel, out_shape=jax.ShapeDtypeStruct((8, block), F3...  0.79 us
    ppermute x2, waiting for transfers between devices, flip(): lax.ppermute(value, 'row', [(i, i ^ row_bit) for i in range(row_count)])  0.58 us
  transfers between devices with their start and end apart: 6, of which 3 were waited for; matrix products, arithmetic and copies ran while one was open for 0% of the time, Pallas kernels for 32%

profile of v6, /device:TPU:0, one launch (start us, length us, event | category | flops | bytes accessed | tf_op | source)
XLA Modules:
  0.0 21.0 jit_solution(11858432167417612480)
XLA Ops:
  1.3 0.8 %payload.1.refs_0_.data_ref = f32[8,512]{1,0:T(8,128)S(1)} custom-call(f32[3,768]{1,0:T(4,128)} %coords_hbm.1, f32[768]{0:T(1024)} %charges_hbm.1, s32[1]{0:T(128)S(6)} %copy.8.counts_hbm, s32[768]{0:T(1024)} %send_hbm.1), custom_call_target="tpu_custom_call" | custom-call | tf_op jit(solution)/shard_map/payload/pallas_call | solution.py:630
  2.1 4.1 %collective-permute-start = (f32[8,512]{1,0:T(8,128)S(1)}, f32[8,512]{1,0:T(8,128)S(1)}, u32[]{:S(2)}, u32[]{:S(2)}) collective-permute-start(f32[8,512]{1,0:T(8,128)S(1)} %payload.1.refs_0_.data_ref), channel_id=1, source_target_pairs={{0,2},{1,3},{2,0},{3,1},{4,6},{5,7},{6,4},{7,5},{8,10},{9,11},{10,... | collective-permute-start | bytes 49160 | tf_op jit(solution)/shard_map/exchange_ions/ppermute | solution.py:649
  6.2 1.9 %counts.1 = f32[8,3840]{1,0:T(8,128)S(1)} custom-call(s32[3,6144]{1,0:T(4,128)} %waves_hbm.1), custom_call_target="tpu_custom_call" | custom-call | flops 377487360 | bytes 1048576 | tf_op jit(solution)/shard_map/counts/pallas_call | solution.py:697
  8.0 0.0 copy-start
  8.1 0.0 collective-permute-done.refs_1_
  8.1 1.8 %collective-permute-start.3 = (f32[8,4864]{1,0:T(8,128)S(1)}, f32[8,4864]{1,0:T(8,128)S(1)}, u32[]{:S(2)}, u32[]{:S(2)}) collective-permute-start(f32[8,4864]{1,0:T(8,128)S(1)} %pad_maximum_fusion), channel_id=1, source_target_pairs={{0,8},{4,12},{8,0},{12,4},{1,9},{5,13},{9,1},{13,5},{2,10},{6,14},... | collective-permute-start | bytes 466952 | tf_op jit(solution)/shard_map/exchange_ions/ppermute | solution.py:647
  9.9 1.5 %collective-permute-start.2 = (f32[8,1024]{1,0:T(8,128)S(1)}, f32[8,1024]{1,0:T(8,128)S(1)}, u32[]{:S(2)}, u32[]{:S(2)}) collective-permute-start(f32[8,1024]{1,0:T(8,128)S(1)} %pad_maximum_fusion.1), channel_id=1, source_target_pairs={{0,1},{1,0},{2,3},{3,2},{4,5},{5,4},{6,7},{7,6},{8,9},{9,8},{10,11... | collective-permute-start | bytes 98312 | tf_op jit(solution)/shard_map/exchange_ions/ppermute | solution.py:649
  11.4 0.2 %collective-permute-start.1 = (f32[8,1024]{1,0:T(8,128)S(1)}, f32[8,1024]{1,0:T(8,128)S(1)}, u32[]{:S(2)}, u32[]{:S(2)}) collective-permute-start(f32[8,1024]{1,0:T(8,128)S(1)} %pad_maximum_fusion.1), channel_id=1, source_target_pairs={{0,9},{1,8},{2,11},{3,10},{4,13},{5,12},{6,15},{7,14},{8,1},{9,0},... | collective-permute-start | bytes 98312 | tf_op jit(solution)/shard_map/exchange_ions/ppermute | solution.py:651
  11.6 1.0 %structure_sums.4.refs_0_ = f32[544,128]{1,0:T(8,128)S(1)} custom-call(f32[8,512]{1,0:T(8,128)S(1)} %payload.1.refs_0_.data_ref, f32[8,512]{1,0:T(8,128)S(1)} %collective-permute-done.refs_1_), custom_call_target="tpu_custom_call" | custom-call | flops 566231040 | bytes 1048576 | tf_op jit(solution)/shard_map/structure_sums/pallas_call | solution.py:667
  12.7 0.0 copy-done
  12.7 0.5 %own_ions.1 = (f32[112,768]{1,0:T(8,128)S(1)}, bf16[256,1536]{1,0:T(8,128)(2,1)S(1)}, bf16[1024,512]{1,0:T(8,128)(2,1)S(1)}, f32[240,128]{1,0:T(8,128)S(1)}) custom-call(f32[8,512]{1,0:T(8,128)S(1)} %payload.1.refs_0_.data_ref, s32[512]{0:T(512)S(1)} %copy-done), custom_call_target="tpu_custom_call" | custom-call | flops 4194304 | bytes 1048576 | tf_op jit(solution)/shard_map/own_ions/pallas_call | solution.py:727
  13.2 0.6 %collective-permute-done.2.refs_1_ = f32[8,1024]{1,0:T(8,128)S(1)} collective-permute-done((f32[8,1024]{1,0:T(8,128)S(1)}, f32[8,1024]{1,0:T(8,128)S(1)}, u32[]{:S(2)}, u32[]{:S(2)}) %collective-permute-start.2) | collective-permute-done | bytes 32800 | tf_op jit(solution)/shard_map/exchange_ions/ppermute | solution.py:649
  13.8 1.0 %structure_sums.5.refs_0_ = f32[544,128]{1,0:T(8,128)S(1)} custom-call(f32[544,128]{1,0:T(8,128)S(1)} %structure_sums.4.refs_0_, f32[8,1024]{1,0:T(8,128)S(1)} %collective-permute-done.2.refs_1_), custom_call_target="tpu_custom_call" | custom-call | flops 28311552 | bytes 1048576 | tf_op jit(solution)/shard_map/structure_sums/pallas_call | solution.py:667
  14.8 0.0 collective-permute-done.3.refs_1_
  14.9 0.1 collective-permute-start.5
  14.9 1.0 %structure_sums.6.refs_0_ = f32[544,128]{1,0:T(8,128)S(1)} custom-call(f32[544,128]{1,0:T(8,128)S(1)} %structure_sums.5.refs_0_, f32[8,4864]{1,0:T(8,128)S(1)} %collective-permute-done.3.refs_1_), custom_call_target="tpu_custom_call" | custom-call | flops 28311552 | bytes 1048576 | tf_op jit(solution)/shard_map/structure_sums/pallas_call | solution.py:667
  16.0 0.2 %collective-permute-done.1.refs_1_ = f32[8,1024]{1,0:T(8,128)S(1)} collective-permute-done((f32[8,1024]{1,0:T(8,128)S(1)}, f32[8,1024]{1,0:T(8,128)S(1)}, u32[]{:S(2)}, u32[]{:S(2)}) %collective-permute-start.1) | collective-permute-done | bytes 32800 | tf_op jit(solution)/shard_map/exchange_ions/ppermute | solution.py:651
  16.2 1.0 %structure_sums.7.mine_ref = f32[544,128]{1,0:T(8,128)S(1)} custom-call(f32[544,128]{1,0:T(8,128)S(1)} %structure_sums.6.refs_0_, f32[8,1024]{1,0:T(8,128)S(1)} %collective-permute-done.1.refs_1_), custom_call_target="tpu_custom_call" | custom-call | flops 9059696640 | bytes 1048576 | tf_op jit(solution)/shard_map/structure_sums/pallas_call | solution.py:667
  17.2 0.3 %collective-permute-start.4 = (f32[544,128]{1,0:T(8,128)S(1)}, f32[544,128]{1,0:T(8,128)S(1)}, u32[]{:S(2)}, u32[]{:S(2)}) collective-permute-start(f32[544,128]{1,0:T(8,128)S(1)} %structure_sums.7.mine_ref), channel_id=1, source_target_pairs={{0,4},{4,0},{8,12},{12,8},{1,5},{5,1},{9,13},{13,9},{2,6},{6,2},{1... | collective-permute-start | bytes 835592 | tf_op jit(solution)/shard_map/exchange_core/ppermute | solution.py:647
  17.6 0.0 collective-permute-done.5.other_count_ref
  17.6 0.2 coefficients.1.coef_ref
  17.8 1.1 %collective-permute-done.4.other_ref = f32[544,128]{1,0:T(8,128)S(1)} collective-permute-done((f32[544,128]{1,0:T(8,128)S(1)}, f32[544,128]{1,0:T(8,128)S(1)}, u32[]{:S(2)}, u32[]{:S(2)}) %collective-permute-start.4) | collective-permute-done | bytes 278560 | tf_op jit(solution)/shard_map/exchange_core/ppermute | solution.py:647
  18.9 2.1 %forces.1 = (f32[3,768]{1,0:T(4,128)}, f32[3,512]{1,0:T(4,128)}) custom-call(f32[544,128]{1,0:T(8,128)S(1)} %structure_sums.7.mine_ref, f32[544,128]{1,0:T(8,128)S(1)} %collective-permute-done.4.other_ref, f32[8,512]{1,0:T(8,128)S(1)} %payload.1.refs_0_.data_ref, f32[112,768]{1,0:T(8,128)S(1)} %get-tuple-element.33.basis_ref, ...), custom_call_target="tpu_custom_call" | custom-call | tf_op jit(solution)/shard_map/forces/pallas_call | solution.py:760
  (3 shorter events, 0.0 us)
Async XLA Ops:
  2.1 6.0 %collective-permute-start = (f32[8,512]{1,0:T(8,128)S(1)}, f32[8,512]{1,0:T(8,128)S(1)}, u32[]{:S(2)}, u32[]{:S(2)}) collective-permute-start(f32[8,512]{1,0:T(8,128)S(1)} %payload.1.refs_0_.data_ref), channel_id=1, source_target_pairs={{0,2},{1,3},{2,0},{3,1},{4,6},{5,7},{6,4},{7,5},{8,10},{9,11},{10,... | collective-permute-start | bytes 49160 | tf_op jit(solution)/shard_map/exchange_ions/ppermute | solution.py:649
  8.0 4.6 %copy-start = (s32[512]{0:T(512)S(1)}, s32[512]{0:T(512)}, u32[]{:S(2)}) copy-start(s32[512]{0:T(512)} %recv_ref) | copy-start | bytes 6148
  8.1 6.7 %collective-permute-start.3 = (f32[8,4864]{1,0:T(8,128)S(1)}, f32[8,4864]{1,0:T(8,128)S(1)}, u32[]{:S(2)}, u32[]{:S(2)}) collective-permute-start(f32[8,4864]{1,0:T(8,128)S(1)} %pad_maximum_fusion), channel_id=1, source_target_pairs={{0,8},{4,12},{8,0},{12,4},{1,9},{5,13},{9,1},{13,5},{2,10},{6,14},... | collective-permute-start | bytes 466952 | tf_op jit(solution)/shard_map/exchange_ions/ppermute | solution.py:647
  9.9 3.9 %collective-permute-start.2 = (f32[8,1024]{1,0:T(8,128)S(1)}, f32[8,1024]{1,0:T(8,128)S(1)}, u32[]{:S(2)}, u32[]{:S(2)}) collective-permute-start(f32[8,1024]{1,0:T(8,128)S(1)} %pad_maximum_fusion.1), channel_id=1, source_target_pairs={{0,1},{1,0},{2,3},{3,2},{4,5},{5,4},{6,7},{7,6},{8,9},{9,8},{10,11... | collective-permute-start | bytes 98312 | tf_op jit(solution)/shard_map/exchange_ions/ppermute | solution.py:649
  11.4 4.8 %collective-permute-start.1 = (f32[8,1024]{1,0:T(8,128)S(1)}, f32[8,1024]{1,0:T(8,128)S(1)}, u32[]{:S(2)}, u32[]{:S(2)}) collective-permute-start(f32[8,1024]{1,0:T(8,128)S(1)} %pad_maximum_fusion.1), channel_id=1, source_target_pairs={{0,9},{1,8},{2,11},{3,10},{4,13},{5,12},{6,15},{7,14},{8,1},{9,0},... | collective-permute-start | bytes 98312 | tf_op jit(solution)/shard_map/exchange_ions/ppermute | solution.py:651
  14.9 2.7 %collective-permute-start.5 = (f32[8,3840]{1,0:T(8,128)S(1)}, f32[8,3840]{1,0:T(8,128)S(1)}, u32[]{:S(2)}, u32[]{:S(2)}) collective-permute-start(f32[8,3840]{1,0:T(8,128)S(1)} %slice_add_fusion.count_ref), channel_id=1, source_target_pairs={{0,4},{4,0},{8,12},{12,8},{1,5},{5,1},{9,13},{13,9},{2,6},{6,2},{1... | collective-permute-start | bytes 368648 | tf_op jit(solution)/shard_map/exchange_core/ppermute | solution.py:647
  17.2 1.6 %collective-permute-start.4 = (f32[544,128]{1,0:T(8,128)S(1)}, f32[544,128]{1,0:T(8,128)S(1)}, u32[]{:S(2)}, u32[]{:S(2)}) collective-permute-start(f32[544,128]{1,0:T(8,128)S(1)} %structure_sums.7.mine_ref), channel_id=1, source_target_pairs={{0,4},{4,0},{8,12},{12,8},{1,5},{5,1},{9,13},{13,9},{2,6},{6,2},{1... | collective-permute-start | bytes 835592 | tf_op jit(solution)/shard_map/exchange_core/ppermute | solution.py:647

commit v7 on v5

--- a/solution.py
+++ b/solution.py
@@ -407,15 +407,16 @@
     return [parts[1], parts[0], pltpu.roll(parts[2], 4, 0)]
 
 
-def store_coefs(part, gain_ref, count_refs, coef_ref):
+def store_coefs(part, core, gain_ref, count_refs, coef_ref):
     lane = lax.broadcasted_iota(jnp.int32, (8, 128), 1)
     is_cos = lane < HARM
     is_wave = lane < 2 * HARM
 
     def gains(row):
         at = COUNT_AT[part] + row
-        lanes = slice(16 * at, 16 * at + 128)
-        tile = (count_refs[0][:, lanes] + count_refs[1][:, lanes]) * gain_ref[at : at + 8]
+        half = 2 * at // COUNT_ROWS
+        lanes = slice(16 * at - 8 * COUNT_ROWS * half, 16 * at - 8 * COUNT_ROWS * half + 128)
+        tile = jnp.where(core == half, count_refs[0][:, lanes], count_refs[1][:, lanes]) * gain_ref[at : at + 8]
         back, far = pltpu.roll(tile, 88, 1), pltpu.roll(tile, 48, 1)
         pairs = ((tile, pltpu.roll(tile, HARM, 1)), (back, tile), (far, back))
         return [jnp.where(is_cos, a, jnp.where(is_wave, b, 0.0)) for a, b in pairs]
@@ -445,8 +446,9 @@
 
 
 def coef_kernel(gain_ref, count_ref, other_count_ref, coef_ref):
+    core = lax.axis_index("blk") % 2
     for part in range(2):
-        store_coefs(part, gain_ref, (count_ref, other_count_ref), coef_ref)
+        store_coefs(part, core, gain_ref, (count_ref, other_count_ref), coef_ref)
 
 
 def weighted_sums(part, mine_ref, other_ref, coef_ref, w_ref):
@@ -713,12 +715,26 @@
         chunks = chunks + [(got, held, held)]
         ions = ions + [got]
         held *= 2
+    low = lax.axis_index("blk") % 2 == 0
+    halves = counted[:, : 8 * COUNT_ROWS], counted[:, 8 * COUNT_ROWS :]
+    with jax.named_scope("exchange_counts"):
+        near = flip(jnp.where(low, halves[1], halves[0]), 1, 0)
+        counted = jnp.where(low, halves[0], halves[1]) + near
     with jax.named_scope("exchange_ions"):
         sent = joined(ions)
+        corner = flip(sent, 2, 1)
+        along = flip(sent, 0, 1)
         across = flip(jnp.concatenate([sent, counted], axis=1), 2, 0)
-        along = flip(sent, 0, 1)
-        corner = flip(sent, 2, 1)
-    table = accumulate(table, chunks)
+    table = accumulate(table, chunks, cost=8)
+    table = accumulate(table, [(corner, held, 3 * held)], cost=0.3)
+    table = accumulate(table, [(along, held, 2 * held)], cost=0.3)
+    with jax.named_scope("exchange_core"):
+        counted = counted + across[:, held * block :]
+        other_counted = flip(counted, 1, 0)
+    across, table, counted = lax.optimization_barrier((across, table, counted))
+    table = accumulate(table, [(across, held, held)], cost=1)
+    with jax.named_scope("exchange_core"):
+        other = flip(table, 1, 0)
     own_ions, recv_index, table = lax.optimization_barrier((own_ions, recv_index, table))
     with jax.named_scope("own_ions"):
         basis, table_z, hot, gain = pl.pallas_call(
@@ -732,18 +748,8 @@
             in_specs=whole(2),
             out_specs=tuple(whole(4)),
             compiler_params=params(),
-            cost_estimate=pl.CostEstimate(flops=1<<22, bytes_accessed=1 << 20, transcendentals=0),
+            cost_estimate=pl.CostEstimate(flops=1<<33, bytes_accessed=1 << 20, transcendentals=0),
         )(own_ions, recv_index)
-    along, table, basis, table_z, hot, gain = lax.optimization_barrier((along, table, basis, table_z, hot, gain))
-    table = accumulate(table, [(along, held, 2 * held)], cost=0.05)
-    table = accumulate(table, [(across, held, held)], cost=0.05)
-    with jax.named_scope("exchange_core"):
-        counted = counted + across[:, held * block :]
-        other_counted = flip(counted, 1, 0)
-    corner, table, counted = lax.optimization_barrier((corner, table, counted))
-    table = accumulate(table, [(corner, held, 3 * held)], cost=16)
-    with jax.named_scope("exchange_core"):
-        other = flip(table, 1, 0)
     with jax.named_scope("coefficients"):
         coefs = pl.pallas_call(
             coef_kernel,

time: 21.3 us -> 21.4 us (level)
  starting transfers between devices: 8.09 us -> 8.42 us
  waiting for transfers between devices: 1.83 us -> 1.55 us
    ppermute x1, starting transfers between devices: 0.25 us -> 2.74 us  [flip(): lax.ppermute(value, ('blk', 'row'), [(i, i ^ distance) for i in range(dev...]
    ppermute x3 -> x4, starting transfers between devices: 2.22 us -> 1.07 us  [flip(): lax.ppermute(value, 'blk', [(i, i ^ blk_bit) for i in range(blk_count)])]
    ppermute x2, starting transfers between devices: 5.62 us -> 4.6 us  [flip(): lax.ppermute(value, 'row', [(i, i ^ row_bit) for i in range(row_count)])]
    ppermute x3 -> x4, waiting for transfers between devices: 1.09 us -> 0.69 us  [flip(): lax.ppermute(value, 'blk', [(i, i ^ blk_bit) for i in range(blk_count)])]
  transfers between devices with their start and end apart: 6 -> 7, of which waited for: 3 -> 4; matrix products, arithmetic and copies ran while one was open for 0% -> 0% of each run, Pallas kernels for 32% -> 32%
where the time goes in v7:
time: 21.4 us; the launch traced here: 21.1 us
  Pallas kernels  9.66 us (45%)
  starting transfers between devices  8.42 us (39%)
  waiting for transfers between devices  1.55 us (7%)
  between operations  1.42 us (7%)
    ppermute x2, starting transfers between devices, flip(): lax.ppermute(value, 'row', [(i, i ^ row_bit) for i in range(row_count)])  4.6 us
    pallas_call x4, Pallas kernels, accumulate(): pl.pallas_call(functools.partial(sums_kernel, plan), out_shape=table_shap...  4.2 us
    ppermute x1, starting transfers between devices, flip(): lax.ppermute(value, ('blk', 'row'), [(i, i ^ distance) for i in range(dev...  2.74 us
    pallas_call x1, Pallas kernels, body(): pl.pallas_call(functools.partial(force_kernel, force_scale, half), out_sh...  2.09 us
    pallas_call x1, Pallas kernels, body(): pl.pallas_call(functools.partial(count_kernel, wave_rows, wave_width), ou...  1.87 us
    ppermute x4, starting transfers between devices, flip(): lax.ppermute(value, 'blk', [(i, i ^ blk_bit) for i in range(blk_count)])  1.07 us
    pallas_call x1, Pallas kernels, body(): pl.pallas_call(prep_kernel, out_shape=jax.ShapeDtypeStruct((8, block), F3...  0.79 us
    ppermute x2, waiting for transfers between devices, flip(): lax.ppermute(value, 'row', [(i, i ^ row_bit) for i in range(row_count)])  0.72 us
  transfers between devices with their start and end apart: 7, of which 4 were waited for; matrix products, arithmetic and copies ran while one was open for 0% of the time, Pallas kernels for 32%

profile of v7, /device:TPU:0, one launch (start us, length us, event | category | flops | bytes accessed | tf_op | source)
XLA Modules:
  0.0 21.1 jit_solution(11952477721944748716)
XLA Ops:
  1.3 0.8 %payload.1.refs_0_.data_ref = f32[8,512]{1,0:T(8,128)S(1)} custom-call(f32[3,768]{1,0:T(4,128)} %coords_hbm.1, f32[768]{0:T(1024)} %charges_hbm.1, s32[1]{0:T(128)S(6)} %copy.8.counts_hbm, s32[768]{0:T(1024)} %send_hbm.1), custom_call_target="tpu_custom_call" | custom-call | tf_op jit(solution)/shard_map/payload/pallas_call | solution.py:629
  2.1 4.1 %collective-permute-start = (f32[8,512]{1,0:T(8,128)S(1)}, f32[8,512]{1,0:T(8,128)S(1)}, u32[]{:S(2)}, u32[]{:S(2)}) collective-permute-start(f32[8,512]{1,0:T(8,128)S(1)} %payload.1.refs_0_.data_ref), channel_id=1, source_target_pairs={{0,2},{1,3},{2,0},{3,1},{4,6},{5,7},{6,4},{7,5},{8,10},{9,11},{10,... | collective-permute-start | bytes 49160 | tf_op jit(solution)/shard_map/exchange_ions/ppermute | solution.py:648
  6.2 1.9 %counts.1 = f32[8,3840]{1,0:T(8,128)S(1)} custom-call(s32[3,6144]{1,0:T(4,128)} %waves_hbm.1), custom_call_target="tpu_custom_call" | custom-call | flops 377487360 | bytes 1048576 | tf_op jit(solution)/shard_map/counts/pallas_call | solution.py:696
  8.1 0.0 collective-permute-done.refs_1_
  8.1 0.1 collective-permute-start.1
  8.2 2.7 %collective-permute-start.3 = (f32[8,1024]{1,0:T(8,128)S(1)}, f32[8,1024]{1,0:T(8,128)S(1)}, u32[]{:S(2)}, u32[]{:S(2)}) collective-permute-start(f32[8,1024]{1,0:T(8,128)S(1)} %pad_maximum_fusion.1), channel_id=1, source_target_pairs={{0,9},{1,8},{2,11},{3,10},{4,13},{5,12},{6,15},{7,14},{8,1},{9,0},... | collective-permute-start | bytes 98312 | tf_op jit(solution)/shard_map/exchange_ions/ppermute | solution.py:650
  10.9 0.5 %collective-permute-start.4 = (f32[8,1024]{1,0:T(8,128)S(1)}, f32[8,1024]{1,0:T(8,128)S(1)}, u32[]{:S(2)}, u32[]{:S(2)}) collective-permute-start(f32[8,1024]{1,0:T(8,128)S(1)} %pad_maximum_fusion.1), channel_id=1, source_target_pairs={{0,1},{1,0},{2,3},{3,2},{4,5},{5,4},{6,7},{7,6},{8,9},{9,8},{10,11... | collective-permute-start | bytes 98312 | tf_op jit(solution)/shard_map/exchange_ions/ppermute | solution.py:648
  11.4 0.0 collective-permute-done.1
  11.5 0.4 %collective-permute-start.2 = (f32[8,2944]{1,0:T(8,128)S(1)}, f32[8,2944]{1,0:T(8,128)S(1)}, u32[]{:S(2)}, u32[]{:S(2)}) collective-permute-start(f32[8,2944]{1,0:T(8,128)S(1)} %pad_maximum_fusion), channel_id=1, source_target_pairs={{0,8},{4,12},{8,0},{12,4},{1,9},{5,13},{9,1},{13,5},{2,10},{6,14},... | collective-permute-start | bytes 282632 | tf_op jit(solution)/shard_map/exchange_ions/ppermute | solution.py:646
  11.8 1.1 %structure_sums.4.refs_0_ = f32[576,128]{1,0:T(8,128)S(1)} custom-call(f32[8,512]{1,0:T(8,128)S(1)} %payload.1.refs_0_.data_ref, f32[8,512]{1,0:T(8,128)S(1)} %collective-permute-done.refs_1_), custom_call_target="tpu_custom_call" | custom-call | flops 4529848320 | bytes 1048576 | tf_op jit(solution)/shard_map/structure_sums/pallas_call | solution.py:666
  12.9 0.1 collective-permute-done.3.refs_1_
  13.1 1.0 %structure_sums.5.refs_0_ = f32[576,128]{1,0:T(8,128)S(1)} custom-call(f32[576,128]{1,0:T(8,128)S(1)} %structure_sums.4.refs_0_, f32[8,1024]{1,0:T(8,128)S(1)} %collective-permute-done.3.refs_1_), custom_call_target="tpu_custom_call" | custom-call | flops 169869312 | bytes 1048576 | tf_op jit(solution)/shard_map/structure_sums/pallas_call | solution.py:666
  14.1 0.0 copy-start
  14.1 0.7 %collective-permute-done.4.refs_1_ = f32[8,1024]{1,0:T(8,128)S(1)} collective-permute-done((f32[8,1024]{1,0:T(8,128)S(1)}, f32[8,1024]{1,0:T(8,128)S(1)}, u32[]{:S(2)}, u32[]{:S(2)}) %collective-permute-start.4) | collective-permute-done | bytes 32800 | tf_op jit(solution)/shard_map/exchange_ions/ppermute | solution.py:648
  14.8 1.0 %structure_sums.6.refs_0_ = f32[576,128]{1,0:T(8,128)S(1)} custom-call(f32[576,128]{1,0:T(8,128)S(1)} %structure_sums.5.refs_0_, f32[8,1024]{1,0:T(8,128)S(1)} %collective-permute-done.4.refs_1_), custom_call_target="tpu_custom_call" | custom-call | flops 169869312 | bytes 1048576 | tf_op jit(solution)/shard_map/structure_sums/pallas_call | solution.py:666
  15.9 0.2 %collective-permute-done.2.refs_1_ = f32[8,2944]{1,0:T(8,128)S(1)} collective-permute-done((f32[8,2944]{1,0:T(8,128)S(1)}, f32[8,2944]{1,0:T(8,128)S(1)}, u32[]{:S(2)}, u32[]{:S(2)}) %collective-permute-start.2) | collective-permute-done | bytes 94240 | tf_op jit(solution)/shard_map/exchange_ions/ppermute | solution.py:646
  16.1 0.1 collective-permute-start.6
  16.2 1.0 %structure_sums.7.mine_ref = f32[576,128]{1,0:T(8,128)S(1)} custom-call(f32[576,128]{1,0:T(8,128)S(1)} %structure_sums.6.refs_0_, f32[8,2944]{1,0:T(8,128)S(1)} %collective-permute-done.2.refs_1_), custom_call_target="tpu_custom_call" | custom-call | flops 566231040 | bytes 1048576 | tf_op jit(solution)/shard_map/structure_sums/pallas_call | solution.py:666
  17.2 0.6 %collective-permute-start.5 = (f32[576,128]{1,0:T(8,128)S(1)}, f32[576,128]{1,0:T(8,128)S(1)}, u32[]{:S(2)}, u32[]{:S(2)}) collective-permute-start(f32[576,128]{1,0:T(8,128)S(1)} %structure_sums.7.mine_ref), channel_id=1, source_target_pairs={{0,4},{4,0},{8,12},{12,8},{1,5},{5,1},{9,13},{13,9},{2,6},{6,2},{1... | collective-permute-start | bytes 884744 | tf_op jit(solution)/shard_map/exchange_core/ppermute | solution.py:646
  17.8 0.0 copy-done
  17.8 0.5 %own_ions.1 = (f32[112,768]{1,0:T(8,128)S(1)}, bf16[256,1536]{1,0:T(8,128)(2,1)S(1)}, bf16[1024,512]{1,0:T(8,128)(2,1)S(1)}, f32[240,128]{1,0:T(8,128)S(1)}) custom-call(f32[8,512]{1,0:T(8,128)S(1)} %payload.1.refs_0_.data_ref, s32[512]{0:T(512)S(1)} %copy-done), custom_call_target="tpu_custom_call" | custom-call | flops 8589934592 | bytes 1048576 | tf_op jit(solution)/shard_map/own_ions/pallas_call | solution.py:740
  18.3 0.0 collective-permute-done.6.other_count_ref
  18.3 0.2 coefficients.1.coef_ref
  18.5 0.5 %collective-permute-done.5.other_ref = f32[576,128]{1,0:T(8,128)S(1)} collective-permute-done((f32[576,128]{1,0:T(8,128)S(1)}, f32[576,128]{1,0:T(8,128)S(1)}, u32[]{:S(2)}, u32[]{:S(2)}) %collective-permute-start.5) | collective-permute-done | bytes 294944 | tf_op jit(solution)/shard_map/exchange_core/ppermute | solution.py:646
  19.0 2.1 %forces.1 = (f32[3,768]{1,0:T(4,128)}, f32[3,512]{1,0:T(4,128)}) custom-call(f32[576,128]{1,0:T(8,128)S(1)} %structure_sums.7.mine_ref, f32[576,128]{1,0:T(8,128)S(1)} %collective-permute-done.5.other_ref, f32[8,512]{1,0:T(8,128)S(1)} %payload.1.refs_0_.data_ref, f32[112,768]{1,0:T(8,128)S(1)} %get-tuple-element.21.basis_ref, ...), custom_call_target="tpu_custom_call" | custom-call | tf_op jit(solution)/shard_map/forces/pallas_call | solution.py:763
  (5 shorter events, 0.0 us)
Async XLA Ops:
  2.1 6.0 %collective-permute-start = (f32[8,512]{1,0:T(8,128)S(1)}, f32[8,512]{1,0:T(8,128)S(1)}, u32[]{:S(2)}, u32[]{:S(2)}) collective-permute-start(f32[8,512]{1,0:T(8,128)S(1)} %payload.1.refs_0_.data_ref), channel_id=1, source_target_pairs={{0,2},{1,3},{2,0},{3,1},{4,6},{5,7},{6,4},{7,5},{8,10},{9,11},{10,... | collective-permute-start | bytes 49160 | tf_op jit(solution)/shard_map/exchange_ions/ppermute | solution.py:648
  8.1 3.3 %collective-permute-start.1 = (f32[8,1920]{1,0:T(8,128)S(1)}, f32[8,1920]{1,0:T(8,128)S(1)}, u32[]{:S(2)}, u32[]{:S(2)}) collective-permute-start(f32[8,1920]{1,0:T(8,128)S(1)} %slice_select_fusion), channel_id=1, source_target_pairs={{0,4},{4,0},{8,12},{12,8},{1,5},{5,1},{9,13},{13,9},{2,6},{6,2},{1... | collective-permute-start | bytes 184328 | tf_op jit(solution)/shard_map/exchange_counts/ppermute | solution.py:646
  8.2 4.9 %collective-permute-start.3 = (f32[8,1024]{1,0:T(8,128)S(1)}, f32[8,1024]{1,0:T(8,128)S(1)}, u32[]{:S(2)}, u32[]{:S(2)}) collective-permute-start(f32[8,1024]{1,0:T(8,128)S(1)} %pad_maximum_fusion.1), channel_id=1, source_target_pairs={{0,9},{1,8},{2,11},{3,10},{4,13},{5,12},{6,15},{7,14},{8,1},{9,0},... | collective-permute-start | bytes 98312 | tf_op jit(solution)/shard_map/exchange_ions/ppermute | solution.py:650
  10.9 3.9 %collective-permute-start.4 = (f32[8,1024]{1,0:T(8,128)S(1)}, f32[8,1024]{1,0:T(8,128)S(1)}, u32[]{:S(2)}, u32[]{:S(2)}) collective-permute-start(f32[8,1024]{1,0:T(8,128)S(1)} %pad_maximum_fusion.1), channel_id=1, source_target_pairs={{0,1},{1,0},{2,3},{3,2},{4,5},{5,4},{6,7},{7,6},{8,9},{9,8},{10,11... | collective-permute-start | bytes 98312 | tf_op jit(solution)/shard_map/exchange_ions/ppermute | solution.py:648
  11.5 4.6 %collective-permute-start.2 = (f32[8,2944]{1,0:T(8,128)S(1)}, f32[8,2944]{1,0:T(8,128)S(1)}, u32[]{:S(2)}, u32[]{:S(2)}) collective-permute-start(f32[8,2944]{1,0:T(8,128)S(1)} %pad_maximum_fusion), channel_id=1, source_target_pairs={{0,8},{4,12},{8,0},{12,4},{1,9},{5,13},{9,1},{13,5},{2,10},{6,14},... | collective-permute-start | bytes 282632 | tf_op jit(solution)/shard_map/exchange_ions/ppermute | solution.py:646
  14.1 3.7 %copy-start = (s32[512]{0:T(512)S(1)}, s32[512]{0:T(512)}, u32[]{:S(2)}) copy-start(s32[512]{0:T(512)} %recv_ref) | copy-start | bytes 6148
  16.1 2.2 %collective-permute-start.6 = (f32[8,1920]{1,0:T(8,128)S(1)}, f32[8,1920]{1,0:T(8,128)S(1)}, u32[]{:S(2)}, u32[]{:S(2)}) collective-permute-start(f32[8,1920]{1,0:T(8,128)S(1)} %slice_add_fusion.count_ref), channel_id=1, source_target_pairs={{0,4},{4,0},{8,12},{12,8},{1,5},{5,1},{9,13},{13,9},{2,6},{6,2},{1... | collective-permute-start | bytes 184328 | tf_op jit(solution)/shard_map/exchange_core/ppermute | solution.py:646
  17.2 1.8 %collective-permute-start.5 = (f32[576,128]{1,0:T(8,128)S(1)}, f32[576,128]{1,0:T(8,128)S(1)}, u32[]{:S(2)}, u32[]{:S(2)}) collective-permute-start(f32[576,128]{1,0:T(8,128)S(1)} %structure_sums.7.mine_ref), channel_id=1, source_target_pairs={{0,4},{4,0},{8,12},{12,8},{1,5},{5,1},{9,13},{13,9},{2,6},{6,2},{1... | collective-permute-start | bytes 884744 | tf_op jit(solution)/shard_map/exchange_core/ppermute | solution.py:646

commit v8 on v7

--- a/solution.py
+++ b/solution.py
@@ -18,7 +18,7 @@
 BASIS = 24
 HARM = 40
 STEMS = (((0, 0), (3, 0), (3, 1), (6, 0), (6, 1)), ((9, 0), (9, 1), (12, 0), (12, 1)))
-SUM_ROWS = (144, 112)
+SUM_ROWS = (128, 112)
 ORDERS = (
     tuple((k, 0) for k in range(8)) + tuple((k, 1) for k in range(1, 8)),
     tuple((k, 0) for k in range(8, 13)) + tuple((k, 1) for k in range(8, 13)),
@@ -254,8 +254,11 @@
     at = 0
     for part in range(2):
         stems = stem_rows(part, basis_y)
-        rows = [stem * basis_x for stem in stems] + [charge * rows for rows in basis_y[2 * part : 2 * part + 2]]
-        fill = SUM_ROWS[part] - BASIS * len(stems) - 16
+        index = lax.broadcasted_iota(jnp.int32, (8, slots), 0)
+        sines = [index == harmonic % 8 + 1 for harmonic, sine in STEMS[part] if sine]
+        tail = jnp.where(jnp.logical_or(*sines), pltpu.roll(basis_y[2 * part + 1], 1, 0), basis_y[2 * part])
+        rows = [stem * basis_x for stem in stems] + [charge * tail]
+        fill = SUM_ROWS[part] - BASIS * len(stems) - 8
         if fill:
             rows.append(jnp.zeros((fill, slots), F32))
         rows = jnp.concatenate(rows, axis=0)
@@ -512,8 +515,8 @@
                 sums_os, turned_o, _ = groups[(harmonic, 1 - sine)]
                 value = value - coefs[2] * turned_o[x] - coefs[3] * sums_os[x]
             store(row, value)
-    tails = [blocks(BASIS * len(STEMS[part]) + 8 * sine) for sine in range(2)]
-    found = harmonics_of({(h, sine): [b[h % 8 : h % 8 + 1] for b in tails[sine]] for h, sine in STEMS[part]})
+    tail = blocks(BASIS * len(STEMS[part]))
+    found = harmonics_of({(h, sine): [b[h % 8 + sine : h % 8 + sine + 1] for b in tail] for h, sine in STEMS[part]})
     index = lax.broadcasted_iota(jnp.int32, (8, 128), 0)
     kinds = []
     for sine in range(2):

time: 21.4 us -> 21.3 us (level)
  no operation moved by 1% of the time
where the time goes in v8:
time: 21.3 us; the launch traced here: 21.1 us
  Pallas kernels  9.56 us (45%)
  starting transfers between devices  8.42 us (40%)
  waiting for transfers between devices  1.61 us (8%)
  between operations  1.42 us (7%)
    ppermute x2, starting transfers between devices, flip(): lax.ppermute(value, 'row', [(i, i ^ row_bit) for i in range(row_count)])  4.6 us
    pallas_call x4, Pallas kernels, accumulate(): pl.pallas_call(functools.partial(sums_kernel, plan), out_shape=table_shap...  4.1 us
    ppermute x1, starting transfers between devices, flip(): lax.ppermute(value, ('blk', 'row'), [(i, i ^ distance) for i in range(dev...  2.74 us
    pallas_call x1, Pallas kernels, body(): pl.pallas_call(functools.partial(force_kernel, force_scale, half), out_sh...  2.09 us
    pallas_call x1, Pallas kernels, body(): pl.pallas_call(functools.partial(count_kernel, wave_rows, wave_width), ou...  1.87 us
    ppermute x4, starting transfers between devices, flip(): lax.ppermute(value, 'blk', [(i, i ^ blk_bit) for i in range(blk_count)])  1.07 us
    pallas_call x1, Pallas kernels, body(): pl.pallas_call(prep_kernel, out_shape=jax.ShapeDtypeStruct((8, block), F3...  0.79 us
    ppermute x2, waiting for transfers between devices, flip(): lax.ppermute(value, 'row', [(i, i ^ row_bit) for i in range(row_count)])  0.74 us
  transfers between devices with their start and end apart: 7, of which 4 were waited for; matrix products, arithmetic and copies ran while one was open for 0% of the time, Pallas kernels for 32%

profile of v8, /device:TPU:0, one launch (start us, length us, event | category | flops | bytes accessed | tf_op | source)
XLA Modules:
  0.0 21.1 jit_solution(16076845671280765132)
XLA Ops:
  1.3 0.8 %payload.1.refs_0_.data_ref = f32[8,512]{1,0:T(8,128)S(1)} custom-call(f32[3,768]{1,0:T(4,128)} %coords_hbm.1, f32[768]{0:T(1024)} %charges_hbm.1, s32[1]{0:T(128)S(6)} %copy.8.counts_hbm, s32[768]{0:T(1024)} %send_hbm.1), custom_call_target="tpu_custom_call" | custom-call | tf_op jit(solution)/shard_map/payload/pallas_call | solution.py:632
  2.1 4.1 %collective-permute-start = (f32[8,512]{1,0:T(8,128)S(1)}, f32[8,512]{1,0:T(8,128)S(1)}, u32[]{:S(2)}, u32[]{:S(2)}) collective-permute-start(f32[8,512]{1,0:T(8,128)S(1)} %payload.1.refs_0_.data_ref), channel_id=1, source_target_pairs={{0,2},{1,3},{2,0},{3,1},{4,6},{5,7},{6,4},{7,5},{8,10},{9,11},{10,... | collective-permute-start | bytes 49160 | tf_op jit(solution)/shard_map/exchange_ions/ppermute | solution.py:651
  6.2 1.9 %counts.1 = f32[8,3840]{1,0:T(8,128)S(1)} custom-call(s32[3,6144]{1,0:T(4,128)} %waves_hbm.1), custom_call_target="tpu_custom_call" | custom-call | flops 377487360 | bytes 1048576 | tf_op jit(solution)/shard_map/counts/pallas_call | solution.py:699
  8.1 0.0 collective-permute-done.refs_1_
  8.1 0.1 collective-permute-start.1
  8.2 2.7 %collective-permute-start.3 = (f32[8,1024]{1,0:T(8,128)S(1)}, f32[8,1024]{1,0:T(8,128)S(1)}, u32[]{:S(2)}, u32[]{:S(2)}) collective-permute-start(f32[8,1024]{1,0:T(8,128)S(1)} %pad_maximum_fusion.1), channel_id=1, source_target_pairs={{0,9},{1,8},{2,11},{3,10},{4,13},{5,12},{6,15},{7,14},{8,1},{9,0},... | collective-permute-start | bytes 98312 | tf_op jit(solution)/shard_map/exchange_ions/ppermute | solution.py:653
  10.9 0.5 %collective-permute-start.4 = (f32[8,1024]{1,0:T(8,128)S(1)}, f32[8,1024]{1,0:T(8,128)S(1)}, u32[]{:S(2)}, u32[]{:S(2)}) collective-permute-start(f32[8,1024]{1,0:T(8,128)S(1)} %pad_maximum_fusion.1), channel_id=1, source_target_pairs={{0,1},{1,0},{2,3},{3,2},{4,5},{5,4},{6,7},{7,6},{8,9},{9,8},{10,11... | collective-permute-start | bytes 98312 | tf_op jit(solution)/shard_map/exchange_ions/ppermute | solution.py:651
  11.4 0.0 collective-permute-done.1
  11.5 0.4 %collective-permute-start.2 = (f32[8,2944]{1,0:T(8,128)S(1)}, f32[8,2944]{1,0:T(8,128)S(1)}, u32[]{:S(2)}, u32[]{:S(2)}) collective-permute-start(f32[8,2944]{1,0:T(8,128)S(1)} %pad_maximum_fusion), channel_id=1, source_target_pairs={{0,8},{4,12},{8,0},{12,4},{1,9},{5,13},{9,1},{13,5},{2,10},{6,14},... | collective-permute-start | bytes 282632 | tf_op jit(solution)/shard_map/exchange_ions/ppermute | solution.py:649
  11.8 1.0 %structure_sums.4.refs_0_ = f32[544,128]{1,0:T(8,128)S(1)} custom-call(f32[8,512]{1,0:T(8,128)S(1)} %payload.1.refs_0_.data_ref, f32[8,512]{1,0:T(8,128)S(1)} %collective-permute-done.refs_1_), custom_call_target="tpu_custom_call" | custom-call | flops 4529848320 | bytes 1048576 | tf_op jit(solution)/shard_map/structure_sums/pallas_call | solution.py:669
  12.9 0.2 collective-permute-done.3.refs_1_
  13.1 1.0 %structure_sums.5.refs_0_ = f32[544,128]{1,0:T(8,128)S(1)} custom-call(f32[544,128]{1,0:T(8,128)S(1)} %structure_sums.4.refs_0_, f32[8,1024]{1,0:T(8,128)S(1)} %collective-permute-done.3.refs_1_), custom_call_target="tpu_custom_call" | custom-call | flops 169869312 | bytes 1048576 | tf_op jit(solution)/shard_map/structure_sums/pallas_call | solution.py:669
  14.1 0.0 copy-start
  14.1 0.7 %collective-permute-done.4.refs_1_ = f32[8,1024]{1,0:T(8,128)S(1)} collective-permute-done((f32[8,1024]{1,0:T(8,128)S(1)}, f32[8,1024]{1,0:T(8,128)S(1)}, u32[]{:S(2)}, u32[]{:S(2)}) %collective-permute-start.4) | collective-permute-done | bytes 32800 | tf_op jit(solution)/shard_map/exchange_ions/ppermute | solution.py:651
  14.8 1.0 %structure_sums.6.refs_0_ = f32[544,128]{1,0:T(8,128)S(1)} custom-call(f32[544,128]{1,0:T(8,128)S(1)} %structure_sums.5.refs_0_, f32[8,1024]{1,0:T(8,128)S(1)} %collective-permute-done.4.refs_1_), custom_call_target="tpu_custom_call" | custom-call | flops 169869312 | bytes 1048576 | tf_op jit(solution)/shard_map/structure_sums/pallas_call | solution.py:669
  15.9 0.2 %collective-permute-done.2.refs_1_ = f32[8,2944]{1,0:T(8,128)S(1)} collective-permute-done((f32[8,2944]{1,0:T(8,128)S(1)}, f32[8,2944]{1,0:T(8,128)S(1)}, u32[]{:S(2)}, u32[]{:S(2)}) %collective-permute-start.2) | collective-permute-done | bytes 94240 | tf_op jit(solution)/shard_map/exchange_ions/ppermute | solution.py:649
  16.1 0.1 collective-permute-start.6
  16.2 1.0 %structure_sums.7.mine_ref = f32[544,128]{1,0:T(8,128)S(1)} custom-call(f32[544,128]{1,0:T(8,128)S(1)} %structure_sums.6.refs_0_, f32[8,2944]{1,0:T(8,128)S(1)} %collective-permute-done.2.refs_1_), custom_call_target="tpu_custom_call" | custom-call | flops 566231040 | bytes 1048576 | tf_op jit(solution)/shard_map/structure_sums/pallas_call | solution.py:669
  17.2 0.6 %collective-permute-start.5 = (f32[544,128]{1,0:T(8,128)S(1)}, f32[544,128]{1,0:T(8,128)S(1)}, u32[]{:S(2)}, u32[]{:S(2)}) collective-permute-start(f32[544,128]{1,0:T(8,128)S(1)} %structure_sums.7.mine_ref), channel_id=1, source_target_pairs={{0,4},{4,0},{8,12},{12,8},{1,5},{5,1},{9,13},{13,9},{2,6},{6,2},{1... | collective-permute-start | bytes 835592 | tf_op jit(solution)/shard_map/exchange_core/ppermute | solution.py:649
  17.8 0.0 copy-done
  17.8 0.5 %own_ions.1 = (f32[112,768]{1,0:T(8,128)S(1)}, bf16[256,1536]{1,0:T(8,128)(2,1)S(1)}, bf16[1024,512]{1,0:T(8,128)(2,1)S(1)}, f32[240,128]{1,0:T(8,128)S(1)}) custom-call(f32[8,512]{1,0:T(8,128)S(1)} %payload.1.refs_0_.data_ref, s32[512]{0:T(512)S(1)} %copy-done), custom_call_target="tpu_custom_call" | custom-call | flops 8589934592 | bytes 1048576 | tf_op jit(solution)/shard_map/own_ions/pallas_call | solution.py:743
  18.3 0.0 collective-permute-done.6.other_count_ref
  18.3 0.2 coefficients.1.coef_ref
  18.5 0.4 %collective-permute-done.5.other_ref = f32[544,128]{1,0:T(8,128)S(1)} collective-permute-done((f32[544,128]{1,0:T(8,128)S(1)}, f32[544,128]{1,0:T(8,128)S(1)}, u32[]{:S(2)}, u32[]{:S(2)}) %collective-permute-start.5) | collective-permute-done | bytes 278560 | tf_op jit(solution)/shard_map/exchange_core/ppermute | solution.py:649
  19.0 2.1 %forces.1 = (f32[3,768]{1,0:T(4,128)}, f32[3,512]{1,0:T(4,128)}) custom-call(f32[544,128]{1,0:T(8,128)S(1)} %structure_sums.7.mine_ref, f32[544,128]{1,0:T(8,128)S(1)} %collective-permute-done.5.other_ref, f32[8,512]{1,0:T(8,128)S(1)} %payload.1.refs_0_.data_ref, f32[112,768]{1,0:T(8,128)S(1)} %get-tuple-element.21.basis_ref, ...), custom_call_target="tpu_custom_call" | custom-call | tf_op jit(solution)/shard_map/forces/pallas_call | solution.py:766
  (5 shorter events, 0.0 us)
Async XLA Ops:
  2.1 6.0 %collective-permute-start = (f32[8,512]{1,0:T(8,128)S(1)}, f32[8,512]{1,0:T(8,128)S(1)}, u32[]{:S(2)}, u32[]{:S(2)}) collective-permute-start(f32[8,512]{1,0:T(8,128)S(1)} %payload.1.refs_0_.data_ref), channel_id=1, source_target_pairs={{0,2},{1,3},{2,0},{3,1},{4,6},{5,7},{6,4},{7,5},{8,10},{9,11},{10,... | collective-permute-start | bytes 49160 | tf_op jit(solution)/shard_map/exchange_ions/ppermute | solution.py:651
  8.1 3.3 %collective-permute-start.1 = (f32[8,1920]{1,0:T(8,128)S(1)}, f32[8,1920]{1,0:T(8,128)S(1)}, u32[]{:S(2)}, u32[]{:S(2)}) collective-permute-start(f32[8,1920]{1,0:T(8,128)S(1)} %slice_select_fusion), channel_id=1, source_target_pairs={{0,4},{4,0},{8,12},{12,8},{1,5},{5,1},{9,13},{13,9},{2,6},{6,2},{1... | collective-permute-start | bytes 184328 | tf_op jit(solution)/shard_map/exchange_counts/ppermute | solution.py:649
  8.2 4.9 %collective-permute-start.3 = (f32[8,1024]{1,0:T(8,128)S(1)}, f32[8,1024]{1,0:T(8,128)S(1)}, u32[]{:S(2)}, u32[]{:S(2)}) collective-permute-start(f32[8,1024]{1,0:T(8,128)S(1)} %pad_maximum_fusion.1), channel_id=1, source_target_pairs={{0,9},{1,8},{2,11},{3,10},{4,13},{5,12},{6,15},{7,14},{8,1},{9,0},... | collective-permute-start | bytes 98312 | tf_op jit(solution)/shard_map/exchange_ions/ppermute | solution.py:653
  10.9 3.9 %collective-permute-start.4 = (f32[8,1024]{1,0:T(8,128)S(1)}, f32[8,1024]{1,0:T(8,128)S(1)}, u32[]{:S(2)}, u32[]{:S(2)}) collective-permute-start(f32[8,1024]{1,0:T(8,128)S(1)} %pad_maximum_fusion.1), channel_id=1, source_target_pairs={{0,1},{1,0},{2,3},{3,2},{4,5},{5,4},{6,7},{7,6},{8,9},{9,8},{10,11... | collective-permute-start | bytes 98312 | tf_op jit(solution)/shard_map/exchange_ions/ppermute | solution.py:651
  11.5 4.6 %collective-permute-start.2 = (f32[8,2944]{1,0:T(8,128)S(1)}, f32[8,2944]{1,0:T(8,128)S(1)}, u32[]{:S(2)}, u32[]{:S(2)}) collective-permute-start(f32[8,2944]{1,0:T(8,128)S(1)} %pad_maximum_fusion), channel_id=1, source_target_pairs={{0,8},{4,12},{8,0},{12,4},{1,9},{5,13},{9,1},{13,5},{2,10},{6,14},... | collective-permute-start | bytes 282632 | tf_op jit(solution)/shard_map/exchange_ions/ppermute | solution.py:649
  14.1 3.7 %copy-start = (s32[512]{0:T(512)S(1)}, s32[512]{0:T(512)}, u32[]{:S(2)}) copy-start(s32[512]{0:T(512)} %recv_ref) | copy-start | bytes 6148
  16.1 2.2 %collective-permute-start.6 = (f32[8,1920]{1,0:T(8,128)S(1)}, f32[8,1920]{1,0:T(8,128)S(1)}, u32[]{:S(2)}, u32[]{:S(2)}) collective-permute-start(f32[8,1920]{1,0:T(8,128)S(1)} %slice_add_fusion.count_ref), channel_id=1, source_target_pairs={{0,4},{4,0},{8,12},{12,8},{1,5},{5,1},{9,13},{13,9},{2,6},{6,2},{1... | collective-permute-start | bytes 184328 | tf_op jit(solution)/shard_map/exchange_core/ppermute | solution.py:649
  17.2 1.7 %collective-permute-start.5 = (f32[544,128]{1,0:T(8,128)S(1)}, f32[544,128]{1,0:T(8,128)S(1)}, u32[]{:S(2)}, u32[]{:S(2)}) collective-permute-start(f32[544,128]{1,0:T(8,128)S(1)} %structure_sums.7.mine_ref), channel_id=1, source_target_pairs={{0,4},{4,0},{8,12},{12,8},{1,5},{5,1},{9,13},{13,9},{2,6},{6,2},{1... | collective-permute-start | bytes 835592 | tf_op jit(solution)/shard_map/exchange_core/ppermute | solution.py:649

commit v9 on v5

--- a/solution.py
+++ b/solution.py
@@ -316,10 +316,18 @@
     return jnp.concatenate([high, mid, rest - mid], axis=0).astype(BF16)
 
 
-def count_kernel(rows, width, waves_hbm, out_ref, waves_ref, stack_ref, sem):
-    copy = pltpu.make_async_copy(waves_hbm, waves_ref, sem)
-    copy.start()
-    copy.wait()
+def count_kernel(rows, width, waves_hbm, out_ref, waves_ref, stack_ref, sems):
+    share = rows * width // COPIES
+    copies = [
+        pltpu.make_async_copy(
+            waves_hbm.at[:, pl.ds(share * i, share)], waves_ref.at[:, pl.ds(share * i, share)], sems.at[i]
+        )
+        for i in range(COPIES)
+    ]
+    for copy in copies:
+        copy.start()
+    for copy in copies:
+        copy.wait()
     for row in range(rows):
         for comp in range(3):
             stack_ref[row : row + 1, comp * width : (comp + 1) * width] = waves_ref[
@@ -566,6 +574,7 @@
 
 
 TILE = 256
+COPIES = 4
 
 
 def force_kernel(
@@ -699,7 +708,7 @@
                     scratch_shapes=[
                         pltpu.VMEM(wave_ints.shape, jnp.int32),
                         pltpu.VMEM((wave_rows, 3 * wave_width), F32),
-                        pltpu.SemaphoreType.DMA,
+                        pltpu.SemaphoreType.DMA((COPIES,)),
                     ],
                     compiler_params=params(),
                     cost_estimate=pl.CostEstimate(

time: 21.3 us -> 21.3 us (level)
  no operation moved by 1% of the time
where the time goes in v9:
time: 21.3 us; the launch traced here: 21 us
  Pallas kernels  9.58 us (45%)
  starting transfers between devices  8.09 us (38%)
  waiting for transfers between devices  1.91 us (9%)
  between operations  1.39 us (7%)
    ppermute x2, starting transfers between devices, flip(): lax.ppermute(value, 'row', [(i, i ^ row_bit) for i in range(row_count)])  5.62 us
    pallas_call x4, Pallas kernels, accumulate(): pl.pallas_call(functools.partial(sums_kernel, plan), out_shape=table_shap...  4.2 us
    ppermute x3, starting transfers between devices, flip(): lax.ppermute(value, 'blk', [(i, i ^ blk_bit) for i in range(blk_count)])  2.29 us
    pallas_call x1, Pallas kernels, body(): pl.pallas_call(functools.partial(force_kernel, force_scale, half), out_sh...  2.1 us
    pallas_call x1, Pallas kernels, body(): pl.pallas_call(functools.partial(count_kernel, wave_rows, wave_width), ou...  1.79 us
    ppermute x3, waiting for transfers between devices, flip(): lax.ppermute(value, 'blk', [(i, i ^ blk_bit) for i in range(blk_count)])  1.09 us
    pallas_call x1, Pallas kernels, body(): pl.pallas_call(prep_kernel, out_shape=jax.ShapeDtypeStruct((8, block), F3...  0.79 us
    ppermute x2, waiting for transfers between devices, flip(): lax.ppermute(value, 'row', [(i, i ^ row_bit) for i in range(row_count)])  0.6 us
  transfers between devices with their start and end apart: 6, of which 3 were waited for; matrix products, arithmetic and copies ran while one was open for 0% of the time, Pallas kernels for 32%

profile of v9, /device:TPU:0, one launch (start us, length us, event | category | flops | bytes accessed | tf_op | source)
XLA Modules:
  0.0 21.0 jit_solution(10345079502062305476)
XLA Ops:
  1.3 0.8 %payload.1.refs_0_.data_ref = f32[8,512]{1,0:T(8,128)S(1)} custom-call(f32[3,768]{1,0:T(4,128)} %coords_hbm.1, f32[768]{0:T(1024)} %charges_hbm.1, s32[1]{0:T(128)S(6)} %copy.8.counts_hbm, s32[768]{0:T(1024)} %send_hbm.1), custom_call_target="tpu_custom_call" | custom-call | tf_op jit(solution)/shard_map/payload/pallas_call | solution.py:636
  2.1 4.1 %collective-permute-start = (f32[8,512]{1,0:T(8,128)S(1)}, f32[8,512]{1,0:T(8,128)S(1)}, u32[]{:S(2)}, u32[]{:S(2)}) collective-permute-start(f32[8,512]{1,0:T(8,128)S(1)} %payload.1.refs_0_.data_ref), channel_id=1, source_target_pairs={{0,2},{1,3},{2,0},{3,1},{4,6},{5,7},{6,4},{7,5},{8,10},{9,11},{10,... | collective-permute-start | bytes 49160 | tf_op jit(solution)/shard_map/exchange_ions/ppermute | solution.py:655
  6.2 1.8 %counts.1 = f32[8,3840]{1,0:T(8,128)S(1)} custom-call(s32[3,6144]{1,0:T(4,128)} %waves_hbm.1), custom_call_target="tpu_custom_call" | custom-call | flops 377487360 | bytes 1048576 | tf_op jit(solution)/shard_map/counts/pallas_call | solution.py:703
  8.0 0.0 copy-start
  8.0 0.0 collective-permute-done.refs_1_
  8.0 1.9 %collective-permute-start.3 = (f32[8,4864]{1,0:T(8,128)S(1)}, f32[8,4864]{1,0:T(8,128)S(1)}, u32[]{:S(2)}, u32[]{:S(2)}) collective-permute-start(f32[8,4864]{1,0:T(8,128)S(1)} %pad_maximum_fusion), channel_id=1, source_target_pairs={{0,8},{4,12},{8,0},{12,4},{1,9},{5,13},{9,1},{13,5},{2,10},{6,14},... | collective-permute-start | bytes 466952 | tf_op jit(solution)/shard_map/exchange_ions/ppermute | solution.py:653
  9.9 1.5 %collective-permute-start.2 = (f32[8,1024]{1,0:T(8,128)S(1)}, f32[8,1024]{1,0:T(8,128)S(1)}, u32[]{:S(2)}, u32[]{:S(2)}) collective-permute-start(f32[8,1024]{1,0:T(8,128)S(1)} %pad_maximum_fusion.1), channel_id=1, source_target_pairs={{0,1},{1,0},{2,3},{3,2},{4,5},{5,4},{6,7},{7,6},{8,9},{9,8},{10,11... | collective-permute-start | bytes 98312 | tf_op jit(solution)/shard_map/exchange_ions/ppermute | solution.py:655
  11.4 0.2 collective-permute-start.1
  11.6 1.1 %structure_sums.4.refs_0_ = f32[576,128]{1,0:T(8,128)S(1)} custom-call(f32[8,512]{1,0:T(8,128)S(1)} %payload.1.refs_0_.data_ref, f32[8,512]{1,0:T(8,128)S(1)} %collective-permute-done.refs_1_), custom_call_target="tpu_custom_call" | custom-call | flops 566231040 | bytes 1048576 | tf_op jit(solution)/shard_map/structure_sums/pallas_call | solution.py:673
  12.7 0.0 copy-done
  12.7 0.5 %own_ions.1 = (f32[112,768]{1,0:T(8,128)S(1)}, bf16[256,1536]{1,0:T(8,128)(2,1)S(1)}, bf16[1024,512]{1,0:T(8,128)(2,1)S(1)}, f32[240,128]{1,0:T(8,128)S(1)}) custom-call(f32[8,512]{1,0:T(8,128)S(1)} %payload.1.refs_0_.data_ref, s32[512]{0:T(512)S(1)} %copy-done), custom_call_target="tpu_custom_call" | custom-call | flops 4194304 | bytes 1048576 | tf_op jit(solution)/shard_map/own_ions/pallas_call | solution.py:733
  13.2 0.6 %collective-permute-done.2.refs_1_ = f32[8,1024]{1,0:T(8,128)S(1)} collective-permute-done((f32[8,1024]{1,0:T(8,128)S(1)}, f32[8,1024]{1,0:T(8,128)S(1)}, u32[]{:S(2)}, u32[]{:S(2)}) %collective-permute-start.2) | collective-permute-done | bytes 32800 | tf_op jit(solution)/shard_map/exchange_ions/ppermute | solution.py:655
  13.8 1.0 %structure_sums.5.refs_0_ = f32[576,128]{1,0:T(8,128)S(1)} custom-call(f32[576,128]{1,0:T(8,128)S(1)} %structure_sums.4.refs_0_, f32[8,1024]{1,0:T(8,128)S(1)} %collective-permute-done.2.refs_1_), custom_call_target="tpu_custom_call" | custom-call | flops 28311552 | bytes 1048576 | tf_op jit(solution)/shard_map/structure_sums/pallas_call | solution.py:673
  14.8 0.0 collective-permute-done.3.refs_1_
  14.9 0.1 collective-permute-start.5
  15.0 1.0 %structure_sums.6.refs_0_ = f32[576,128]{1,0:T(8,128)S(1)} custom-call(f32[576,128]{1,0:T(8,128)S(1)} %structure_sums.5.refs_0_, f32[8,4864]{1,0:T(8,128)S(1)} %collective-permute-done.3.refs_1_), custom_call_target="tpu_custom_call" | custom-call | flops 28311552 | bytes 1048576 | tf_op jit(solution)/shard_map/structure_sums/pallas_call | solution.py:673
  16.0 0.2 collective-permute-done.1.refs_1_
  16.2 1.0 %structure_sums.7.mine_ref = f32[576,128]{1,0:T(8,128)S(1)} custom-call(f32[576,128]{1,0:T(8,128)S(1)} %structure_sums.6.refs_0_, f32[8,1024]{1,0:T(8,128)S(1)} %collective-permute-done.1.refs_1_), custom_call_target="tpu_custom_call" | custom-call | flops 9059696640 | bytes 1048576 | tf_op jit(solution)/shard_map/structure_sums/pallas_call | solution.py:673
  17.3 0.4 %collective-permute-start.4 = (f32[576,128]{1,0:T(8,128)S(1)}, f32[576,128]{1,0:T(8,128)S(1)}, u32[]{:S(2)}, u32[]{:S(2)}) collective-permute-start(f32[576,128]{1,0:T(8,128)S(1)} %structure_sums.7.mine_ref), channel_id=1, source_target_pairs={{0,4},{4,0},{8,12},{12,8},{1,5},{5,1},{9,13},{13,9},{2,6},{6,2},{1... | collective-permute-start | bytes 884744 | tf_op jit(solution)/shard_map/exchange_core/ppermute | solution.py:653
  17.6 0.0 collective-permute-done.5.other_count_ref
  17.6 0.2 coefficients.1.coef_ref
  17.8 1.1 %collective-permute-done.4.other_ref = f32[576,128]{1,0:T(8,128)S(1)} collective-permute-done((f32[576,128]{1,0:T(8,128)S(1)}, f32[576,128]{1,0:T(8,128)S(1)}, u32[]{:S(2)}, u32[]{:S(2)}) %collective-permute-start.4) | collective-permute-done | bytes 294944 | tf_op jit(solution)/shard_map/exchange_core/ppermute | solution.py:653
  18.9 2.1 %forces.1 = (f32[3,768]{1,0:T(4,128)}, f32[3,512]{1,0:T(4,128)}) custom-call(f32[576,128]{1,0:T(8,128)S(1)} %structure_sums.7.mine_ref, f32[576,128]{1,0:T(8,128)S(1)} %collective-permute-done.4.other_ref, f32[8,512]{1,0:T(8,128)S(1)} %payload.1.refs_0_.data_ref, f32[112,768]{1,0:T(8,128)S(1)} %get-tuple-element.33.basis_ref, ...), custom_call_target="tpu_custom_call" | custom-call | tf_op jit(solution)/shard_map/forces/pallas_call | solution.py:766
  (3 shorter events, 0.0 us)
Async XLA Ops:
  2.1 5.9 %collective-permute-start = (f32[8,512]{1,0:T(8,128)S(1)}, f32[8,512]{1,0:T(8,128)S(1)}, u32[]{:S(2)}, u32[]{:S(2)}) collective-permute-start(f32[8,512]{1,0:T(8,128)S(1)} %payload.1.refs_0_.data_ref), channel_id=1, source_target_pairs={{0,2},{1,3},{2,0},{3,1},{4,6},{5,7},{6,4},{7,5},{8,10},{9,11},{10,... | collective-permute-start | bytes 49160 | tf_op jit(solution)/shard_map/exchange_ions/ppermute | solution.py:655
  8.0 4.7 %copy-start = (s32[512]{0:T(512)S(1)}, s32[512]{0:T(512)}, u32[]{:S(2)}) copy-start(s32[512]{0:T(512)} %recv_ref) | copy-start | bytes 6148
  8.0 6.8 %collective-permute-start.3 = (f32[8,4864]{1,0:T(8,128)S(1)}, f32[8,4864]{1,0:T(8,128)S(1)}, u32[]{:S(2)}, u32[]{:S(2)}) collective-permute-start(f32[8,4864]{1,0:T(8,128)S(1)} %pad_maximum_fusion), channel_id=1, source_target_pairs={{0,8},{4,12},{8,0},{12,4},{1,9},{5,13},{9,1},{13,5},{2,10},{6,14},... | collective-permute-start | bytes 466952 | tf_op jit(solution)/shard_map/exchange_ions/ppermute | solution.py:653
  9.9 3.9 %collective-permute-start.2 = (f32[8,1024]{1,0:T(8,128)S(1)}, f32[8,1024]{1,0:T(8,128)S(1)}, u32[]{:S(2)}, u32[]{:S(2)}) collective-permute-start(f32[8,1024]{1,0:T(8,128)S(1)} %pad_maximum_fusion.1), channel_id=1, source_target_pairs={{0,1},{1,0},{2,3},{3,2},{4,5},{5,4},{6,7},{7,6},{8,9},{9,8},{10,11... | collective-permute-start | bytes 98312 | tf_op jit(solution)/shard_map/exchange_ions/ppermute | solution.py:655
  11.4 4.8 %collective-permute-start.1 = (f32[8,1024]{1,0:T(8,128)S(1)}, f32[8,1024]{1,0:T(8,128)S(1)}, u32[]{:S(2)}, u32[]{:S(2)}) collective-permute-start(f32[8,1024]{1,0:T(8,128)S(1)} %pad_maximum_fusion.1), channel_id=1, source_target_pairs={{0,9},{1,8},{2,11},{3,10},{4,13},{5,12},{6,15},{7,14},{8,1},{9,0},... | collective-permute-start | bytes 98312 | tf_op jit(solution)/shard_map/exchange_ions/ppermute | solution.py:657
  14.9 2.8 %collective-permute-start.5 = (f32[8,3840]{1,0:T(8,128)S(1)}, f32[8,3840]{1,0:T(8,128)S(1)}, u32[]{:S(2)}, u32[]{:S(2)}) collective-permute-start(f32[8,3840]{1,0:T(8,128)S(1)} %slice_add_fusion.count_ref), channel_id=1, source_target_pairs={{0,4},{4,0},{8,12},{12,8},{1,5},{5,1},{9,13},{13,9},{2,6},{6,2},{1... | collective-permute-start | bytes 368648 | tf_op jit(solution)/shard_map/exchange_core/ppermute | solution.py:653
  17.3 1.6 %collective-permute-start.4 = (f32[576,128]{1,0:T(8,128)S(1)}, f32[576,128]{1,0:T(8,128)S(1)}, u32[]{:S(2)}, u32[]{:S(2)}) collective-permute-start(f32[576,128]{1,0:T(8,128)S(1)} %structure_sums.7.mine_ref), channel_id=1, source_target_pairs={{0,4},{4,0},{8,12},{12,8},{1,5},{5,1},{9,13},{13,9},{2,6},{6,2},{1... | collective-permute-start | bytes 884744 | tf_op jit(solution)/shard_map/exchange_core/ppermute | solution.py:653
